TPU v7x, 32 devices: a whole 2x2x4 slice. The times are simulated.
32 devices in a mesh: depth: 2 (over x), row: 4 (over y, core), col: 4 (over z).
Axes of the slice: x: 2, y: 2, z: 4, core: 2. Of those that a mesh axis runs over, the one named last changes fastest.
Arguments:
- inputs: bfloat16 [1280, 4096], P(('depth', 'col'), 'row'), may hold values from -6 to 6
- in_bits: int32 [1280, 4096], P(('depth', 'col'), 'row'), may hold values from 0 to 1
- out_grads: bfloat16 [1280, 14336], P(('depth', 'row'), 'col'), may hold values from -6 to 6
- out_bits: int32 [1280, 14336], P(('depth', 'row'), 'col'), may hold values from 0 to 1
- mean_weight: bfloat16 [14336, 4096], P(('col', 'depth'), 'row'), may hold values from -0.09375 to 0.09375
- sigma_weight: bfloat16 [14336, 4096], P(('col', 'depth'), 'row'), may hold values from 0.0049743652 to 0.049804688
- noise: bfloat16 [14336, 4096], P(('col', 'depth'), 'row'), may hold values from -6 to 6
Outputs:
- input_grad: bfloat16 [1280, 4096], P(('depth', 'col'), 'row')
- mean_grad: float32 [14336, 4096], P(('col', 'depth'), 'row')
- sigma_grad: float32 [14336, 4096], P(('col', 'depth'), 'row')
All inputs are finite; a program needn't handle non-finite values.
Results may differ from a plain program's by a relative error of at most 0.017.
Values may be sent and summed in bfloat16 or wider, within the bound.
No kernel may reach another device: no remote copies, remote signals or barrier semaphores. Data moves between devices by JAX's collectives and lax.ppermute only.
A program may use at most 128 MiB of HBM per device.

v0:
```python
import jax
import jax.numpy as jnp
from jax import lax
from jax.sharding import PartitionSpec as P


def local(inputs, in_bits, out_grads, out_bits, mean_weight, sigma_weight, noise):
    in_sign = (1 - 2 * in_bits).astype(jnp.bfloat16)
    signed_inputs = inputs * in_sign
    signed_grads = out_grads * (1 - 2 * out_bits).astype(jnp.bfloat16)
    perturbed = (sigma_weight.astype(jnp.float32) * noise.astype(jnp.float32)).astype(jnp.bfloat16)
    slab_inputs, slab_signed = (
        lax.all_gather(inputs, "col", axis=0, tiled=True),
        lax.all_gather(signed_inputs, "col", axis=0, tiled=True),
    )
    slab_grads, slab_signed_grads = (
        lax.all_gather(out_grads, "row", axis=0, tiled=True),
        lax.all_gather(signed_grads, "row", axis=0, tiled=True),
    )
    feat_width = inputs.shape[1]
    tokens_total = slab_grads.shape[0] * lax.axis_size("depth")
    dims = (((0,), (0,)), ((), ()))

    def add_block(grads, block_rows):
        return jnp.dot(grads, block_rows, preferred_element_type=jnp.float32)

    part_a = add_block(slab_grads, lax.all_gather(mean_weight, "depth", axis=0, tiled=True))
    part_b = add_block(slab_signed_grads, lax.all_gather(perturbed, "depth", axis=0, tiled=True))
    part_a, part_b = (part_a, part_b)
    term_mean = lax.dot_general(slab_grads, slab_inputs, dims, preferred_element_type=jnp.float32)
    term_sigma = lax.dot_general(
        slab_signed_grads, slab_signed, dims, preferred_element_type=jnp.float32
    )
    summed = lax.psum_scatter(
        jnp.concatenate([term_mean, term_sigma], axis=1).astype(jnp.bfloat16),
        "depth",
        scatter_dimension=0,
        tiled=True,
    ).astype(jnp.float32)
    owned_a, owned_b = (
        lax.psum_scatter(
            part_a.astype(jnp.bfloat16), "col", scatter_dimension=0, tiled=True
        ).astype(jnp.float32),
        lax.psum_scatter(
            part_b.astype(jnp.bfloat16), "col", scatter_dimension=0, tiled=True
        ).astype(jnp.float32),
    )
    input_grad = (owned_a + owned_b * in_sign.astype(jnp.float32)).astype(jnp.bfloat16)
    grad_scale = tokens_total ** (-0.5)
    mean_grad = summed[:, :feat_width] * grad_scale
    sigma_grad = summed[:, feat_width:] * grad_scale * noise.astype(jnp.float32)
    return (input_grad, mean_grad, sigma_grad)


def solution(mesh):
    placed = (
        P(("depth", "col"), "row"),
        P(("depth", "col"), "row"),
        P(("depth", "row"), "col"),
        P(("depth", "row"), "col"),
        P(("col", "depth"), "row"),
        P(("col", "depth"), "row"),
        P(("col", "depth"), "row"),
    )
    return jax.shard_map(
        local,
        mesh=mesh,
        in_specs=placed,
        out_specs=(
            P(("depth", "col"), "row"),
            P(("col", "depth"), "row"),
            P(("col", "depth"), "row"),
        ),
        check_vma=False,
    )
```

profile of v0, /device:TPU:0, one launch (start us, length us, event | category | flops | bytes accessed | tf_op | source)
XLA Modules:
  0.0 599.4 jit_solution(8830945893818740650)
XLA Ops:
  7.2 0.7 all-gather.15.cloned.1.call-update
  8.0 0.7 all-gather.7.cloned.1.call-update
  8.7 0.0 all-gather.17.cloned.1.call-start
  8.7 2.0 fusion.2
  10.8 0.0 all-gather.11.cloned.1.call-start
  10.8 2.7 fusion.1
  13.5 0.0 reduce-scatter.8.cloned.1.call-start
  13.6 31.4 %all-gather.15.cloned.1.call-done = bf16[640,1024]{1,0:T(8,128)(2,1)} async-done(((bf16[160,1024]{1,0:T(8,128)(2,1)}), bf16[640,1024]{1,0:T(8,128)(2,1)}) %all-gather.15.cloned.1.call-update) | async-done | bytes 1310736 | tf_op jit(solution)/shard_map/all_gather | solution.py:13
  45.0 37.3 %all-gather.7.cloned.1.call-done = bf16[640,3584]{1,0:T(8,128)(2,1)} async-done(((bf16[160,3584]{1,0:T(8,128)(2,1)}), bf16[640,3584]{1,0:T(8,128)(2,1)}) %all-gather.7.cloned.1.call-update) | async-done | bytes 4587536 | tf_op jit(solution)/shard_map/all_gather | solution.py:17
  82.3 10.5 %convolution_convert_fusion.1 = bf16[3584,1024]{0,1:T(8,128)(2,1)} fusion(bf16[640,3584]{1,0:T(8,128)(2,1)} %all-gather.7.cloned.1.call-done, bf16[640,1024]{1,0:T(8,128)(2,1)} %all-gather.15.cloned.1.call-done), kind=kOutput, calls=%fused_computation.4 | convolution fusion | flops 4701290496 | bytes 13238272 | tf_op jit(solution)/shard_map/dot_general | solution.py:30
  92.8 24.4 %all-gather.17.cloned.1.call-done = bf16[640,1024]{1,0:T(8,128)(2,1)} async-done(((bf16[160,1024]{1,0:T(8,128)(2,1)}), bf16[640,1024]{1,0:T(8,128)(2,1)}) %all-gather.17.cloned.1.call-update) | async-done | bytes 1310736 | tf_op jit(solution)/shard_map/all_gather | solution.py:14
  117.2 37.7 %all-gather.11.cloned.1.call-done = bf16[640,3584]{1,0:T(8,128)(2,1)} async-done(((bf16[160,3584]{1,0:T(8,128)(2,1)}), bf16[640,3584]{1,0:T(8,128)(2,1)}) %all-gather.11.cloned.1.call-update) | async-done | bytes 4587536 | tf_op jit(solution)/shard_map/all_gather | solution.py:18
  154.9 8.8 %convolution_convert_fusion = bf16[3584,1024]{0,1:T(8,128)(2,1)S(1)} fusion(bf16[640,3584]{1,0:T(8,128)(2,1)} %all-gather.11.cloned.1.call-done, bf16[640,1024]{1,0:T(8,128)(2,1)} %all-gather.17.cloned.1.call-done), kind=kOutput, calls=%fused_computation.3 | convolution fusion | flops 4701290496 | bytes 13238272 | tf_op jit(solution)/shard_map/dot_general | solution.py:31
  163.7 6.0 %pad_maximum_fusion = bf16[3584,2048]{0,1:T(8,128)(2,1)} fusion(bf16[3584,1024]{0,1:T(8,128)(2,1)S(1)} %convolution_convert_fusion, bf16[3584,1024]{0,1:T(8,128)(2,1)S(1)} %copy-done.2), kind=kLoop, calls=%fused_computation | loop fusion | flops 29360128 | bytes 29360128 | tf_op jit(solution)/shard_map/concatenate | solution.py:35
  169.8 0.0 all-gather.9.cloned.1.call-start
  169.8 0.5 all-gather.9.cloned.1.call-update
  170.4 5.9 copy.10
  176.3 6.1 %copy.11 = bf16[1792,1024]{0,1:T(8,128)(2,1)} copy(bf16[1792,1024]{1,0:T(8,128)(2,1)} %param.13) | data formatting | bytes 7340032 | tf_op args[6]
  182.4 154.6 %reduce-scatter.8.cloned.1.call-done = bf16[1792,2048]{0,1:T(8,128)(2,1)} async-done(((bf16[3584,2048]{0,1:T(8,128)(2,1)}), bf16[1792,2048]{0,1:T(8,128)(2,1)}) %reduce-scatter.8.cloned.1.call-update) | async-done | bytes 7340048 | tf_op jit(solution)/shard_map/reduce_scatter | solution.py:34
  337.0 10.9 %convert_element_type.49 = f32[1792,2048]{0,1:T(8,128)} convert(bf16[1792,2048]{0,1:T(8,128)(2,1)} %reduce-scatter.8.cloned.1.call-done) | non-fusion elementwise | flops 3670016 | bytes 22020096 | tf_op jit(solution)/shard_map/convert_element_type | solution.py:39
  347.9 13.3 %convert_multiply_fusion = (f32[1792,1024]{0,1:T(8,128)}, f32[1792,1024]{0,1:T(8,128)}, bf16[1792,1024]{0,1:T(8,128)(2,1)}) fusion(bf16[1792,1024]{0,1:T(8,128)(2,1)S(1)} %copy-done.1, f32[1792,2048]{0,1:T(8,128)} %convert_element_type.49, bf16[1792,1024]{0,1:T(8,128)(2,1)S(1)} %copy-done), kind=kLoop, calls=%fused_computation.1 | loop fusion | flops 12845056 | bytes 40370176 | tf_op jit(solution)/shard_map/mul | solution.py:51
  361.2 0.2 reduce-scatter.4.cloned.1.call-start
  361.4 69.2 %all-gather.9.cloned.1.call-done = bf16[3584,1024]{1,0:T(8,128)(2,1)} async-done(((bf16[1792,1024]{1,0:T(8,128)(2,1)}), bf16[3584,1024]{1,0:T(8,128)(2,1)}) %all-gather.9.cloned.1.call-update) | async-done | bytes 7340048 | tf_op jit(solution)/shard_map/all_gather | solution.py:27
  430.6 10.5 %convolution_convert_fusion.3 = bf16[640,1024]{1,0:T(8,128)(2,1)} fusion(bf16[640,3584]{1,0:T(8,128)(2,1)} %all-gather.7.cloned.1.call-done, bf16[3584,1024]{1,0:T(8,128)(2,1)} %all-gather.9.cloned.1.call-done), kind=kOutput, calls=%fused_computation.10 | convolution fusion | flops 4698275840 | bytes 13238272 | tf_op jit(solution)/shard_map/dot_general | solution.py:25
  441.2 0.0 reduce-scatter.6.cloned.1.call-start
  441.2 83.7 %all-gather.13.cloned.1.call-done = bf16[3584,1024]{0,1:T(8,128)(2,1)} async-done(((bf16[1792,1024]{0,1:T(8,128)(2,1)}), bf16[3584,1024]{0,1:T(8,128)(2,1)}) %all-gather.13.cloned.1.call-update) | async-done | bytes 7340048 | tf_op jit(solution)/shard_map/all_gather | solution.py:28
  525.0 10.5 %convolution_convert_fusion.2 = bf16[640,1024]{1,0:T(8,128)(2,1)} fusion(bf16[640,3584]{1,0:T(8,128)(2,1)} %all-gather.11.cloned.1.call-done, bf16[3584,1024]{0,1:T(8,128)(2,1)} %all-gather.13.cloned.1.call-done), kind=kOutput, calls=%fused_computation.9 | convolution fusion | flops 4698275840 | bytes 13238272 | tf_op jit(solution)/shard_map/dot_general | solution.py:25
  535.5 8.4 %copy.13 = f32[1792,1024]{1,0:T(8,128)} copy(f32[1792,1024]{0,1:T(8,128)} %get-tuple-element.6) | data formatting | bytes 14680064
  543.9 8.5 %copy.12 = f32[1792,1024]{1,0:T(8,128)} copy(f32[1792,1024]{0,1:T(8,128)} %get-tuple-element.7) | data formatting | bytes 14680064
  552.4 6.2 %reduce-scatter.4.cloned.1.call-done = bf16[160,1024]{1,0:T(8,128)(2,1)} async-done(((bf16[640,1024]{1,0:T(8,128)(2,1)}), bf16[160,1024]{1,0:T(8,128)(2,1)}) %reduce-scatter.4.cloned.1.call-update) | async-done | bytes 327696 | tf_op jit(solution)/shard_map/reduce_scatter | solution.py:41
  558.5 32.4 %reduce-scatter.6.cloned.1.call-done = bf16[160,1024]{1,0:T(8,128)(2,1)} async-done(((bf16[640,1024]{1,0:T(8,128)(2,1)}), bf16[160,1024]{1,0:T(8,128)(2,1)}) %reduce-scatter.6.cloned.1.call-update) | async-done | bytes 327696 | tf_op jit(solution)/shard_map/reduce_scatter | solution.py:44
  590.9 2.0 add_convert_fusion
  (19 shorter events, 0.2 us)
Async XLA Ops:
  7.2 3.7 copy-start.4
  7.2 37.8 %all-gather.15.cloned.1.call-start = ((), (), s32[]{:S(2)}) async-start(), calls=%async_computation.9 | async-start | bytes 1638400 | tf_op jit(solution)/shard_map/all_gather | solution.py:13
  7.9 74.4 %all-gather.7.cloned.1.call-start = ((), (), s32[]{:S(2)}) async-start(), calls=%async_computation.3 | async-start | bytes 5734400 | tf_op jit(solution)/shard_map/all_gather | solution.py:17
  8.7 108.5 %all-gather.17.cloned.1.call-start = ((), (), s32[]{:S(2)}) async-start(), calls=%async_computation.10 | async-start | bytes 1638400 | tf_op jit(solution)/shard_map/all_gather | solution.py:14
  10.8 144.2 %all-gather.11.cloned.1.call-start = ((), (), s32[]{:S(2)}) async-start(), calls=%async_computation.6 | async-start | bytes 5734400 | tf_op jit(solution)/shard_map/all_gather | solution.py:18
  13.5 323.5 %reduce-scatter.8.cloned.1.call-start = ((), (), s32[]{:S(2)}) async-start(), calls=%async_computation.11 | async-start | bytes 22020096 | tf_op jit(solution)/shard_map/reduce_scatter | solution.py:34
  154.9 8.8 %copy-start.2 = (bf16[3584,1024]{0,1:T(8,128)(2,1)S(1)}, bf16[3584,1024]{0,1:T(8,128)(2,1)}, u32[]{:S(2)}) copy-start(bf16[3584,1024]{0,1:T(8,128)(2,1)} %convolution_convert_fusion.1) | copy-start | bytes 22020100
  169.8 260.9 %all-gather.9.cloned.1.call-start = ((), (), s32[]{:S(2)}) async-start(), calls=%async_computation.4 | async-start | bytes 11010048 | tf_op jit(solution)/shard_map/all_gather | solution.py:27
  170.3 354.6 %all-gather.13.cloned.1.call-start = ((), (), s32[]{:S(2)}) async-start(), calls=%async_computation.7 | async-start | bytes 11010048 | tf_op jit(solution)/shard_map/all_gather | solution.py:28
  337.0 10.9 %copy-start = (bf16[1792,1024]{0,1:T(8,128)(2,1)S(1)}, bf16[1792,1024]{0,1:T(8,128)(2,1)}, u32[]{:S(2)}) copy-start(bf16[1792,1024]{0,1:T(8,128)(2,1)} %copy.10) | copy-start | bytes 11010052
  337.0 10.9 %copy-start.1 = (bf16[1792,1024]{0,1:T(8,128)(2,1)S(1)}, bf16[1792,1024]{0,1:T(8,128)(2,1)}, u32[]{:S(2)}) copy-start(bf16[1792,1024]{0,1:T(8,128)(2,1)} %copy.11) | copy-start | bytes 11010052
  361.2 197.4 %reduce-scatter.4.cloned.1.call-start = ((), (), s32[]{:S(2)}) async-start(), calls=%async_computation.5 | async-start | bytes 1638400 | tf_op jit(solution)/shard_map/reduce_scatter | solution.py:41
  441.2 149.7 %reduce-scatter.6.cloned.1.call-start = ((), (), s32[]{:S(2)}) async-start(), calls=%async_computation.8 | async-start | bytes 1638400 | tf_op jit(solution)/shard_map/reduce_scatter | solution.py:44
  543.9 47.0 %copy-start.3 = (s32[160,1024]{1,0:T(8,128)S(1)}, s32[160,1024]{1,0:T(8,128)}, u32[]{:S(2)}) copy-start(s32[160,1024]{1,0:T(8,128)} %param.8) | copy-start | bytes 1966084
Sparse Core Ops, SparseCore 0:
  9.6 35.3 all-gather.14
  46.6 35.6 all-gather.6
  84.5 32.6 all-gather.16
  119.2 35.6 all-gather.10
  169.9 167.0 reduce-scatter.7
  338.4 92.1 all-gather.8
  432.7 92.1 all-gather.12
  527.3 31.2 reduce-scatter.3
  560.8 29.9 reduce-scatter.5
where the time goes:
time: 600 us; the launch traced here: 599 us
  waiting for transfers between devices  479 us (80%)
  matrix products  40.3 us (7%)
  other arithmetic  36.8 us (6%)
  local copies, waits for them, and re-layouts  28.9 us (5%)
  between operations  13.9 us (2%)
    reduce_scatter x1, waiting for transfers between devices, local(): lax.psum_scatter(jnp.concatenate([term_mean, term_sigma], axis=1).astype(...  155 us
    all_gather x1, waiting for transfers between devices, local(): lax.all_gather(perturbed, 'depth', axis=0, tiled=True)  83.7 us
    all_gather x1, waiting for transfers between devices, local(): lax.all_gather(mean_weight, 'depth', axis=0, tiled=True)  69.2 us
    all_gather x1, waiting for transfers between devices, local(): lax.all_gather(signed_grads, 'row', axis=0, tiled=True)  37.7 us
    all_gather x1, waiting for transfers between devices, local(): lax.all_gather(out_grads, 'row', axis=0, tiled=True)  37.3 us
    reduce_scatter x1, waiting for transfers between devices, local(): lax.psum_scatter(part_b.astype(jnp.bfloat16), 'col', scatter_dimension=0,...  32.4 us
    all_gather x1, waiting for transfers between devices, local(): lax.all_gather(inputs, 'col', axis=0, tiled=True)  31.4 us
    unnamed x14, local copies, waits for them, and re-layouts  28.9 us
  transfers between devices with their start and end apart: 9, of which 9 were waited for; matrix products, arithmetic and copies ran while one was open for 15% of the time, Pallas kernels for 0%

commit v1 on v0

v1 whole, which is shorter than its diff:
```python
import functools

import jax
import jax.numpy as jnp
from jax import lax
from jax.experimental import pallas as pl
from jax.experimental.pallas import tpu as pltpu
from jax.sharding import PartitionSpec as P

VMEM_LIMIT = 56 * 1024 * 1024


def grad_kernel(n_piece, row_ref, *refs):
    pieces, (mean_ref, pert_ref, sign_ref, out_ref, both, sems) = refs[:n_piece], refs[n_piece:]

    @pl.when(pl.program_id(0) == 0)
    def _():
        copies = [
            pltpu.make_async_copy(pieces[k], both.at[row_ref[0] ^ k], sems.at[k])
            for k in range(n_piece)
        ]
        for copy in copies:
            copy.start()
        for copy in copies:
            copy.wait()

    tokens, hidden = sign_ref.shape[0], mean_ref.shape[0]
    grads = both[:, 0].reshape(tokens, hidden)
    signed = both[:, 1].reshape(tokens, hidden)
    part_a = jnp.dot(grads, mean_ref[...], preferred_element_type=jnp.float32)
    part_b = jnp.dot(signed, pert_ref[...], preferred_element_type=jnp.float32)
    out_ref[...] = (part_a + part_b * sign_ref[...].astype(jnp.float32)).astype(out_ref.dtype)


def partial_input_grad(row, pieces, mean_weight, perturbed, sign):
    hidden, feats = mean_weight.shape
    tokens = sign.shape[0]
    n_piece = len(pieces)
    tile = min(256, feats)
    any_spec = pl.BlockSpec(memory_space=pl.ANY)
    return pl.pallas_call(
        functools.partial(grad_kernel, n_piece),
        grid_spec=pltpu.PrefetchScalarGridSpec(
            num_scalar_prefetch=1,
            grid=(feats // tile,),
            in_specs=[any_spec] * n_piece
            + [
                pl.BlockSpec((hidden, tile), lambda f, row: (0, f)),
                pl.BlockSpec((hidden, tile), lambda f, row: (0, f)),
                pl.BlockSpec((tokens, tile), lambda f, row: (0, f)),
            ],
            out_specs=pl.BlockSpec((tokens, tile), lambda f, row: (0, f)),
            scratch_shapes=[
                pltpu.VMEM((n_piece,) + pieces[0].shape, jnp.bfloat16),
                pltpu.SemaphoreType.DMA((n_piece,)),
            ],
        ),
        out_shape=jax.ShapeDtypeStruct((tokens, feats), jnp.bfloat16),
        compiler_params=pltpu.CompilerParams(vmem_limit_bytes=VMEM_LIMIT),
        cost_estimate=pl.CostEstimate(
            flops=4 * tokens * hidden * feats,
            bytes_accessed=4 * (tokens * hidden + hidden * feats + tokens * feats),
            transcendentals=0,
        ),
        name="input_grad",
    )(row, *pieces, mean_weight, perturbed, sign)


def weight_kernel(n_slab, n_piece, scale, row_ref, *refs):
    n_grads = n_slab * n_piece
    grads, inputs, signs = refs[:n_grads], refs[n_grads:n_grads + n_slab], refs[n_grads + n_slab:n_grads + 2 * n_slab]
    noise_ref, mean_ref, sigma_ref, plain, signed = refs[n_grads + 2 * n_slab:]
    rows = grads[0].shape[1]

    @pl.when(pl.program_id(1) == 0)
    def _():
        for j in range(n_slab):
            for k in range(n_piece):
                start = pl.multiple_of((row_ref[0] ^ k) * rows, rows)
                value = inputs[j][pl.ds(start, rows), :]
                at = (j * n_piece + k) * rows
                plain[at:at + rows, :] = value
                signed[at:at + rows, :] = value * signs[j][pl.ds(start, rows), :]

    dims = (((0,), (0,)), ((), ()))
    grad = jnp.concatenate([g[0] for g in grads], axis=0)
    mean = lax.dot_general(grad, plain[...], dims, preferred_element_type=jnp.float32)
    mean_ref[...] = mean * scale
    grad = jnp.concatenate([g[1] for g in grads], axis=0)
    sigma = lax.dot_general(grad, signed[...], dims, preferred_element_type=jnp.float32)
    sigma_ref[...] = sigma * scale * noise_ref[...].astype(jnp.float32)


def weight_grads(row, pieces, inputs, signs, noise, scale):
    n_slab, n_piece = len(pieces), len(pieces[0])
    hidden, feats = noise.shape
    slab = inputs[0].shape[0]
    tokens = slab * n_slab
    rows = pieces[0][0].shape[1]
    width = feats if tokens <= 1280 else min(256, feats)
    tile = 256 if hidden % 256 == 0 else hidden
    grad_spec = pl.BlockSpec((2, rows, tile), lambda f, h, row: (0, 0, h))
    slab_spec = pl.BlockSpec((slab, width), lambda f, h, row: (0, f))
    out_spec = pl.BlockSpec((tile, width), lambda f, h, row: (h, f))
    return pl.pallas_call(
        functools.partial(weight_kernel, n_slab, n_piece, scale),
        grid_spec=pltpu.PrefetchScalarGridSpec(
            num_scalar_prefetch=1,
            grid=(feats // width, hidden // tile),
            in_specs=[grad_spec] * (n_slab * n_piece) + [slab_spec] * (2 * n_slab) + [out_spec],
            out_specs=[out_spec, out_spec],
            scratch_shapes=[
                pltpu.VMEM((tokens, width), jnp.bfloat16),
                pltpu.VMEM((tokens, width), jnp.bfloat16),
            ],
        ),
        out_shape=[jax.ShapeDtypeStruct((hidden, feats), jnp.float32)] * 2,
        compiler_params=pltpu.CompilerParams(vmem_limit_bytes=VMEM_LIMIT),
        cost_estimate=pl.CostEstimate(
            flops=4 * tokens * hidden * feats,
            bytes_accessed=4 * (tokens * hidden + tokens * feats) + 10 * hidden * feats,
            transcendentals=0,
        ),
        name="weight_grads",
    )(row, *[p for slab_pieces in pieces for p in slab_pieces], *inputs, *signs, noise)


def local(inputs, in_bits, out_grads, out_bits, mean_weight, sigma_weight, noise):
    n_depth, n_row = lax.axis_size("depth"), lax.axis_size("row")
    depth = lax.axis_index("depth")
    row = lax.axis_index("row").astype(jnp.int32).reshape(1)
    hidden = mean_weight.shape[0]
    tokens_total = inputs.shape[0] * lax.axis_size("col") * n_depth

    in_sign = (1 - 2 * in_bits).astype(jnp.bfloat16)
    signed_grads = out_grads * (1 - 2 * out_bits).astype(jnp.bfloat16)
    perturbed = (sigma_weight.astype(jnp.float32) * noise.astype(jnp.float32)).astype(jnp.bfloat16)

    def hop(value, step):
        pairs = [(i, (i + step) % n_depth) for i in range(n_depth)]
        return lax.ppermute(value, "depth", pairs)

    def swap(value, bit):
        return lax.ppermute(value, "row", [(i, i ^ bit) for i in range(n_row)])

    def half(step):
        start = ((depth + step) % n_depth) * hidden
        return jnp.stack([lax.dynamic_slice_in_dim(a, start, hidden, 1) for a in (out_grads, signed_grads)])

    slab_sign = [lax.all_gather(in_sign, "col", axis=0, tiled=True)]
    slab_inputs = [lax.all_gather(inputs, "col", axis=0, tiled=True)]
    pieces = []
    for j in range(n_depth):
        mine = half(j)
        if j:
            mine = hop(mine, j)
        slab_pieces = [mine]
        bit = 1
        while bit < n_row:
            slab_pieces += [None] * bit
            bit *= 2
        filled = [0]
        bit = n_row // 2
        while bit:
            for at in list(filled):
                slab_pieces[at ^ bit] = swap(slab_pieces[at], bit)
                filled.append(at ^ bit)
            bit //= 2
        pieces.append(slab_pieces)
    for j in range(1, n_depth):
        slab_sign.append(hop(slab_sign[0], j))
        slab_inputs.append(hop(slab_inputs[0], j))

    total = None
    for j in range(n_depth):
        part = partial_input_grad(row, pieces[j], mean_weight, perturbed, slab_sign[j])
        owned = lax.psum_scatter(part, "col", scatter_dimension=0, tiled=True)
        if j:
            owned = hop(owned, n_depth - j)
        owned = owned.astype(jnp.float32)
        total = owned if total is None else total + owned
    input_grad = total.astype(jnp.bfloat16)

    mean_grad, sigma_grad = weight_grads(
        row, pieces, slab_inputs, slab_sign, noise, tokens_total ** (-0.5)
    )
    return (input_grad, mean_grad, sigma_grad)


def solution(mesh):
    return jax.shard_map(
        local,
        mesh=mesh,
        in_specs=(
            P(("depth", "col"), "row"),
            P(("depth", "col"), "row"),
            P(("depth", "row"), "col"),
            P(("depth", "row"), "col"),
            P(("col", "depth"), "row"),
            P(("col", "depth"), "row"),
            P(("col", "depth"), "row"),
        ),
        out_specs=(
            P(("depth", "col"), "row"),
            P(("col", "depth"), "row"),
            P(("col", "depth"), "row"),
        ),
        check_vma=False,
    )
```

time: 600 us -> 168 us (0.28)
  waiting for transfers between devices: 479 us -> 89 us
  matrix products: 40.3 us -> 0 us
  Pallas kernels: 0 us -> 38.7 us
  local copies, waits for them, and re-layouts: 28.9 us -> 2.3 us
  other arithmetic: 36.8 us -> 12.9 us
  starting transfers between devices: 0.54 us -> 11 us
    all_gather x6 -> x2, waiting for transfers between devices: 284 us -> 3.82 us  [the longest x1 3.8 us: local(): slab_sign = [lax.all_gather(in_sign, 'col', axis=0, tiled=True)]]
    reduce_scatter x3 -> x2, waiting for transfers between devices: 193 us -> 7.04 us  [local(): owned = lax.psum_scatter(part, 'col', scatter_dimension=0, tiled=True)]
    ppermute x0 -> x10, waiting for transfers between devices: none -> 78.1 us  [the longest x4 47.8 us: hop(): return lax.ppermute(value, 'depth', pairs)]
    dot_general x4 -> x0, matrix products: 40.3 us -> none  [the longest x2 21 us: add_block(): return jnp.dot(grads, block_rows, preferred_element_type=jnp.float32)]
    pallas_call x0 -> x3, Pallas kernels: none -> 38.7 us  [the longest x2 21.3 us: partial_input_grad(): pl.pallas_call(functools.partial(grad_kernel, n_piece), grid_spec=pltpu.P...]
    unnamed x14, local copies, waits for them, and re-layouts: 28.9 us -> 2.15 us
    mul x2 -> x0, other arithmetic: 15.3 us -> none  [the longest x1 13.3 us: local(): sigma_grad = summed[:, feat_width:] * grad_scale * noise.astype(jnp.float32)]
    ppermute x0 -> x10, starting transfers between devices: none -> 10.8 us  [the longest x4 7.43 us: hop(): return lax.ppermute(value, 'depth', pairs)]
  transfers between devices with their start and end apart: 9 -> 14, of which waited for: 9 -> 8; matrix products, arithmetic and copies ran while one was open for 15% -> 6% of each run, Pallas kernels for 0% -> 23%
where the time goes in v1:
time: 168 us
  waiting for transfers between devices  89 us (53%)
  Pallas kernels  38.7 us (23%)
  between operations  13.9 us (8%)
  other arithmetic  12.9 us (8%)
  starting transfers between devices  11 us (7%)
  local copies, waits for them, and re-layouts  2.3 us (1%)
    ppermute x4, waiting for transfers between devices, hop(): return lax.ppermute(value, 'depth', pairs)  47.8 us
    ppermute x6, waiting for transfers between devices, swap(): return lax.ppermute(value, 'row', [(i, i ^ bit) for i in range(n_row)])  30.3 us
    pallas_call x2, Pallas kernels, partial_input_grad(): pl.pallas_call(functools.partial(grad_kernel, n_piece), grid_spec=pltpu.P...  21.3 us
    pallas_call x1, Pallas kernels, weight_grads(): pl.pallas_call(functools.partial(weight_kernel, n_slab, n_piece, scale),...  17.4 us
    ppermute x4, starting transfers between devices, hop(): return lax.ppermute(value, 'depth', pairs)  7.43 us
    reduce_scatter x2, waiting for transfers between devices, local(): owned = lax.psum_scatter(part, 'col', scatter_dimension=0, tiled=True)  7.04 us
    convert_element_type x1, other arithmetic, local(): (sigma_weight.astype(jnp.float32) * noise.astype(jnp.float32)).astype(jnp...  6.84 us
    all_gather x1, waiting for transfers between devices, local(): slab_sign = [lax.all_gather(in_sign, 'col', axis=0, tiled=True)]  3.8 us
  transfers between devices with their start and end apart: 14, of which 8 were waited for; matrix products, arithmetic and copies ran while one was open for 6% of the time, Pallas kernels for 23%

profile of v1, /device:TPU:0, one launch (start us, length us, event | category | flops | bytes accessed | tf_op | source)
XLA Modules:
  0.0 167.9 jit_solution(3417137314464853276)
XLA Ops:
  7.2 0.0 all-gather.3.cloned.1.call-start
  7.2 2.0 %subtract_convert_fusion.1 = bf16[160,1024]{1,0:T(8,128)(2,1)} fusion(s32[160,1024]{1,0:T(8,128)} %param.8), kind=kLoop, calls=%fused_computation.6 | loop fusion | flops 491520 | bytes 983040 | tf_op jit(solution)/shard_map/convert_element_type | solution.py:135
  9.2 0.0 all-gather.5.cloned.1.call-start
  9.3 2.1 %fusion = bf16[160,3584]{1,0:T(8,128)(2,1)S(1)} fusion(bf16[160,3584]{1,0:T(8,128)(2,1)S(1)} %copy-done, s32[160,3584]{1,0:T(8,128)} %param.10), kind=kLoop, calls=%fused_computation.2 | loop fusion | flops 2293760 | bytes 4587520 | tf_op jit(solution)/shard_map/mul | solution.py:136
  11.4 0.2 dynamic-slice_bitcast_fusion.2
  11.6 0.1 pad_maximum_fusion.1
  11.7 3.0 %collective-permute-start.3 = (bf16[2,160,1792]{2,1,0:T(8,128)(2,1)S(1)}, bf16[2,160,1792]{2,1,0:T(8,128)(2,1)S(1)}, u32[]{:S(2)}, u32[]{:S(2)}) collective-permute-start(bf16[2,160,1792]{2,1,0:T(8,128)(2,1)S(1)} %pad_maximum_fusion.1), channel_id=1, source_target_pairs={{0,16},{16,0},{1,17},{17,1},{2,18},{18,2},{3,19},{19,3},{4,20},{20... | collective-permute-start | bytes 3440648 | tf_op jit(solution)/shard_map/ppermute | solution.py:141
  14.7 25.3 %collective-permute-done.3.refs_0_.refs_4_ = bf16[2,160,1792]{2,1,0:T(8,128)(2,1)S(1)} collective-permute-done((bf16[2,160,1792]{2,1,0:T(8,128)(2,1)S(1)}, bf16[2,160,1792]{2,1,0:T(8,128)(2,1)S(1)}, u32[]{:S(2)}, u32[]{:S(2)}) %collective-permute-start.3) | collective-permute-done | bytes 1146912 | tf_op jit(solution)/shard_map/ppermute | solution.py:141
  39.9 1.8 %collective-permute-start.5 = (bf16[2,160,1792]{2,1,0:T(8,128)(2,1)S(1)}, bf16[2,160,1792]{2,1,0:T(8,128)(2,1)}, u32[]{:S(2)}, u32[]{:S(2)}) collective-permute-start(bf16[2,160,1792]{2,1,0:T(8,128)(2,1)S(1)} %collective-permute-done.3.refs_0_.refs_4_), channel_id=1, source_target_pairs={{0,8},{4,12},{8,0},{12,4},{1,9},{5,13},{9,1},{13,5},{2,10},{6,14},... | collective-permute-start | bytes 3440648 | tf_op jit(solution)/shard_map/ppermute | solution.py:144
  41.7 0.0 reduce-scatter.5.cloned.1.call-start
  41.8 3.8 %all-gather.3.cloned.1.call-done.refs_6_.refs_10_ = bf16[640,1024]{1,0:T(8,128)(2,1)} async-done(((bf16[160,1024]{1,0:T(8,128)(2,1)}), bf16[640,1024]{1,0:T(8,128)(2,1)}) %all-gather.3.cloned.1.call-update) | async-done | bytes 1310736 | tf_op jit(solution)/shard_map/all_gather | solution.py:150
  45.6 1.5 collective-permute-start.7
  47.1 19.5 %collective-permute-done.5.refs_2_.refs_6_ = bf16[2,160,1792]{2,1,0:T(8,128)(2,1)} collective-permute-done((bf16[2,160,1792]{2,1,0:T(8,128)(2,1)S(1)}, bf16[2,160,1792]{2,1,0:T(8,128)(2,1)}, u32[]{:S(2)}, u32[]{:S(2)}) %collective-permute-start.5) | collective-permute-done | bytes 1146912 | tf_op jit(solution)/shard_map/ppermute | solution.py:144
  66.6 0.1 pad_maximum_fusion.refs_0_
  66.7 1.5 collective-permute-start.1
  68.3 6.8 %multiply_convert_fusion.refs_5_ = bf16[1792,1024]{1,0:T(8,128)(2,1)} fusion(bf16[1792,1024]{1,0:T(8,128)(2,1)} %refs_12_.1, bf16[1792,1024]{1,0:T(8,128)(2,1)} %param.12), kind=kLoop, calls=%fused_computation | loop fusion | flops 7340032 | bytes 11010048 | tf_op jit(solution)/shard_map/convert_element_type | solution.py:137
  75.1 0.7 collective-permute-done.7.refs_6_.refs_11_
  75.8 10.6 %input_grad.3 = bf16[640,1024]{1,0:T(8,128)(2,1)} custom-call(s32[1]{0:T(128)} %bitcast.row_ref, bf16[2,160,1792]{2,1,0:T(8,128)(2,1)} %copy-done.3, bf16[2,160,1792]{2,1,0:T(8,128)(2,1)} %collective-permute-done.4.refs_1_.refs_5_, bf16[2,160,1792]{2,1,0:T(8,128)(2,1)} %collective-permute-done.5.refs_2_.refs_6_, ...), custom_call_target="tpu_custom_call" | custom-call | flops 4697620480 | bytes 14548992 | tf_op jit(solution)/shard_map/input_grad/pallas_call | solution.py:41
  86.4 0.0 reduce-scatter.3.cloned.1.call-start
  86.5 0.1 collective-permute-start
  86.5 7.9 %collective-permute-done.1.refs_2_ = bf16[2,160,1792]{2,1,0:T(8,128)(2,1)S(1)} collective-permute-done((bf16[2,160,1792]{2,1,0:T(8,128)(2,1)S(1)}, bf16[2,160,1792]{2,1,0:T(8,128)(2,1)S(1)}, u32[]{:S(2)}, u32[]{:S(2)}) %collective-permute-start.1) | collective-permute-done | bytes 1146912 | tf_op jit(solution)/shard_map/ppermute | solution.py:144
  94.5 2.8 %collective-permute-done.2.refs_3_ = bf16[2,160,1792]{2,1,0:T(8,128)(2,1)S(1)} collective-permute-done((bf16[2,160,1792]{2,1,0:T(8,128)(2,1)S(1)}, bf16[2,160,1792]{2,1,0:T(8,128)(2,1)S(1)}, u32[]{:S(2)}, u32[]{:S(2)}) %collective-permute-start.2) | collective-permute-done | bytes 1146912 | tf_op jit(solution)/shard_map/ppermute | solution.py:144
  97.3 1.0 copy-done.6
  98.3 10.7 %input_grad.2 = bf16[640,1024]{1,0:T(8,128)(2,1)} custom-call(s32[1]{0:T(128)} %bitcast.row_ref, bf16[2,160,1792]{2,1,0:T(8,128)(2,1)} %copy-done.1, bf16[2,160,1792]{2,1,0:T(8,128)(2,1)} %copy-done.5, bf16[2,160,1792]{2,1,0:T(8,128)(2,1)} %copy-done.4, bf16[2,160,1792]{2,1,0:T(8,128)(2,1)} %copy-done.6, bf16[1792,1024]{1,0:T(8,128)(2,1)} %refs_4_.3, ...), custom_call_target="tpu_custom_call" | custom-call | flops 4697620480 | bytes 14548992 | tf_op jit(solution)/shard_map/input_grad/pallas_call | solution.py:41
  109.0 0.0 all-gather.5.cloned.1.call-done.refs_8_
  109.1 1.5 collective-permute-start.9
  110.6 7.0 %reduce-scatter.5.cloned.1.call-done = bf16[160,1024]{1,0:T(8,128)(2,1)} async-done(((bf16[640,1024]{1,0:T(8,128)(2,1)}), bf16[160,1024]{1,0:T(8,128)(2,1)}) %reduce-scatter.5.cloned.1.call-update) | async-done | bytes 327696 | tf_op jit(solution)/shard_map/reduce_scatter | solution.py:177
  117.6 1.5 collective-permute-start.8
  119.0 21.9 %collective-permute-done.9.refs_9_ = bf16[640,1024]{1,0:T(8,128)(2,1)S(1)} collective-permute-done((bf16[640,1024]{1,0:T(8,128)(2,1)}, bf16[640,1024]{1,0:T(8,128)(2,1)S(1)}, u32[]{:S(2)}, u32[]{:S(2)}) %collective-permute-start.9) | collective-permute-done | bytes 1310752 | tf_op jit(solution)/shard_map/ppermute | solution.py:141
  141.0 1.1 copy-done.2
  142.1 17.4 %weight_grads.1 = (f32[1792,1024]{1,0:T(8,128)}, f32[1792,1024]{1,0:T(8,128)}) custom-call(s32[1]{0:T(128)} %bitcast.row_ref, bf16[2,160,1792]{2,1,0:T(8,128)(2,1)} %copy-done.1, bf16[2,160,1792]{2,1,0:T(8,128)(2,1)} %copy-done.5, bf16[2,160,1792]{2,1,0:T(8,128)(2,1)} %copy-done.4, bf16[2,160,1792]{2,1,0:T(8,128)(2,1)} %copy-done.6, ...), custom_call_target="tpu_custom_call" | custom-call | flops 9395240960 | bytes 32768000 | tf_op jit(solution)/shard_map/weight_grads/pallas_call | solution.py:105
  159.5 1.8 %add_convert_fusion = bf16[160,1024]{1,0:T(8,128)(2,1)} fusion(bf16[160,1024]{1,0:T(8,128)(2,1)S(1)} %collective-permute-done.8, bf16[160,1024]{1,0:T(8,128)(2,1)} %reduce-scatter.3.cloned.1.call-done), kind=kLoop, calls=%fused_computation.5 | loop fusion | flops 655360 | bytes 983040 | tf_op jit(solution)/shard_map/convert_element_type | solution.py:182
  (24 shorter events, 0.1 us)
Async XLA Ops:
  7.2 2.1 %copy-start = (bf16[160,3584]{1,0:T(8,128)(2,1)S(1)}, bf16[160,3584]{1,0:T(8,128)(2,1)}, u32[]{:S(2)}) copy-start(bf16[160,3584]{1,0:T(8,128)(2,1)} %param.9) | copy-start | bytes 3440644
  7.2 38.4 %all-gather.3.cloned.1.call-start = ((), (), s32[]{:S(2)}) async-start(), calls=%async_computation.2 | async-start | bytes 1638400 | tf_op jit(solution)/shard_map/all_gather | solution.py:150
  9.2 99.8 %all-gather.5.cloned.1.call-start = ((), (), s32[]{:S(2)}) async-start(), calls=%async_computation.5 | async-start | bytes 1638400 | tf_op jit(solution)/shard_map/all_gather | solution.py:151
  11.7 28.3 %collective-permute-start.3 = (bf16[2,160,1792]{2,1,0:T(8,128)(2,1)S(1)}, bf16[2,160,1792]{2,1,0:T(8,128)(2,1)S(1)}, u32[]{:S(2)}, u32[]{:S(2)}) collective-permute-start(bf16[2,160,1792]{2,1,0:T(8,128)(2,1)S(1)} %pad_maximum_fusion.1), channel_id=1, source_target_pairs={{0,16},{16,0},{1,17},{17,1},{2,18},{18,2},{3,19},{19,3},{4,20},{20... | collective-permute-start | bytes 3440648 | tf_op jit(solution)/shard_map/ppermute | solution.py:141
  39.9 26.8 %copy-start.3 = (bf16[2,160,1792]{2,1,0:T(8,128)(2,1)}, bf16[2,160,1792]{2,1,0:T(8,128)(2,1)S(1)}, u32[]{:S(2)}) copy-start(bf16[2,160,1792]{2,1,0:T(8,128)(2,1)S(1)} %collective-permute-done.3.refs_0_.refs_4_) | copy-start | bytes 3440644
  39.9 26.7 %collective-permute-start.5 = (bf16[2,160,1792]{2,1,0:T(8,128)(2,1)S(1)}, bf16[2,160,1792]{2,1,0:T(8,128)(2,1)}, u32[]{:S(2)}, u32[]{:S(2)}) collective-permute-start(bf16[2,160,1792]{2,1,0:T(8,128)(2,1)S(1)} %collective-permute-done.3.refs_0_.refs_4_), channel_id=1, source_target_pairs={{0,8},{4,12},{8,0},{12,4},{1,9},{5,13},{9,1},{13,5},{2,10},{6,14},... | collective-permute-start | bytes 3440648 | tf_op jit(solution)/shard_map/ppermute | solution.py:144
  41.7 75.8 %reduce-scatter.5.cloned.1.call-start = ((), (), s32[]{:S(2)}) async-start(), calls=%async_computation.4 | async-start | bytes 1638400 | tf_op jit(solution)/shard_map/reduce_scatter | solution.py:177
  45.6 30.2 %collective-permute-start.7 = (bf16[640,1024]{1,0:T(8,128)(2,1)}, bf16[640,1024]{1,0:T(8,128)(2,1)}, u32[]{:S(2)}, u32[]{:S(2)}) collective-permute-start(bf16[640,1024]{1,0:T(8,128)(2,1)} %all-gather.3.cloned.1.call-done.refs_6_.refs_10_), channel_id=1, source_target_pairs={{0,16},{16,0},{1,17},{17,1},{2,18},{18,2},{3,19},{19,3},{4,20},{20... | collective-permute-start | bytes 3932168 | tf_op jit(solution)/shard_map/ppermute | solution.py:141
  47.0 28.0 %collective-permute-start.4 = (bf16[2,160,1792]{2,1,0:T(8,128)(2,1)S(1)}, bf16[2,160,1792]{2,1,0:T(8,128)(2,1)}, u32[]{:S(2)}, u32[]{:S(2)}) collective-permute-start(bf16[2,160,1792]{2,1,0:T(8,128)(2,1)S(1)} %collective-permute-done.3.refs_0_.refs_4_), channel_id=1, source_target_pairs={{0,4},{4,0},{8,12},{12,8},{1,5},{5,1},{9,13},{13,9},{2,6},{6,2},{1... | collective-permute-start | bytes 3440648 | tf_op jit(solution)/shard_map/ppermute | solution.py:144
  66.6 9.2 %collective-permute-start.6 = (bf16[2,160,1792]{2,1,0:T(8,128)(2,1)}, bf16[2,160,1792]{2,1,0:T(8,128)(2,1)}, u32[]{:S(2)}, u32[]{:S(2)}) collective-permute-start(bf16[2,160,1792]{2,1,0:T(8,128)(2,1)} %collective-permute-done.5.refs_2_.refs_6_), channel_id=1, source_target_pairs={{0,4},{4,0},{8,12},{12,8},{1,5},{5,1},{9,13},{13,9},{2,6},{6,2},{1... | collective-permute-start | bytes 3440648 | tf_op jit(solution)/shard_map/ppermute | solution.py:144
  66.7 19.7 %copy-start.1 = (bf16[2,160,1792]{2,1,0:T(8,128)(2,1)}, bf16[2,160,1792]{2,1,0:T(8,128)(2,1)S(1)}, u32[]{:S(2)}) copy-start(bf16[2,160,1792]{2,1,0:T(8,128)(2,1)S(1)} %pad_maximum_fusion.refs_0_) | copy-start | bytes 3440644
  66.7 27.7 %collective-permute-start.1 = (bf16[2,160,1792]{2,1,0:T(8,128)(2,1)S(1)}, bf16[2,160,1792]{2,1,0:T(8,128)(2,1)S(1)}, u32[]{:S(2)}, u32[]{:S(2)}) collective-permute-start(bf16[2,160,1792]{2,1,0:T(8,128)(2,1)S(1)} %pad_maximum_fusion.refs_0_), channel_id=1, source_target_pairs={{0,8},{4,12},{8,0},{12,4},{1,9},{5,13},{9,1},{13,5},{2,10},{6,14},... | collective-permute-start | bytes 3440648 | tf_op jit(solution)/shard_map/ppermute | solution.py:144
  86.4 73.1 %reduce-scatter.3.cloned.1.call-start = ((), (), s32[]{:S(2)}) async-start(), calls=%async_computation.3 | async-start | bytes 1638400 | tf_op jit(solution)/shard_map/reduce_scatter | solution.py:177
  86.5 8.0 %collective-permute-start = (bf16[2,160,1792]{2,1,0:T(8,128)(2,1)S(1)}, bf16[2,160,1792]{2,1,0:T(8,128)(2,1)S(1)}, u32[]{:S(2)}, u32[]{:S(2)}) collective-permute-start(bf16[2,160,1792]{2,1,0:T(8,128)(2,1)S(1)} %pad_maximum_fusion.refs_0_), channel_id=1, source_target_pairs={{0,4},{4,0},{8,12},{12,8},{1,5},{5,1},{9,13},{13,9},{2,6},{6,2},{1... | collective-permute-start | bytes 3440648 | tf_op jit(solution)/shard_map/ppermute | solution.py:144
  94.5 2.8 %copy-start.4 = (bf16[2,160,1792]{2,1,0:T(8,128)(2,1)}, bf16[2,160,1792]{2,1,0:T(8,128)(2,1)S(1)}, u32[]{:S(2)}) copy-start(bf16[2,160,1792]{2,1,0:T(8,128)(2,1)S(1)} %collective-permute-done.1.refs_2_) | copy-start | bytes 3440644
  94.5 2.8 %collective-permute-start.2 = (bf16[2,160,1792]{2,1,0:T(8,128)(2,1)S(1)}, bf16[2,160,1792]{2,1,0:T(8,128)(2,1)S(1)}, u32[]{:S(2)}, u32[]{:S(2)}) collective-permute-start(bf16[2,160,1792]{2,1,0:T(8,128)(2,1)S(1)} %collective-permute-done.1.refs_2_), channel_id=1, source_target_pairs={{0,4},{4,0},{8,12},{12,8},{1,5},{5,1},{9,13},{13,9},{2,6},{6,2},{1... | collective-permute-start | bytes 3440648 | tf_op jit(solution)/shard_map/ppermute | solution.py:144
  94.5 2.8 %copy-start.5 = (bf16[2,160,1792]{2,1,0:T(8,128)(2,1)}, bf16[2,160,1792]{2,1,0:T(8,128)(2,1)S(1)}, u32[]{:S(2)}) copy-start(bf16[2,160,1792]{2,1,0:T(8,128)(2,1)S(1)} %collective-permute-done.refs_1_) | copy-start | bytes 3440644
  97.3 1.0 copy-start.6
  109.1 31.9 %collective-permute-start.9 = (bf16[640,1024]{1,0:T(8,128)(2,1)}, bf16[640,1024]{1,0:T(8,128)(2,1)S(1)}, u32[]{:S(2)}, u32[]{:S(2)}) collective-permute-start(bf16[640,1024]{1,0:T(8,128)(2,1)} %all-gather.5.cloned.1.call-done.refs_8_), channel_id=1, source_target_pairs={{0,16},{16,0},{1,17},{17,1},{2,18},{18,2},{3,19},{19,3},{4,20},{20... | collective-permute-start | bytes 3932168 | tf_op jit(solution)/shard_map/ppermute | solution.py:141
  117.6 41.9 %collective-permute-start.8 = (bf16[160,1024]{1,0:T(8,128)(2,1)}, bf16[160,1024]{1,0:T(8,128)(2,1)S(1)}, u32[]{:S(2)}, u32[]{:S(2)}) collective-permute-start(bf16[160,1024]{1,0:T(8,128)(2,1)} %reduce-scatter.5.cloned.1.call-done), channel_id=1, source_target_pairs={{0,16},{16,0},{1,17},{17,1},{2,18},{18,2},{3,19},{19,3},{4,20},{20... | collective-permute-start | bytes 983048 | tf_op jit(solution)/shard_map/ppermute | solution.py:141
  141.0 1.1 copy-start.2
Sparse Core Ops, SparseCore 0:
  10.2 35.3 all-gather.2
  47.1 31.6 all-gather.4
  86.5 31.0 reduce-scatter.4
  119.7 29.9 reduce-scatter.2

commit v2 on v1

v2 whole, which is shorter than its diff:
```python
import functools

import jax
import jax.numpy as jnp
from jax import lax
from jax.experimental import pallas as pl
from jax.experimental.pallas import tpu as pltpu
from jax.sharding import PartitionSpec as P

VMEM_LIMIT = 56 * 1024 * 1024


def grad_kernel(n_piece, turn_ref, *refs):
    pieces, (mean_ref, pert_ref, sign_ref, out_ref, both, sems) = refs[:n_piece], refs[n_piece:]

    @pl.when(pl.program_id(0) == 0)
    def _():
        copies = [
            pltpu.make_async_copy(pieces[k], both.at[turn_ref[0] ^ k], sems.at[k])
            for k in range(n_piece)
        ]
        for copy in copies:
            copy.start()
        for copy in copies:
            copy.wait()

    rows, hidden = both.shape[2:]
    grads = both[:, 0].reshape(n_piece * rows, hidden)
    signed = both[:, 1].reshape(n_piece * rows, hidden)
    part_a = jnp.dot(grads, mean_ref[...], preferred_element_type=jnp.float32)
    part_b = jnp.dot(signed, pert_ref[...], preferred_element_type=jnp.float32)
    for k in range(n_piece):
        at = slice(k * rows, (k + 1) * rows)
        sign = sign_ref[k].astype(jnp.float32)
        out_ref[k] = (part_a[at] + part_b[at] * sign).astype(out_ref.dtype)


def partial_input_grad(turn, pieces, mean_weight, perturbed, sign, weight):
    hidden, feats = mean_weight.shape
    n_piece = len(pieces)
    rows = sign.shape[1]
    tile = min(256, feats)
    any_spec = pl.BlockSpec(memory_space=pl.ANY)
    weight_spec = pl.BlockSpec((hidden, tile), lambda f, turn: (0, f))
    return pl.pallas_call(
        functools.partial(grad_kernel, n_piece),
        grid_spec=pltpu.PrefetchScalarGridSpec(
            num_scalar_prefetch=1,
            grid=(feats // tile,),
            in_specs=[any_spec] * n_piece
            + [weight_spec, weight_spec, pl.BlockSpec((n_piece, rows, tile), lambda f, turn: (0, 0, f))],
            out_specs=pl.BlockSpec((n_piece, rows, tile), lambda f, turn: (0, 0, f)),
            scratch_shapes=[
                pltpu.VMEM((n_piece,) + pieces[0].shape, jnp.bfloat16),
                pltpu.SemaphoreType.DMA((n_piece,)),
            ],
        ),
        out_shape=jax.ShapeDtypeStruct((n_piece, rows, feats), jnp.bfloat16),
        compiler_params=pltpu.CompilerParams(vmem_limit_bytes=VMEM_LIMIT),
        cost_estimate=pl.CostEstimate(
            flops=int(weight * n_piece * rows * hidden * feats),
            bytes_accessed=4 * (n_piece * rows * (hidden + feats) + hidden * feats),
            transcendentals=0,
        ),
        name="input_grad",
    )(turn, *pieces, mean_weight, perturbed, sign)


def weight_kernel(n_slab, n_piece, n_input, scale, turn_ref, *refs):
    n_grads = n_slab * n_piece
    grads, inputs, refs = refs[:n_grads], refs[n_grads:n_grads + n_input], refs[n_grads + n_input:]
    signs, noise_ref, (mean_ref, sigma_ref, plain, signed) = refs[:n_slab], refs[n_slab], refs[-4:]
    rows = grads[0].shape[1]

    @pl.when(pl.program_id(1) == 0)
    def _():
        blocks = [ref.at[at] for ref in inputs for at in range(ref.shape[0])]
        for i, block in enumerate(blocks):
            j, k = i // n_piece, i % n_piece
            to = pl.ds(pl.multiple_of((j * n_piece + (k ^ turn_ref[0])) * rows, rows), rows)
            value = block[...]
            plain[to, :] = value
            signed[to, :] = value * signs[j][k]

    dims = (((0,), (0,)), ((), ()))
    grad = jnp.concatenate([g[0] for g in grads], axis=0)
    mean = lax.dot_general(grad, plain[...], dims, preferred_element_type=jnp.float32)
    mean_ref[...] = mean * scale
    grad = jnp.concatenate([g[1] for g in grads], axis=0)
    sigma = lax.dot_general(grad, signed[...], dims, preferred_element_type=jnp.float32)
    sigma_ref[...] = sigma * scale * noise_ref[...].astype(jnp.float32)


def weight_grads(turn, pieces, inputs, signs, noise, scale, part, partial):
    n_slab, n_piece = len(pieces), len(pieces[0])
    hidden, feats = noise.shape
    rows = pieces[0][0].shape[1]
    tokens = n_slab * n_piece * rows
    width = feats if tokens <= 1280 else min(256, feats)
    tile = 256 if hidden % 256 == 0 else hidden
    cut = (hidden // tile + 1) // 2
    first, steps = (0, cut) if part == 0 else (cut, hidden // tile - cut)
    if not steps:
        return partial
    grad_spec = pl.BlockSpec((2, rows, tile), lambda f, h, turn: (0, 0, h + first))
    out_spec = pl.BlockSpec((tile, width), lambda f, h, turn: (h + first, f))
    operands = [p for slab_pieces in pieces for p in slab_pieces] + inputs + signs + [noise]
    return pl.pallas_call(
        functools.partial(weight_kernel, n_slab, n_piece, len(inputs), scale),
        grid_spec=pltpu.PrefetchScalarGridSpec(
            num_scalar_prefetch=1,
            grid=(feats // width, steps),
            in_specs=[grad_spec] * (n_slab * n_piece)
            + [pl.BlockSpec(x.shape[:2] + (width,), lambda f, h, turn: (0, 0, f)) for x in inputs + signs]
            + [out_spec]
            + [pl.BlockSpec(memory_space=pl.ANY)] * len(partial),
            out_specs=[out_spec, out_spec],
            scratch_shapes=[
                pltpu.VMEM((tokens, width), jnp.bfloat16),
                pltpu.VMEM((tokens, width), jnp.bfloat16),
            ],
        ),
        out_shape=[jax.ShapeDtypeStruct((hidden, feats), jnp.float32)] * 2,
        input_output_aliases={1 + len(operands) + i: i for i in range(len(partial))},
        compiler_params=pltpu.CompilerParams(vmem_limit_bytes=VMEM_LIMIT),
        cost_estimate=pl.CostEstimate(
            flops=4 * tokens * tile * steps * feats,
            bytes_accessed=4 * (tokens * tile * steps + tokens * feats) + 10 * tile * steps * feats,
            transcendentals=0,
        ),
        name="weight_grads",
    )(turn, *operands, *partial)


def local(inputs, in_bits, out_grads, out_bits, mean_weight, sigma_weight, noise):
    n_depth, n_row, n_col = (lax.axis_size(a) for a in ("depth", "row", "col"))
    depth, row, col = (lax.axis_index(a) for a in ("depth", "row", "col"))
    hidden = mean_weight.shape[0]
    scale = (inputs.shape[0] * n_col * n_depth) ** (-0.5)
    turn = (row ^ col).astype(jnp.int32).reshape(1)

    def hop(value, step):
        return lax.ppermute(value, "depth", [(i, (i + step) % n_depth) for i in range(n_depth)])

    def swap(value, bit):
        return lax.ppermute(value, "row", [(i, i ^ bit) for i in range(n_row)])

    def cross(value, bits):
        return lax.ppermute(value, "col", [(i, i ^ bits) for i in range(n_col)])

    def half(step):
        start = ((depth + step) % n_depth) * hidden
        return jnp.stack([lax.dynamic_slice_in_dim(a, start, hidden, 1) for a in (out_grads, signed_grads)])

    def tie(*values):
        return lax.optimization_barrier(values)

    signed_grads = out_grads * (1 - 2 * out_bits).astype(jnp.bfloat16)
    signed_grads, in_bits = tie(signed_grads, in_bits)
    in_sign = (1 - 2 * in_bits).astype(jnp.bfloat16)
    perturbed = (sigma_weight.astype(jnp.float32) * noise.astype(jnp.float32)).astype(jnp.bfloat16)

    mine = half(0)
    others = [hop(half(j), j) for j in range(1, n_depth)]
    signs = [in_sign, cross(in_sign, 1), None, cross(in_sign, 3)]
    signs[1], signs[3] = tie(signs[1], signs[3])
    signs[2] = cross(signs[3], 1)
    across, perturbed, signs[2] = tie(swap(mine, 2), perturbed, signs[2])
    pieces = [[mine, swap(mine, 1), across, swap(across, 1)]]
    pieces[0], others, signs, inputs = tie(pieces[0], others, jnp.stack(signs), inputs)

    own = partial_input_grad(turn, pieces[0], mean_weight, perturbed, signs, 64)
    blocks = [inputs, cross(inputs, 1), None, cross(inputs, 3)]
    blocks[1], blocks[3], own = tie(blocks[1], blocks[3], own)
    blocks[2] = cross(blocks[3], 1)
    passed = cross(own[2], 1)
    across = [swap(other, 2) for other in others]
    slab_sign = [signs] + [hop(signs, j) for j in range(1, n_depth)]
    across, slab_sign, blocks[2], passed = tie(across, slab_sign, blocks[2], passed)
    blocks = jnp.stack(blocks)

    def scatter(part, passed):
        joined = (part[3].astype(jnp.float32) + passed.astype(jnp.float32)).astype(jnp.bfloat16)
        return [part[0], cross(part[1], 1), cross(joined, 3)]

    owned = scatter(own, passed)
    slab_inputs = [blocks]
    total, grads = None, []
    for j in range(1, n_depth):
        hopped = hop(blocks, j)
        pieces.append([others[j - 1], swap(others[j - 1], 1), across[j - 1], swap(across[j - 1], 1)])
        part = partial_input_grad(turn, pieces[j], mean_weight, perturbed, slab_sign[j], 64)
        part, owned = tie(part, owned)
        if j == 1:
            total = sum(x.astype(jnp.float32) for x in owned)
        parts = scatter(part, cross(part[2], 1))
        parts[0], hopped = tie(parts[0], hopped)
        slab_inputs.append(hopped)
        if j == n_depth - 1:
            grads = weight_grads(turn, pieces, slab_inputs, slab_sign, noise, scale, 0, [])
            parts, grads = tie(parts, grads)
        part = sum(x.astype(jnp.float32) for x in parts).astype(jnp.bfloat16)
        total += hop(part, n_depth - j).astype(jnp.float32)
    input_grad = total.astype(jnp.bfloat16)
    grads = weight_grads(turn, pieces, slab_inputs, slab_sign, noise, scale, 1, grads)
    mean_grad, sigma_grad = grads
    return (input_grad, mean_grad, sigma_grad)


def solution(mesh):
    return jax.shard_map(
        local,
        mesh=mesh,
        in_specs=(
            P(("depth", "col"), "row"),
            P(("depth", "col"), "row"),
            P(("depth", "row"), "col"),
            P(("depth", "row"), "col"),
            P(("col", "depth"), "row"),
            P(("col", "depth"), "row"),
            P(("col", "depth"), "row"),
        ),
        out_specs=(
            P(("depth", "col"), "row"),
            P(("col", "depth"), "row"),
            P(("col", "depth"), "row"),
        ),
        check_vma=False,
    )
```

time: 168 us -> 137 us (0.82)
  waiting for transfers between devices: 89 us -> 48.6 us
  starting transfers between devices: 11 us -> 24.9 us
  between operations: 13.9 us -> 0.94 us
  Pallas kernels: 38.7 us -> 42.8 us
  local copies, waits for them, and re-layouts: 2.3 us -> 5.49 us
    ppermute x6, waiting for transfers between devices: 30.3 us -> 0.02 us  [swap(): return lax.ppermute(value, 'row', [(i, i ^ bit) for i in range(n_row)])]
    ppermute x4 -> x16, starting transfers between devices: 7.43 us -> 21.2 us  [the longest x12 15.1 us: cross(): return lax.ppermute(value, 'col', [(i, i ^ bits) for i in range(n_col)])]
    reduce_scatter x2 -> x0, waiting for transfers between devices: 7.04 us -> none  [local(): owned = lax.psum_scatter(part, 'col', scatter_dimension=0, tiled=True)]
    pallas_call x1 -> x2, Pallas kernels: 17.4 us -> 21.5 us  [weight_grads(): pl.pallas_call(functools.partial(weight_kernel, n_slab, n_piece, len(inpu...]
    all_gather x2 -> x0, waiting for transfers between devices: 3.82 us -> none  [the longest x1 3.8 us: local(): slab_sign = [lax.all_gather(in_sign, 'col', axis=0, tiled=True)]]
    convert_element_type x0 -> x3, other arithmetic: none -> 3.24 us  [the longest x2 3.08 us: scatter(): (part[3].astype(jnp.float32) + passed.astype(jnp.float32)).astype(jnp.bfl...]
    squeeze x0 -> x2, local copies, waits for them, and re-layouts: none -> 3.2 us  [the longest x1 1.96 us: scatter(): return [part[0], cross(part[1], 1), cross(joined, 3)]]
    convert_element_type x1, other arithmetic: 6.84 us -> 3.68 us  [local(): (sigma_weight.astype(jnp.float32) * noise.astype(jnp.float32)).astype(jnp...]
  transfers between devices with their start and end apart: 14 -> 22, of which waited for: 8 -> 9; matrix products, arithmetic and copies ran while one was open for 6% -> 9% of each run, Pallas kernels for 23% -> 32%
where the time goes in v2:
time: 137 us; the launch traced here: 136 us
  waiting for transfers between devices  48.6 us (35%)
  Pallas kernels  42.8 us (31%)
  starting transfers between devices  24.9 us (18%)
  other arithmetic  13 us (9%)
  local copies, waits for them, and re-layouts  5.49 us (4%)
    ppermute x12, waiting for transfers between devices, cross(): return lax.ppermute(value, 'col', [(i, i ^ bits) for i in range(n_col)])  28.8 us
    pallas_call x2, Pallas kernels, weight_grads(): pl.pallas_call(functools.partial(weight_kernel, n_slab, n_piece, len(inpu...  21.5 us
    pallas_call x2, Pallas kernels, partial_input_grad(): pl.pallas_call(functools.partial(grad_kernel, n_piece), grid_spec=pltpu.P...  21.2 us
    ppermute x4, waiting for transfers between devices, hop(): lax.ppermute(value, 'depth', [(i, (i + step) % n_depth) for i in range(n_...  19.8 us
    ppermute x12, starting transfers between devices, cross(): return lax.ppermute(value, 'col', [(i, i ^ bits) for i in range(n_col)])  15.1 us
    ppermute x4, starting transfers between devices, hop(): lax.ppermute(value, 'depth', [(i, (i + step) % n_depth) for i in range(n_...  6.11 us
    ppermute x6, starting transfers between devices, swap(): return lax.ppermute(value, 'row', [(i, i ^ bit) for i in range(n_row)])  3.72 us
    convert_element_type x1, other arithmetic, local(): (sigma_weight.astype(jnp.float32) * noise.astype(jnp.float32)).astype(jnp...  3.68 us
  transfers between devices with their start and end apart: 22, of which 9 were waited for; matrix products, arithmetic and copies ran while one was open for 9% of the time, Pallas kernels for 32%

profile of v2, /device:TPU:0, one launch (start us, length us, event | category | flops | bytes accessed | tf_op | source)
XLA Modules:
  0.0 135.7 jit_solution(13699462940254593502)
XLA Ops:
  0.7 2.5 %fusion = bf16[160,3584]{1,0:T(8,128)(2,1)S(1)} fusion(bf16[160,3584]{1,0:T(8,128)(2,1)} %param.9, s32[160,3584]{1,0:T(8,128)} %param.10), kind=kLoop, calls=%fused_computation.4 | loop fusion | flops 2293760 | bytes 4587520 | tf_op jit(solution)/shard_map/mul | solution.py:158
  3.5 3.0 %collective-permute-start.1 = (bf16[2,160,1792]{2,1,0:T(8,128)(2,1)S(1)}, bf16[2,160,1792]{2,1,0:T(8,128)(2,1)}, u32[]{:S(2)}, u32[]{:S(2)}) collective-permute-start(bf16[2,160,1792]{2,1,0:T(8,128)(2,1)S(1)} %pad_maximum_fusion.2.refs_0_), channel_id=1, source_target_pairs={{0,8},{4,12},{8,0},{12,4},{1,9},{5,13},{9,1},{13,5},{2,10},{6,14},... | collective-permute-start | bytes 3440648 | tf_op jit(solution)/shard_map/ppermute | solution.py:146
  6.7 1.6 %collective-permute-start.2 = (bf16[160,1024]{1,0:T(8,128)(2,1)S(1)}, bf16[160,1024]{1,0:T(8,128)(2,1)S(1)}, u32[]{:S(2)}, u32[]{:S(2)}) collective-permute-start(bf16[160,1024]{1,0:T(8,128)(2,1)S(1)} %subtract_convert_fusion.1), channel_id=1, source_target_pairs={{0,1},{1,0},{2,3},{3,2},{4,5},{5,4},{6,7},{7,6},{8,9},{9,8},{10,11... | collective-permute-start | bytes 983048 | tf_op jit(solution)/shard_map/ppermute | solution.py:149
  8.3 2.5 %collective-permute-start.3 = (bf16[160,1024]{1,0:T(8,128)(2,1)S(1)}, bf16[160,1024]{1,0:T(8,128)(2,1)S(1)}, u32[]{:S(2)}, u32[]{:S(2)}) collective-permute-start(bf16[160,1024]{1,0:T(8,128)(2,1)S(1)} %subtract_convert_fusion.1), channel_id=1, source_target_pairs={{0,3},{1,2},{2,1},{3,0},{4,7},{5,6},{6,5},{7,4},{8,11},{9,10},{10,... | collective-permute-start | bytes 983048 | tf_op jit(solution)/shard_map/ppermute | solution.py:149
  10.8 1.1 pad_maximum_fusion.3
  11.9 1.5 %collective-permute-start.6 = (bf16[2,160,1792]{2,1,0:T(8,128)(2,1)}, bf16[2,160,1792]{2,1,0:T(8,128)(2,1)}, u32[]{:S(2)}, u32[]{:S(2)}) collective-permute-start(bf16[2,160,1792]{2,1,0:T(8,128)(2,1)} %pad_maximum_fusion.3), channel_id=1, source_target_pairs={{0,16},{16,0},{1,17},{17,1},{2,18},{18,2},{3,19},{19,3},{4,20},{20... | collective-permute-start | bytes 3440648 | tf_op jit(solution)/shard_map/ppermute | solution.py:143
  13.4 3.1 %collective-permute-done.2 = bf16[160,1024]{1,0:T(8,128)(2,1)S(1)} collective-permute-done((bf16[160,1024]{1,0:T(8,128)(2,1)S(1)}, bf16[160,1024]{1,0:T(8,128)(2,1)S(1)}, u32[]{:S(2)}, u32[]{:S(2)}) %collective-permute-start.2) | collective-permute-done | bytes 327712 | tf_op jit(solution)/shard_map/ppermute | solution.py:149
  16.5 8.6 %collective-permute-done.3 = bf16[160,1024]{1,0:T(8,128)(2,1)S(1)} collective-permute-done((bf16[160,1024]{1,0:T(8,128)(2,1)S(1)}, bf16[160,1024]{1,0:T(8,128)(2,1)S(1)}, u32[]{:S(2)}, u32[]{:S(2)}) %collective-permute-start.3) | collective-permute-done | bytes 327712 | tf_op jit(solution)/shard_map/ppermute | solution.py:149
  25.6 3.7 %multiply_convert_fusion.refs_5_ = bf16[1792,1024]{1,0:T(8,128)(2,1)} fusion(bf16[1792,1024]{1,0:T(8,128)(2,1)S(1)} %copy-done, bf16[1792,1024]{1,0:T(8,128)(2,1)S(1)} %copy-done.5), kind=kLoop, calls=%fused_computation | loop fusion | flops 7340032 | bytes 11010048 | tf_op jit(solution)/shard_map/convert_element_type | solution.py:161
  29.3 3.9 %collective-permute-done.4 = bf16[160,1024]{1,0:T(8,128)(2,1)S(1)} collective-permute-done((bf16[160,1024]{1,0:T(8,128)(2,1)S(1)}, bf16[160,1024]{1,0:T(8,128)(2,1)S(1)}, u32[]{:S(2)}, u32[]{:S(2)}) %collective-permute-start.4) | collective-permute-done | bytes 327712 | tf_op jit(solution)/shard_map/ppermute | solution.py:149
  33.5 6.3 %collective-permute-done.6.refs_0_.refs_4_ = bf16[2,160,1792]{2,1,0:T(8,128)(2,1)} collective-permute-done((bf16[2,160,1792]{2,1,0:T(8,128)(2,1)}, bf16[2,160,1792]{2,1,0:T(8,128)(2,1)}, u32[]{:S(2)}, u32[]{:S(2)}) %collective-permute-start.6) | collective-permute-done | bytes 1146912 | tf_op jit(solution)/shard_map/ppermute | solution.py:143
  42.1 1.5 %collective-permute-start.9 = (bf16[4,160,1024]{2,1,0:T(8,128)(2,1)S(1)}, bf16[4,160,1024]{2,1,0:T(8,128)(2,1)S(1)}, u32[]{:S(2)}, u32[]{:S(2)}) collective-permute-start(bf16[4,160,1024]{2,1,0:T(8,128)(2,1)S(1)} %pad_maximum_fusion.refs_6_.refs_10_), channel_id=1, source_target_pairs={{0,16},{16,0},{1,17},{17,1},{2,18},{18,2},{3,19},{19,3},{4,20},{20... | collective-permute-start | bytes 3932168 | tf_op jit(solution)/shard_map/ppermute | solution.py:143
  43.6 10.6 %input_grad.2 = bf16[4,160,1024]{2,1,0:T(8,128)(2,1)} custom-call(s32[1]{0:T(128)} %bitcast.turn_ref, bf16[2,160,1792]{2,1,0:T(8,128)(2,1)} %copy-done.4, bf16[2,160,1792]{2,1,0:T(8,128)(2,1)} %collective-permute-done.refs_1_, bf16[2,160,1792]{2,1,0:T(8,128)(2,1)} %collective-permute-done.1.refs_2_, bf16[2,160,1792]{2,1,0:T(8,128)(2,1)} %collective-permute-done.5.refs_3_, ...), custom_call_target="tpu_custom_call" | custom-call | flops 75161927680 | bytes 14548992 | tf_op jit(solution)/shard_map/input_grad/pallas_call | solution.py:45
  54.3 2.0 %collective-permute-done.10 = bf16[160,1024]{1,0:T(8,128)(2,1)S(1)} collective-permute-done((bf16[160,1024]{1,0:T(8,128)(2,1)S(1)}, bf16[160,1024]{1,0:T(8,128)(2,1)S(1)}, u32[]{:S(2)}, u32[]{:S(2)}) %collective-permute-start.10) | collective-permute-done | bytes 327712 | tf_op jit(solution)/shard_map/ppermute | solution.py:149
  56.2 1.7 %collective-permute-start.12 = (bf16[160,1024]{1,0:T(8,128)(2,1)S(1)}, bf16[160,1024]{1,0:T(8,128)(2,1)S(1)}, u32[]{:S(2)}, u32[]{:S(2)}) collective-permute-start(bf16[160,1024]{1,0:T(8,128)(2,1)S(1)} %collective-permute-done.11), channel_id=1, source_target_pairs={{0,1},{1,0},{2,3},{3,2},{4,5},{5,4},{6,7},{7,6},{8,9},{9,8},{10,11... | collective-permute-start | bytes 983048 | tf_op jit(solution)/shard_map/ppermute | solution.py:149
  58.0 2.0 %slice_bitcast_fusion.3 = (bf16[160,1024]{1,0:T(8,128)(2,1)}, bf16[160,1024]{1,0:T(8,128)(2,1)S(1)}, bf16[160,1024]{1,0:T(8,128)(2,1)S(1)}) fusion(bf16[4,160,1024]{2,1,0:T(8,128)(2,1)} %input_grad.2), kind=kLoop, calls=%fused_computation.21 | loop fusion | bytes 1966080 | tf_op jit(solution)/shard_map/squeeze | solution.py:184
  60.2 6.7 %collective-permute-done.12 = bf16[160,1024]{1,0:T(8,128)(2,1)S(1)} collective-permute-done((bf16[160,1024]{1,0:T(8,128)(2,1)S(1)}, bf16[160,1024]{1,0:T(8,128)(2,1)S(1)}, u32[]{:S(2)}, u32[]{:S(2)}) %collective-permute-start.12) | collective-permute-done | bytes 327712 | tf_op jit(solution)/shard_map/ppermute | solution.py:149
  66.9 4.5 %collective-permute-done.13 = bf16[160,1024]{1,0:T(8,128)(2,1)S(1)} collective-permute-done((bf16[160,1024]{1,0:T(8,128)(2,1)S(1)}, bf16[160,1024]{1,0:T(8,128)(2,1)S(1)}, u32[]{:S(2)}, u32[]{:S(2)}) %collective-permute-start.13) | collective-permute-done | bytes 327712 | tf_op jit(solution)/shard_map/ppermute | solution.py:149
  72.6 1.8 %fusion.2 = bf16[160,1024]{1,0:T(8,128)(2,1)} fusion(bf16[160,1024]{1,0:T(8,128)(2,1)S(1)} %collective-permute-done.13, bf16[4,160,1024]{2,1,0:T(8,128)(2,1)} %input_grad.2), kind=kLoop, calls=%fused_computation.10 | loop fusion | flops 655360 | bytes 983040 | tf_op jit(solution)/shard_map/convert_element_type | solution.py:183
  74.4 2.5 %collective-permute-start.16 = (bf16[160,1024]{1,0:T(8,128)(2,1)}, bf16[160,1024]{1,0:T(8,128)(2,1)}, u32[]{:S(2)}, u32[]{:S(2)}) collective-permute-start(bf16[160,1024]{1,0:T(8,128)(2,1)} %fusion.2), channel_id=1, source_target_pairs={{0,3},{1,2},{2,1},{3,0},{4,7},{5,6},{6,5},{7,4},{8,11},{9,10},{10,... | collective-permute-start | bytes 983048 | tf_op jit(solution)/shard_map/ppermute | solution.py:149
  77.1 1.6 %collective-permute-start.17 = (bf16[4,160,1024]{2,1,0:T(8,128)(2,1)S(1)}, bf16[4,160,1024]{2,1,0:T(8,128)(2,1)S(1)}, u32[]{:S(2)}, u32[]{:S(2)}) collective-permute-start(bf16[4,160,1024]{2,1,0:T(8,128)(2,1)S(1)} %pad_maximum_fusion.1.refs_8_), channel_id=1, source_target_pairs={{0,16},{16,0},{1,17},{17,1},{2,18},{18,2},{3,19},{19,3},{4,20},{20... | collective-permute-start | bytes 3932168 | tf_op jit(solution)/shard_map/ppermute | solution.py:143
  78.7 1.1 copy-done.10
  80.7 10.6 %input_grad.3 = bf16[4,160,1024]{2,1,0:T(8,128)(2,1)} custom-call(s32[1]{0:T(128)} %bitcast.turn_ref, bf16[2,160,1792]{2,1,0:T(8,128)(2,1)} %collective-permute-done.6.refs_0_.refs_4_, bf16[2,160,1792]{2,1,0:T(8,128)(2,1)} %copy-done.10, bf16[2,160,1792]{2,1,0:T(8,128)(2,1)} %copy-done.9, bf16[2,160,1792]{2,1,0:T(8,128)(2,1)} %copy-done.11, ...), custom_call_target="tpu_custom_call" | custom-call | flops 75161927680 | bytes 14548992 | tf_op jit(solution)/shard_map/input_grad/pallas_call | solution.py:45
  91.4 1.2 slice_bitcast_fusion
  92.6 1.7 %collective-permute-start.19 = (bf16[160,1024]{1,0:T(8,128)(2,1)S(1)}, bf16[160,1024]{1,0:T(8,128)(2,1)S(1)}, u32[]{:S(2)}, u32[]{:S(2)}) collective-permute-start(bf16[160,1024]{1,0:T(8,128)(2,1)S(1)} %get-tuple-element.77), channel_id=1, source_target_pairs={{0,1},{1,0},{2,3},{3,2},{4,5},{5,4},{6,7},{7,6},{8,9},{9,8},{10,11... | collective-permute-start | bytes 983048 | tf_op jit(solution)/shard_map/ppermute | solution.py:149
  94.7 13.1 %collective-permute-done.17.refs_9_ = bf16[4,160,1024]{2,1,0:T(8,128)(2,1)S(1)} collective-permute-done((bf16[4,160,1024]{2,1,0:T(8,128)(2,1)S(1)}, bf16[4,160,1024]{2,1,0:T(8,128)(2,1)S(1)}, u32[]{:S(2)}, u32[]{:S(2)}) %collective-permute-start.17) | collective-permute-done | bytes 1310752 | tf_op jit(solution)/shard_map/ppermute | solution.py:143
  107.8 1.3 fusion.1
  109.1 1.4 %collective-permute-start.20 = (bf16[160,1024]{1,0:T(8,128)(2,1)S(1)}, bf16[160,1024]{1,0:T(8,128)(2,1)S(1)}, u32[]{:S(2)}, u32[]{:S(2)}) collective-permute-start(bf16[160,1024]{1,0:T(8,128)(2,1)S(1)} %fusion.1), channel_id=1, source_target_pairs={{0,3},{1,2},{2,1},{3,0},{4,7},{5,6},{6,5},{7,4},{8,11},{9,10},{10,... | collective-permute-start | bytes 983048 | tf_op jit(solution)/shard_map/ppermute | solution.py:149
  110.5 11.6 %weight_grads.2 = (f32[1792,1024]{1,0:T(8,128)}, f32[1792,1024]{1,0:T(8,128)}) custom-call(s32[1]{0:T(128)} %bitcast.turn_ref, bf16[2,160,1792]{2,1,0:T(8,128)(2,1)} %copy-done.4, bf16[2,160,1792]{2,1,0:T(8,128)(2,1)} %collective-permute-done.refs_1_, bf16[2,160,1792]{2,1,0:T(8,128)(2,1)} %collective-permute-done.1.refs_2_, ...), custom_call_target="tpu_custom_call" | custom-call | flops 5368709120 | bytes 20971520 | tf_op jit(solution)/shard_map/weight_grads/pallas_call | solution.py:108
  122.3 1.6 %collective-permute-start.21 = (bf16[160,1024]{1,0:T(8,128)(2,1)S(1)}, bf16[160,1024]{1,0:T(8,128)(2,1)S(1)}, u32[]{:S(2)}, u32[]{:S(2)}) collective-permute-start(bf16[160,1024]{1,0:T(8,128)(2,1)S(1)} %add_convert_fusion.1), channel_id=1, source_target_pairs={{0,16},{16,0},{1,17},{17,1},{2,18},{18,2},{3,19},{19,3},{4,20},{20... | collective-permute-start | bytes 983048 | tf_op jit(solution)/shard_map/ppermute | solution.py:143
  123.8 9.9 %weight_grads.3 = (f32[1792,1024]{1,0:T(8,128)}, f32[1792,1024]{1,0:T(8,128)}) custom-call(s32[1]{0:T(128)} %bitcast.turn_ref, bf16[2,160,1792]{2,1,0:T(8,128)(2,1)} %copy-done.4, bf16[2,160,1792]{2,1,0:T(8,128)(2,1)} %collective-permute-done.refs_1_, ...), custom_call_target="tpu_custom_call", output_to_operand_aliasing={{0}: (14, {}), {1}: (15, {})} | custom-call | flops 4026531840 | bytes 17039360 | tf_op jit(solution)/shard_map/weight_grads/pallas_call | solution.py:108
  133.8 1.9 %add_convert_fusion = bf16[160,1024]{1,0:T(8,128)(2,1)} fusion(bf16[160,1024]{1,0:T(8,128)(2,1)S(1)} %collective-permute-done.21, bf16[160,1024]{1,0:T(8,128)(2,1)} %collective-permute-done.16, bf16[160,1024]{1,0:T(8,128)(2,1)S(1)} %collective-permute-done.15, bf16[160,1024]{1,0:T(8,128)(2,1)S(1)} %get-tuple-element.59), kind=kLoop, calls=%fused_computation.11 | loop fusion | flops 1310720 | bytes 1638400 | tf_op jit(solution)/shard_map/convert_element_type | solution.py:204
  (58 shorter events, 6.7 us)
Async XLA Ops:
  3.2 3.4 %copy-start.6 = (s32[160,1024]{1,0:T(8,128)S(1)}, s32[160,1024]{1,0:T(8,128)}, u32[]{:S(2)}) copy-start(s32[160,1024]{1,0:T(8,128)} %param.8) | copy-start | bytes 1966084
  3.3 22.3 %copy-start.5 = (bf16[1792,1024]{1,0:T(8,128)(2,1)S(1)}, bf16[1792,1024]{1,0:T(8,128)(2,1)}, u32[]{:S(2)}) copy-start(bf16[1792,1024]{1,0:T(8,128)(2,1)} %param.12) | copy-start | bytes 11010052
  3.4 22.2 %copy-start = (bf16[1792,1024]{1,0:T(8,128)(2,1)S(1)}, bf16[1792,1024]{1,0:T(8,128)(2,1)}, u32[]{:S(2)}) copy-start(bf16[1792,1024]{1,0:T(8,128)(2,1)} %refs_12_.3) | copy-start | bytes 11010052
  3.5 8.4 %copy-start.4 = (bf16[2,160,1792]{2,1,0:T(8,128)(2,1)}, bf16[2,160,1792]{2,1,0:T(8,128)(2,1)S(1)}, u32[]{:S(2)}) copy-start(bf16[2,160,1792]{2,1,0:T(8,128)(2,1)S(1)} %pad_maximum_fusion.2.refs_0_) | copy-start | bytes 3440644
  3.5 29.7 %collective-permute-start.1 = (bf16[2,160,1792]{2,1,0:T(8,128)(2,1)S(1)}, bf16[2,160,1792]{2,1,0:T(8,128)(2,1)}, u32[]{:S(2)}, u32[]{:S(2)}) collective-permute-start(bf16[2,160,1792]{2,1,0:T(8,128)(2,1)S(1)} %pad_maximum_fusion.2.refs_0_), channel_id=1, source_target_pairs={{0,8},{4,12},{8,0},{12,4},{1,9},{5,13},{9,1},{13,5},{2,10},{6,14},... | collective-permute-start | bytes 3440648 | tf_op jit(solution)/shard_map/ppermute | solution.py:146
  6.7 9.8 %collective-permute-start.2 = (bf16[160,1024]{1,0:T(8,128)(2,1)S(1)}, bf16[160,1024]{1,0:T(8,128)(2,1)S(1)}, u32[]{:S(2)}, u32[]{:S(2)}) collective-permute-start(bf16[160,1024]{1,0:T(8,128)(2,1)S(1)} %subtract_convert_fusion.1), channel_id=1, source_target_pairs={{0,1},{1,0},{2,3},{3,2},{4,5},{5,4},{6,7},{7,6},{8,9},{9,8},{10,11... | collective-permute-start | bytes 983048 | tf_op jit(solution)/shard_map/ppermute | solution.py:149
  8.3 16.7 %collective-permute-start.3 = (bf16[160,1024]{1,0:T(8,128)(2,1)S(1)}, bf16[160,1024]{1,0:T(8,128)(2,1)S(1)}, u32[]{:S(2)}, u32[]{:S(2)}) collective-permute-start(bf16[160,1024]{1,0:T(8,128)(2,1)S(1)} %subtract_convert_fusion.1), channel_id=1, source_target_pairs={{0,3},{1,2},{2,1},{3,0},{4,7},{5,6},{6,5},{7,4},{8,11},{9,10},{10,... | collective-permute-start | bytes 983048 | tf_op jit(solution)/shard_map/ppermute | solution.py:149
  10.8 22.8 %collective-permute-start = (bf16[2,160,1792]{2,1,0:T(8,128)(2,1)S(1)}, bf16[2,160,1792]{2,1,0:T(8,128)(2,1)}, u32[]{:S(2)}, u32[]{:S(2)}) collective-permute-start(bf16[2,160,1792]{2,1,0:T(8,128)(2,1)S(1)} %pad_maximum_fusion.2.refs_0_), channel_id=1, source_target_pairs={{0,4},{4,0},{8,12},{12,8},{1,5},{5,1},{9,13},{13,9},{2,6},{6,2},{1... | collective-permute-start | bytes 3440648 | tf_op jit(solution)/shard_map/ppermute | solution.py:146
  11.9 28.0 %collective-permute-start.6 = (bf16[2,160,1792]{2,1,0:T(8,128)(2,1)}, bf16[2,160,1792]{2,1,0:T(8,128)(2,1)}, u32[]{:S(2)}, u32[]{:S(2)}) collective-permute-start(bf16[2,160,1792]{2,1,0:T(8,128)(2,1)} %pad_maximum_fusion.3), channel_id=1, source_target_pairs={{0,16},{16,0},{1,17},{17,1},{2,18},{18,2},{3,19},{19,3},{4,20},{20... | collective-permute-start | bytes 3440648 | tf_op jit(solution)/shard_map/ppermute | solution.py:143
  25.0 8.2 %collective-permute-start.4 = (bf16[160,1024]{1,0:T(8,128)(2,1)S(1)}, bf16[160,1024]{1,0:T(8,128)(2,1)S(1)}, u32[]{:S(2)}, u32[]{:S(2)}) collective-permute-start(bf16[160,1024]{1,0:T(8,128)(2,1)S(1)} %collective-permute-done.3), channel_id=1, source_target_pairs={{0,1},{1,0},{2,3},{3,2},{4,5},{5,4},{6,7},{7,6},{8,9},{9,8},{10,11... | collective-permute-start | bytes 983048 | tf_op jit(solution)/shard_map/ppermute | solution.py:149
  33.2 6.6 %collective-permute-start.5 = (bf16[2,160,1792]{2,1,0:T(8,128)(2,1)}, bf16[2,160,1792]{2,1,0:T(8,128)(2,1)}, u32[]{:S(2)}, u32[]{:S(2)}) collective-permute-start(bf16[2,160,1792]{2,1,0:T(8,128)(2,1)} %collective-permute-done.1.refs_2_), channel_id=1, source_target_pairs={{0,4},{4,0},{8,12},{12,8},{1,5},{5,1},{9,13},{13,9},{2,6},{6,2},{1... | collective-permute-start | bytes 3440648 | tf_op jit(solution)/shard_map/ppermute | solution.py:146
  33.3 6.5 %copy-start.12 = (bf16[160,1024]{1,0:T(8,128)(2,1)S(1)}, bf16[160,1024]{1,0:T(8,128)(2,1)}, u32[]{:S(2)}) copy-start(bf16[160,1024]{1,0:T(8,128)(2,1)} %param.7) | copy-start | bytes 983044
  33.5 10.1 %copy-start.1 = (bf16[4,160,1024]{2,1,0:T(8,128)(2,1)}, bf16[4,160,1024]{2,1,0:T(8,128)(2,1)S(1)}, u32[]{:S(2)}) copy-start(bf16[4,160,1024]{2,1,0:T(8,128)(2,1)S(1)} %pad_maximum_fusion.refs_6_.refs_10_) | copy-start | bytes 3932164
  39.9 16.4 %collective-permute-start.10 = (bf16[160,1024]{1,0:T(8,128)(2,1)S(1)}, bf16[160,1024]{1,0:T(8,128)(2,1)S(1)}, u32[]{:S(2)}, u32[]{:S(2)}) collective-permute-start(bf16[160,1024]{1,0:T(8,128)(2,1)S(1)} %copy-done.12), channel_id=1, source_target_pairs={{0,1},{1,0},{2,3},{3,2},{4,5},{5,4},{6,7},{7,6},{8,9},{9,8},{10,11... | collective-permute-start | bytes 983048 | tf_op jit(solution)/shard_map/ppermute | solution.py:149
  40.6 15.7 %collective-permute-start.11 = (bf16[160,1024]{1,0:T(8,128)(2,1)S(1)}, bf16[160,1024]{1,0:T(8,128)(2,1)S(1)}, u32[]{:S(2)}, u32[]{:S(2)}) collective-permute-start(bf16[160,1024]{1,0:T(8,128)(2,1)S(1)} %copy-done.12), channel_id=1, source_target_pairs={{0,3},{1,2},{2,1},{3,0},{4,7},{5,6},{6,5},{7,4},{8,11},{9,10},{10,... | collective-permute-start | bytes 983048 | tf_op jit(solution)/shard_map/ppermute | solution.py:149
  41.5 30.0 %collective-permute-start.8 = (bf16[2,160,1792]{2,1,0:T(8,128)(2,1)}, bf16[2,160,1792]{2,1,0:T(8,128)(2,1)S(1)}, u32[]{:S(2)}, u32[]{:S(2)}) collective-permute-start(bf16[2,160,1792]{2,1,0:T(8,128)(2,1)} %collective-permute-done.6.refs_0_.refs_4_), channel_id=1, source_target_pairs={{0,8},{4,12},{8,0},{12,4},{1,9},{5,13},{9,1},{13,5},{2,10},{6,14},... | collective-permute-start | bytes 3440648 | tf_op jit(solution)/shard_map/ppermute | solution.py:146
  42.1 29.7 %collective-permute-start.9 = (bf16[4,160,1024]{2,1,0:T(8,128)(2,1)S(1)}, bf16[4,160,1024]{2,1,0:T(8,128)(2,1)S(1)}, u32[]{:S(2)}, u32[]{:S(2)}) collective-permute-start(bf16[4,160,1024]{2,1,0:T(8,128)(2,1)S(1)} %pad_maximum_fusion.refs_6_.refs_10_), channel_id=1, source_target_pairs={{0,16},{16,0},{1,17},{17,1},{2,18},{18,2},{3,19},{19,3},{4,20},{20... | collective-permute-start | bytes 3932168 | tf_op jit(solution)/shard_map/ppermute | solution.py:143
  56.2 10.7 %collective-permute-start.12 = (bf16[160,1024]{1,0:T(8,128)(2,1)S(1)}, bf16[160,1024]{1,0:T(8,128)(2,1)S(1)}, u32[]{:S(2)}, u32[]{:S(2)}) collective-permute-start(bf16[160,1024]{1,0:T(8,128)(2,1)S(1)} %collective-permute-done.11), channel_id=1, source_target_pairs={{0,1},{1,0},{2,3},{3,2},{4,5},{5,4},{6,7},{7,6},{8,9},{9,8},{10,11... | collective-permute-start | bytes 983048 | tf_op jit(solution)/shard_map/ppermute | solution.py:149
  60.0 11.5 %collective-permute-start.13 = (bf16[160,1024]{1,0:T(8,128)(2,1)S(1)}, bf16[160,1024]{1,0:T(8,128)(2,1)S(1)}, u32[]{:S(2)}, u32[]{:S(2)}) collective-permute-start(bf16[160,1024]{1,0:T(8,128)(2,1)S(1)} %get-tuple-element.82), channel_id=1, source_target_pairs={{0,1},{1,0},{2,3},{3,2},{4,5},{5,4},{6,7},{7,6},{8,9},{9,8},{10,11... | collective-permute-start | bytes 983048 | tf_op jit(solution)/shard_map/ppermute | solution.py:149
  60.2 18.4 %collective-permute-start.7 = (bf16[2,160,1792]{2,1,0:T(8,128)(2,1)}, bf16[2,160,1792]{2,1,0:T(8,128)(2,1)S(1)}, u32[]{:S(2)}, u32[]{:S(2)}) collective-permute-start(bf16[2,160,1792]{2,1,0:T(8,128)(2,1)} %collective-permute-done.6.refs_0_.refs_4_), channel_id=1, source_target_pairs={{0,4},{4,0},{8,12},{12,8},{1,5},{5,1},{9,13},{13,9},{2,6},{6,2},{1... | collective-permute-start | bytes 3440648 | tf_op jit(solution)/shard_map/ppermute | solution.py:146
  71.4 5.6 %copy-start.9 = (bf16[2,160,1792]{2,1,0:T(8,128)(2,1)}, bf16[2,160,1792]{2,1,0:T(8,128)(2,1)S(1)}, u32[]{:S(2)}) copy-start(bf16[2,160,1792]{2,1,0:T(8,128)(2,1)S(1)} %collective-permute-done.8.refs_2_.refs_6_) | copy-start | bytes 3440644
  71.8 5.2 %copy-start.7 = (bf16[4,160,1024]{2,1,0:T(8,128)(2,1)}, bf16[4,160,1024]{2,1,0:T(8,128)(2,1)S(1)}, u32[]{:S(2)}) copy-start(bf16[4,160,1024]{2,1,0:T(8,128)(2,1)S(1)} %collective-permute-done.9.refs_6_.refs_11_) | copy-start | bytes 3932164
  71.8 6.8 %collective-permute-start.14 = (bf16[2,160,1792]{2,1,0:T(8,128)(2,1)S(1)}, bf16[2,160,1792]{2,1,0:T(8,128)(2,1)S(1)}, u32[]{:S(2)}, u32[]{:S(2)}) collective-permute-start(bf16[2,160,1792]{2,1,0:T(8,128)(2,1)S(1)} %collective-permute-done.8.refs_2_.refs_6_), channel_id=1, source_target_pairs={{0,4},{4,0},{8,12},{12,8},{1,5},{5,1},{9,13},{13,9},{2,6},{6,2},{1... | collective-permute-start | bytes 3440648 | tf_op jit(solution)/shard_map/ppermute | solution.py:146
  71.8 19.5 %collective-permute-start.15 = (bf16[160,1024]{1,0:T(8,128)(2,1)}, bf16[160,1024]{1,0:T(8,128)(2,1)S(1)}, u32[]{:S(2)}, u32[]{:S(2)}) collective-permute-start(bf16[160,1024]{1,0:T(8,128)(2,1)} %get-tuple-element.80), channel_id=1, source_target_pairs={{0,1},{1,0},{2,3},{3,2},{4,5},{5,4},{6,7},{7,6},{8,9},{9,8},{10,11... | collective-permute-start | bytes 983048 | tf_op jit(solution)/shard_map/ppermute | solution.py:149
  74.4 17.0 %collective-permute-start.16 = (bf16[160,1024]{1,0:T(8,128)(2,1)}, bf16[160,1024]{1,0:T(8,128)(2,1)}, u32[]{:S(2)}, u32[]{:S(2)}) collective-permute-start(bf16[160,1024]{1,0:T(8,128)(2,1)} %fusion.2), channel_id=1, source_target_pairs={{0,3},{1,2},{2,1},{3,0},{4,7},{5,6},{6,5},{7,4},{8,11},{9,10},{10,... | collective-permute-start | bytes 983048 | tf_op jit(solution)/shard_map/ppermute | solution.py:149
  77.1 14.3 %copy-start.2 = (bf16[4,160,1024]{2,1,0:T(8,128)(2,1)}, bf16[4,160,1024]{2,1,0:T(8,128)(2,1)S(1)}, u32[]{:S(2)}) copy-start(bf16[4,160,1024]{2,1,0:T(8,128)(2,1)S(1)} %pad_maximum_fusion.1.refs_8_) | copy-start | bytes 3932164
  77.1 30.7 %collective-permute-start.17 = (bf16[4,160,1024]{2,1,0:T(8,128)(2,1)S(1)}, bf16[4,160,1024]{2,1,0:T(8,128)(2,1)S(1)}, u32[]{:S(2)}, u32[]{:S(2)}) collective-permute-start(bf16[4,160,1024]{2,1,0:T(8,128)(2,1)S(1)} %pad_maximum_fusion.1.refs_8_), channel_id=1, source_target_pairs={{0,16},{16,0},{1,17},{17,1},{2,18},{18,2},{3,19},{19,3},{4,20},{20... | collective-permute-start | bytes 3932168 | tf_op jit(solution)/shard_map/ppermute | solution.py:143
  92.6 15.2 %collective-permute-start.19 = (bf16[160,1024]{1,0:T(8,128)(2,1)S(1)}, bf16[160,1024]{1,0:T(8,128)(2,1)S(1)}, u32[]{:S(2)}, u32[]{:S(2)}) collective-permute-start(bf16[160,1024]{1,0:T(8,128)(2,1)S(1)} %get-tuple-element.77), channel_id=1, source_target_pairs={{0,1},{1,0},{2,3},{3,2},{4,5},{5,4},{6,7},{7,6},{8,9},{9,8},{10,11... | collective-permute-start | bytes 983048 | tf_op jit(solution)/shard_map/ppermute | solution.py:149
  94.3 27.8 %collective-permute-start.18 = (bf16[160,1024]{1,0:T(8,128)(2,1)S(1)}, bf16[160,1024]{1,0:T(8,128)(2,1)S(1)}, u32[]{:S(2)}, u32[]{:S(2)}) collective-permute-start(bf16[160,1024]{1,0:T(8,128)(2,1)S(1)} %get-tuple-element.78), channel_id=1, source_target_pairs={{0,1},{1,0},{2,3},{3,2},{4,5},{5,4},{6,7},{7,6},{8,9},{9,8},{10,11... | collective-permute-start | bytes 983048 | tf_op jit(solution)/shard_map/ppermute | solution.py:149
  107.8 2.7 %copy-start.8 = (bf16[4,160,1024]{2,1,0:T(8,128)(2,1)}, bf16[4,160,1024]{2,1,0:T(8,128)(2,1)S(1)}, u32[]{:S(2)}) copy-start(bf16[4,160,1024]{2,1,0:T(8,128)(2,1)S(1)} %collective-permute-done.17.refs_9_) | copy-start | bytes 3932164
  109.1 13.0 %collective-permute-start.20 = (bf16[160,1024]{1,0:T(8,128)(2,1)S(1)}, bf16[160,1024]{1,0:T(8,128)(2,1)S(1)}, u32[]{:S(2)}, u32[]{:S(2)}) collective-permute-start(bf16[160,1024]{1,0:T(8,128)(2,1)S(1)} %fusion.1), channel_id=1, source_target_pairs={{0,3},{1,2},{2,1},{3,0},{4,7},{5,6},{6,5},{7,4},{8,11},{9,10},{10,... | collective-permute-start | bytes 983048 | tf_op jit(solution)/shard_map/ppermute | solution.py:149
  122.3 11.5 %collective-permute-start.21 = (bf16[160,1024]{1,0:T(8,128)(2,1)S(1)}, bf16[160,1024]{1,0:T(8,128)(2,1)S(1)}, u32[]{:S(2)}, u32[]{:S(2)}) collective-permute-start(bf16[160,1024]{1,0:T(8,128)(2,1)S(1)} %add_convert_fusion.1), channel_id=1, source_target_pairs={{0,16},{16,0},{1,17},{17,1},{2,18},{18,2},{3,19},{19,3},{4,20},{20... | collective-permute-start | bytes 983048 | tf_op jit(solution)/shard_map/ppermute | solution.py:143
  (3 other events, 4.6 us)

commit v3 on v2

--- a/solution.py
+++ b/solution.py
@@ -7,11 +7,14 @@
 from jax.experimental.pallas import tpu as pltpu
 from jax.sharding import PartitionSpec as P
 
-VMEM_LIMIT = 56 * 1024 * 1024
+VMEM_LIMIT = 34 * 1024 * 1024
+VMEM_LIMIT_GRAD = 18 * 1024 * 1024
+ORDER = (0, 1, 3, 2)
 
 
 def grad_kernel(n_piece, turn_ref, *refs):
-    pieces, (mean_ref, pert_ref, sign_ref, out_ref, both, sems) = refs[:n_piece], refs[n_piece:]
+    pieces, (mean_ref, pert_ref, head_ref, tail_ref) = refs[:n_piece], refs[n_piece:n_piece + 4]
+    outs, (both, sems) = refs[n_piece + 4:-2], refs[-2:]
 
     @pl.when(pl.program_id(0) == 0)
     def _():
@@ -31,56 +34,58 @@
     part_b = jnp.dot(signed, pert_ref[...], preferred_element_type=jnp.float32)
     for k in range(n_piece):
         at = slice(k * rows, (k + 1) * rows)
-        sign = sign_ref[k].astype(jnp.float32)
-        out_ref[k] = (part_a[at] + part_b[at] * sign).astype(out_ref.dtype)
-
-
-def partial_input_grad(turn, pieces, mean_weight, perturbed, sign, weight):
+        block = ORDER.index(k)
+        sign = (head_ref[block] if block < n_piece - 1 else tail_ref[...]).astype(jnp.float32)
+        outs[k][...] = (part_a[at] + part_b[at] * sign).astype(outs[k].dtype)
+
+
+def partial_input_grad(turn, pieces, mean_weight, perturbed, signs, weight):
     hidden, feats = mean_weight.shape
-    n_piece = len(pieces)
-    rows = sign.shape[1]
+    n_piece, rows = len(pieces), pieces[0].shape[1]
     tile = min(256, feats)
     any_spec = pl.BlockSpec(memory_space=pl.ANY)
     weight_spec = pl.BlockSpec((hidden, tile), lambda f, turn: (0, f))
+    block_spec = pl.BlockSpec((rows, tile), lambda f, turn: (0, f))
     return pl.pallas_call(
         functools.partial(grad_kernel, n_piece),
         grid_spec=pltpu.PrefetchScalarGridSpec(
             num_scalar_prefetch=1,
             grid=(feats // tile,),
             in_specs=[any_spec] * n_piece
-            + [weight_spec, weight_spec, pl.BlockSpec((n_piece, rows, tile), lambda f, turn: (0, 0, f))],
-            out_specs=pl.BlockSpec((n_piece, rows, tile), lambda f, turn: (0, 0, f)),
+            + [weight_spec, weight_spec, pl.BlockSpec((n_piece - 1, rows, tile), lambda f, turn: (0, 0, f)), block_spec],
+            out_specs=[block_spec] * n_piece,
             scratch_shapes=[
                 pltpu.VMEM((n_piece,) + pieces[0].shape, jnp.bfloat16),
                 pltpu.SemaphoreType.DMA((n_piece,)),
             ],
         ),
-        out_shape=jax.ShapeDtypeStruct((n_piece, rows, feats), jnp.bfloat16),
-        compiler_params=pltpu.CompilerParams(vmem_limit_bytes=VMEM_LIMIT),
+        out_shape=[jax.ShapeDtypeStruct((rows, feats), jnp.bfloat16)] * n_piece,
+        compiler_params=pltpu.CompilerParams(vmem_limit_bytes=VMEM_LIMIT_GRAD),
         cost_estimate=pl.CostEstimate(
             flops=int(weight * n_piece * rows * hidden * feats),
             bytes_accessed=4 * (n_piece * rows * (hidden + feats) + hidden * feats),
             transcendentals=0,
         ),
         name="input_grad",
-    )(turn, *pieces, mean_weight, perturbed, sign)
-
-
-def weight_kernel(n_slab, n_piece, n_input, scale, turn_ref, *refs):
+    )(turn, *pieces, mean_weight, perturbed, *signs)
+
+
+def weight_kernel(n_slab, n_piece, scale, turn_ref, *refs):
     n_grads = n_slab * n_piece
-    grads, inputs, refs = refs[:n_grads], refs[n_grads:n_grads + n_input], refs[n_grads + n_input:]
-    signs, noise_ref, (mean_ref, sigma_ref, plain, signed) = refs[:n_slab], refs[n_slab], refs[-4:]
+    grads, inputs, signs = refs[:n_grads], refs[n_grads:n_grads + 2 * n_slab], refs[n_grads + 2 * n_slab:n_grads + 4 * n_slab]
+    noise_ref, (mean_ref, sigma_ref, plain, signed) = refs[n_grads + 4 * n_slab], refs[-4:]
     rows = grads[0].shape[1]
 
     @pl.when(pl.program_id(1) == 0)
     def _():
-        blocks = [ref.at[at] for ref in inputs for at in range(ref.shape[0])]
-        for i, block in enumerate(blocks):
-            j, k = i // n_piece, i % n_piece
-            to = pl.ds(pl.multiple_of((j * n_piece + (k ^ turn_ref[0])) * rows, rows), rows)
-            value = block[...]
-            plain[to, :] = value
-            signed[to, :] = value * signs[j][k]
+        for j in range(n_slab):
+            for i, k in enumerate(ORDER):
+                to = pl.ds(pl.multiple_of((j * n_piece + (k ^ turn_ref[0])) * rows, rows), rows)
+                value, sign = (
+                    group[2 * j][i] if i < n_piece - 1 else group[2 * j + 1][...] for group in (inputs, signs)
+                )
+                plain[to, :] = value
+                signed[to, :] = value * sign
 
     dims = (((0,), (0,)), ((), ()))
     grad = jnp.concatenate([g[0] for g in grads], axis=0)
@@ -104,14 +109,18 @@
         return partial
     grad_spec = pl.BlockSpec((2, rows, tile), lambda f, h, turn: (0, 0, h + first))
     out_spec = pl.BlockSpec((tile, width), lambda f, h, turn: (h + first, f))
+    inputs, signs = ([x for slab in group for x in slab] for group in (inputs, signs))
     operands = [p for slab_pieces in pieces for p in slab_pieces] + inputs + signs + [noise]
     return pl.pallas_call(
-        functools.partial(weight_kernel, n_slab, n_piece, len(inputs), scale),
+        functools.partial(weight_kernel, n_slab, n_piece, scale),
         grid_spec=pltpu.PrefetchScalarGridSpec(
             num_scalar_prefetch=1,
             grid=(feats // width, steps),
             in_specs=[grad_spec] * (n_slab * n_piece)
-            + [pl.BlockSpec(x.shape[:2] + (width,), lambda f, h, turn: (0, 0, f)) for x in inputs + signs]
+            + [
+                pl.BlockSpec(x.shape[:-1] + (width,), lambda f, h, turn, lead=x.ndim - 1: (0,) * lead + (f,))
+                for x in inputs + signs
+            ]
             + [out_spec]
             + [pl.BlockSpec(memory_space=pl.ANY)] * len(partial),
             out_specs=[out_spec, out_spec],
@@ -124,8 +133,8 @@
         input_output_aliases={1 + len(operands) + i: i for i in range(len(partial))},
         compiler_params=pltpu.CompilerParams(vmem_limit_bytes=VMEM_LIMIT),
         cost_estimate=pl.CostEstimate(
-            flops=4 * tokens * tile * steps * feats,
-            bytes_accessed=4 * (tokens * tile * steps + tokens * feats) + 10 * tile * steps * feats,
+            flops=4 * tokens * tile * steps * feats if part else 1,
+            bytes_accessed=4 * (tokens * tile * steps + tokens * feats) + 10 * tile * steps * feats if part else 1,
             transcendentals=0,
         ),
         name="weight_grads",
@@ -156,28 +165,28 @@
         return lax.optimization_barrier(values)
 
     signed_grads = out_grads * (1 - 2 * out_bits).astype(jnp.bfloat16)
-    signed_grads, in_bits = tie(signed_grads, in_bits)
+    mine, others = half(0), [half(j) for j in range(1, n_depth)]
+    others, in_bits = tie(others, in_bits)
     in_sign = (1 - 2 * in_bits).astype(jnp.bfloat16)
     perturbed = (sigma_weight.astype(jnp.float32) * noise.astype(jnp.float32)).astype(jnp.bfloat16)
 
-    mine = half(0)
-    others = [hop(half(j), j) for j in range(1, n_depth)]
+    others = [hop(other, j + 1) for j, other in enumerate(others)]
     signs = [in_sign, cross(in_sign, 1), None, cross(in_sign, 3)]
     signs[1], signs[3] = tie(signs[1], signs[3])
     signs[2] = cross(signs[3], 1)
-    across, perturbed, signs[2] = tie(swap(mine, 2), perturbed, signs[2])
+    across, others, perturbed, signs, inputs = tie(swap(mine, 2), others, perturbed, signs, inputs)
+    head, tail = jnp.stack([signs[0], signs[1], signs[3]]), signs[2]
     pieces = [[mine, swap(mine, 1), across, swap(across, 1)]]
-    pieces[0], others, signs, inputs = tie(pieces[0], others, jnp.stack(signs), inputs)
-
-    own = partial_input_grad(turn, pieces[0], mean_weight, perturbed, signs, 64)
+
+    slab_sign = [[head, tail]] + [[hop(head, j), hop(tail, j)] for j in range(1, n_depth)]
+    own = partial_input_grad(turn, pieces[0], mean_weight, perturbed, slab_sign[0], 64)
     blocks = [inputs, cross(inputs, 1), None, cross(inputs, 3)]
     blocks[1], blocks[3], own = tie(blocks[1], blocks[3], own)
     blocks[2] = cross(blocks[3], 1)
     passed = cross(own[2], 1)
     across = [swap(other, 2) for other in others]
-    slab_sign = [signs] + [hop(signs, j) for j in range(1, n_depth)]
     across, slab_sign, blocks[2], passed = tie(across, slab_sign, blocks[2], passed)
-    blocks = jnp.stack(blocks)
+    blocks = [jnp.stack([blocks[0], blocks[1], blocks[3]]), blocks[2]]
 
     def scatter(part, passed):
         joined = (part[3].astype(jnp.float32) + passed.astype(jnp.float32)).astype(jnp.bfloat16)
@@ -187,13 +196,14 @@
     slab_inputs = [blocks]
     total, grads = None, []
     for j in range(1, n_depth):
-        hopped = hop(blocks, j)
+        hopped = [hop(x, j) for x in blocks]
         pieces.append([others[j - 1], swap(others[j - 1], 1), across[j - 1], swap(across[j - 1], 1)])
-        part = partial_input_grad(turn, pieces[j], mean_weight, perturbed, slab_sign[j], 64)
-        part, owned = tie(part, owned)
+        part = partial_input_grad(turn, pieces[j], mean_weight, perturbed, slab_sign[j], 4)
+        passed = cross(part[2], 1)
         if j == 1:
+            passed, owned = tie(passed, owned)
             total = sum(x.astype(jnp.float32) for x in owned)
-        parts = scatter(part, cross(part[2], 1))
+        parts = scatter(part, passed)
         parts[0], hopped = tie(parts[0], hopped)
         slab_inputs.append(hopped)
         if j == n_depth - 1:

time: 137 us -> 122 us (0.89)
  Pallas kernels: 42.8 us -> 32.8 us
  other arithmetic: 13 us -> 9.15 us
    pallas_call x2, Pallas kernels: 21.5 us -> 16 us  [weight_grads(): pl.pallas_call(functools.partial(weight_kernel, n_slab, n_piece, scale),...]
    pallas_call x2, Pallas kernels: 21.2 us -> 16.8 us  [partial_input_grad(): pl.pallas_call(functools.partial(grad_kernel, n_piece), grid_spec=pltpu.P...]
    squeeze x2 -> x0, local copies, waits for them, and re-layouts: 3.2 us -> none  [the longest x1 1.96 us: scatter(): return [part[0], cross(part[1], 1), cross(joined, 3)]]
    convert_element_type x2, other arithmetic: 3.08 us -> 0.19 us  [scatter(): (part[3].astype(jnp.float32) + passed.astype(jnp.float32)).astype(jnp.bfl...]
    ppermute x4 -> x6, waiting for transfers between devices: 19.8 us -> 16.9 us  [hop(): lax.ppermute(value, 'depth', [(i, (i + step) % n_depth) for i in range(n_...]
    unnamed x26 -> x30, local copies, waits for them, and re-layouts: 2.13 us -> 4.85 us
    ppermute x12, waiting for transfers between devices: 28.8 us -> 31.1 us  [cross(): return lax.ppermute(value, 'col', [(i, i ^ bits) for i in range(n_col)])]
    ppermute x4 -> x6, starting transfers between devices: 6.11 us -> 6.69 us  [hop(): lax.ppermute(value, 'depth', [(i, (i + step) % n_depth) for i in range(n_...]
  transfers between devices with their start and end apart: 22 -> 24, of which waited for: 9 -> 10; matrix products, arithmetic and copies ran while one was open for 9% -> 4% of each run, Pallas kernels for 32% -> 27%
where the time goes in v3:
time: 122 us; the launch traced here: 121 us
  waiting for transfers between devices  48.1 us (39%)
  Pallas kernels  32.8 us (27%)
  starting transfers between devices  25.5 us (21%)
  other arithmetic  9.15 us (8%)
  local copies, waits for them, and re-layouts  5.01 us (4%)
    ppermute x12, waiting for transfers between devices, cross(): return lax.ppermute(value, 'col', [(i, i ^ bits) for i in range(n_col)])  31.1 us
    ppermute x6, waiting for transfers between devices, hop(): lax.ppermute(value, 'depth', [(i, (i + step) % n_depth) for i in range(n_...  16.9 us
    pallas_call x2, Pallas kernels, partial_input_grad(): pl.pallas_call(functools.partial(grad_kernel, n_piece), grid_spec=pltpu.P...  16.8 us
    pallas_call x2, Pallas kernels, weight_grads(): pl.pallas_call(functools.partial(weight_kernel, n_slab, n_piece, scale),...  16 us
    ppermute x12, starting transfers between devices, cross(): return lax.ppermute(value, 'col', [(i, i ^ bits) for i in range(n_col)])  15.4 us
    ppermute x6, starting transfers between devices, hop(): lax.ppermute(value, 'depth', [(i, (i + step) % n_depth) for i in range(n_...  6.69 us
    unnamed x30, local copies, waits for them, and re-layouts  4.85 us
    convert_element_type x1, other arithmetic, local(): (sigma_weight.astype(jnp.float32) * noise.astype(jnp.float32)).astype(jnp...  3.68 us
  transfers between devices with their start and end apart: 24, of which 10 were waited for; matrix products, arithmetic and copies ran while one was open for 4% of the time, Pallas kernels for 27%

profile of v3, /device:TPU:0, one launch (start us, length us, event | category | flops | bytes accessed | tf_op | source)
XLA Modules:
  0.0 121.5 jit_solution(3136450007926130143)
XLA Ops:
  0.7 2.5 %fusion = bf16[160,3584]{1,0:T(8,128)(2,1)S(1)} fusion(bf16[160,3584]{1,0:T(8,128)(2,1)} %param.9, s32[160,3584]{1,0:T(8,128)} %param.10), kind=kLoop, calls=%fused_computation.2 | loop fusion | flops 2293760 | bytes 4587520 | tf_op jit(solution)/shard_map/mul | solution.py:167
  3.5 3.0 %collective-permute-start = (bf16[2,160,1792]{2,1,0:T(8,128)(2,1)S(1)}, bf16[2,160,1792]{2,1,0:T(8,128)(2,1)S(1)}, u32[]{:S(2)}, u32[]{:S(2)}) collective-permute-start(bf16[2,160,1792]{2,1,0:T(8,128)(2,1)S(1)} %pad_maximum_fusion.refs_0_), channel_id=1, source_target_pairs={{0,8},{4,12},{8,0},{12,4},{1,9},{5,13},{9,1},{13,5},{2,10},{6,14},... | collective-permute-start | bytes 3440648 | tf_op jit(solution)/shard_map/ppermute | solution.py:155
  6.6 1.6 %collective-permute-start.1 = (bf16[2,160,1792]{2,1,0:T(8,128)(2,1)S(1)}, bf16[2,160,1792]{2,1,0:T(8,128)(2,1)S(1)}, u32[]{:S(2)}, u32[]{:S(2)}) collective-permute-start(bf16[2,160,1792]{2,1,0:T(8,128)(2,1)S(1)} %pad_maximum_fusion.1), channel_id=1, source_target_pairs={{0,16},{16,0},{1,17},{17,1},{2,18},{18,2},{3,19},{19,3},{4,20},{20... | collective-permute-start | bytes 3440648 | tf_op jit(solution)/shard_map/ppermute | solution.py:152
  8.3 1.6 %collective-permute-start.2 = (bf16[160,1024]{1,0:T(8,128)(2,1)S(1)}, bf16[160,1024]{1,0:T(8,128)(2,1)S(1)}, u32[]{:S(2)}, u32[]{:S(2)}) collective-permute-start(bf16[160,1024]{1,0:T(8,128)(2,1)S(1)} %subtract_convert_fusion.1), channel_id=1, source_target_pairs={{0,1},{1,0},{2,3},{3,2},{4,5},{5,4},{6,7},{7,6},{8,9},{9,8},{10,11... | collective-permute-start | bytes 983048 | tf_op jit(solution)/shard_map/ppermute | solution.py:158
  9.9 2.5 %collective-permute-start.3 = (bf16[160,1024]{1,0:T(8,128)(2,1)S(1)}, bf16[160,1024]{1,0:T(8,128)(2,1)S(1)}, u32[]{:S(2)}, u32[]{:S(2)}) collective-permute-start(bf16[160,1024]{1,0:T(8,128)(2,1)S(1)} %subtract_convert_fusion.1), channel_id=1, source_target_pairs={{0,3},{1,2},{2,1},{3,0},{4,7},{5,6},{6,5},{7,4},{8,11},{9,10},{10,... | collective-permute-start | bytes 983048 | tf_op jit(solution)/shard_map/ppermute | solution.py:158
  12.4 5.7 %collective-permute-done.2 = bf16[160,1024]{1,0:T(8,128)(2,1)S(1)} collective-permute-done((bf16[160,1024]{1,0:T(8,128)(2,1)S(1)}, bf16[160,1024]{1,0:T(8,128)(2,1)S(1)}, u32[]{:S(2)}, u32[]{:S(2)}) %collective-permute-start.2) | collective-permute-done | bytes 327712 | tf_op jit(solution)/shard_map/ppermute | solution.py:158
  18.1 8.5 %collective-permute-done.3 = bf16[160,1024]{1,0:T(8,128)(2,1)S(1)} collective-permute-done((bf16[160,1024]{1,0:T(8,128)(2,1)S(1)}, bf16[160,1024]{1,0:T(8,128)(2,1)S(1)}, u32[]{:S(2)}, u32[]{:S(2)}) %collective-permute-start.3) | collective-permute-done | bytes 327712 | tf_op jit(solution)/shard_map/ppermute | solution.py:158
  27.2 3.7 %multiply_convert_fusion.refs_5_ = bf16[1792,1024]{1,0:T(8,128)(2,1)} fusion(bf16[1792,1024]{1,0:T(8,128)(2,1)S(1)} %copy-done, bf16[1792,1024]{1,0:T(8,128)(2,1)S(1)} %copy-done.9), kind=kLoop, calls=%fused_computation | loop fusion | flops 7340032 | bytes 11010048 | tf_op jit(solution)/shard_map/convert_element_type | solution.py:171
  30.9 3.9 %collective-permute-done.4.refs_7_.refs_13_ = bf16[160,1024]{1,0:T(8,128)(2,1)S(1)} collective-permute-done((bf16[160,1024]{1,0:T(8,128)(2,1)S(1)}, bf16[160,1024]{1,0:T(8,128)(2,1)S(1)}, u32[]{:S(2)}, u32[]{:S(2)}) %collective-permute-start.4) | collective-permute-done | bytes 327712 | tf_op jit(solution)/shard_map/ppermute | solution.py:158
  34.8 0.7 copy-done.4
  35.8 1.9 %collective-permute-start.10 = (bf16[160,1024]{1,0:T(8,128)(2,1)}, bf16[160,1024]{1,0:T(8,128)(2,1)S(1)}, u32[]{:S(2)}, u32[]{:S(2)}) collective-permute-start(bf16[160,1024]{1,0:T(8,128)(2,1)} %param.7), channel_id=1, source_target_pairs={{0,3},{1,2},{2,1},{3,0},{4,7},{5,6},{6,5},{7,4},{8,11},{9,10},{10,... | collective-permute-start | bytes 983048 | tf_op jit(solution)/shard_map/ppermute | solution.py:158
  38.1 1.3 %pad_maximum_fusion.2.refs_6_.refs_12_ = bf16[3,160,1024]{2,1,0:T(8,128)(2,1)S(1)} fusion(bf16[1,160,1024]{2,1,0:T(8,128)(2,1)} %bitcast.20, bf16[1,160,1024]{2,1,0:T(8,128)(2,1)} %bitcast.19, bf16[1,160,1024]{2,1,0:T(8,128)(2,1)} %bitcast.15), kind=kLoop, calls=%fused_computation.5 | loop fusion | flops 983040 | bytes 1966080 | tf_op jit(solution)/shard_map/stack | solution.py:178
  39.4 1.6 %collective-permute-start.7 = (bf16[3,160,1024]{2,1,0:T(8,128)(2,1)S(1)}, bf16[3,160,1024]{2,1,0:T(8,128)(2,1)S(1)}, u32[]{:S(2)}, u32[]{:S(2)}) collective-permute-start(bf16[3,160,1024]{2,1,0:T(8,128)(2,1)S(1)} %pad_maximum_fusion.2.refs_6_.refs_12_), channel_id=1, source_target_pairs={{0,16},{16,0},{1,17},{17,1},{2,18},{18,2},{3,19},{19,3},{4,20},{20... | collective-permute-start | bytes 2949128 | tf_op jit(solution)/shard_map/ppermute | solution.py:152
  41.5 2.0 %copy-done.2 = bf16[1792,1024]{1,0:T(8,128)(2,1)S(1)} copy-done((bf16[1792,1024]{1,0:T(8,128)(2,1)S(1)}, bf16[1792,1024]{1,0:T(8,128)(2,1)}, u32[]{:S(2)}) %copy-start.2) | copy-done | bytes 3670040
  43.5 2.0 %copy-done.6 = bf16[1792,1024]{1,0:T(8,128)(2,1)S(1)} copy-done((bf16[1792,1024]{1,0:T(8,128)(2,1)S(1)}, bf16[1792,1024]{1,0:T(8,128)(2,1)}, u32[]{:S(2)}) %copy-start.6) | copy-done | bytes 3670040
  45.5 9.1 %input_grad.2 = (bf16[160,1024]{1,0:T(8,128)(2,1)S(1)}, bf16[160,1024]{1,0:T(8,128)(2,1)S(1)}, bf16[160,1024]{1,0:T(8,128)(2,1)S(1)}, bf16[160,1024]{1,0:T(8,128)(2,1)S(1)}) custom-call(s32[1]{0:T(128)} %bitcast.turn_ref, bf16[2,160,1792]{2,1,0:T(8,128)(2,1)S(1)} %pad_maximum_fusion.refs_0_, bf16[2,160,1792]{2,1,0:T(8,128)(2,1)} %collective-permute-done.11.refs_1_, ...), custom_call_target="tpu_custom_call" | custom-call | flops 75161927680 | bytes 14548992 | tf_op jit(solution)/shard_map/input_grad/pallas_call | solution.py:49
  54.7 0.7 collective-permute-start.13
  55.4 1.3 %collective-permute-start.14 = (bf16[160,1024]{1,0:T(8,128)(2,1)S(1)}, bf16[160,1024]{1,0:T(8,128)(2,1)S(1)}, u32[]{:S(2)}, u32[]{:S(2)}) collective-permute-start(bf16[160,1024]{1,0:T(8,128)(2,1)S(1)} %get-tuple-element.69), channel_id=1, source_target_pairs={{0,1},{1,0},{2,3},{3,2},{4,5},{5,4},{6,7},{7,6},{8,9},{9,8},{10,11... | collective-permute-start | bytes 983048 | tf_op jit(solution)/shard_map/ppermute | solution.py:158
  56.7 13.0 %collective-permute-done.8.refs_7_.refs_15_ = bf16[160,1024]{1,0:T(8,128)(2,1)S(1)} collective-permute-done((bf16[160,1024]{1,0:T(8,128)(2,1)S(1)}, bf16[160,1024]{1,0:T(8,128)(2,1)S(1)}, u32[]{:S(2)}, u32[]{:S(2)}) %collective-permute-start.8) | collective-permute-done | bytes 327712 | tf_op jit(solution)/shard_map/ppermute | solution.py:152
  70.5 1.6 %collective-permute-start.19 = (bf16[3,160,1024]{2,1,0:T(8,128)(2,1)S(1)}, bf16[3,160,1024]{2,1,0:T(8,128)(2,1)S(1)}, u32[]{:S(2)}, u32[]{:S(2)}) collective-permute-start(bf16[3,160,1024]{2,1,0:T(8,128)(2,1)S(1)} %pad_maximum_fusion.3.refs_8_), channel_id=1, source_target_pairs={{0,16},{16,0},{1,17},{17,1},{2,18},{18,2},{3,19},{19,3},{4,20},{20... | collective-permute-start | bytes 2949128 | tf_op jit(solution)/shard_map/ppermute | solution.py:152
  72.9 2.5 %collective-permute-start.18 = (bf16[160,1024]{1,0:T(8,128)(2,1)S(1)}, bf16[160,1024]{1,0:T(8,128)(2,1)S(1)}, u32[]{:S(2)}, u32[]{:S(2)}) collective-permute-start(bf16[160,1024]{1,0:T(8,128)(2,1)S(1)} %add_convert_fusion.3), channel_id=1, source_target_pairs={{0,3},{1,2},{2,1},{3,0},{4,7},{5,6},{6,5},{7,4},{8,11},{9,10},{10,... | collective-permute-start | bytes 983048 | tf_op jit(solution)/shard_map/ppermute | solution.py:158
  75.4 7.7 %input_grad.3 = (bf16[160,1024]{1,0:T(8,128)(2,1)S(1)}, bf16[160,1024]{1,0:T(8,128)(2,1)S(1)}, bf16[160,1024]{1,0:T(8,128)(2,1)S(1)}, bf16[160,1024]{1,0:T(8,128)(2,1)S(1)}) custom-call(s32[1]{0:T(128)} %bitcast.turn_ref, bf16[2,160,1792]{2,1,0:T(8,128)(2,1)S(1)} %collective-permute-done.1.refs_0_.refs_4_, ...), custom_call_target="tpu_custom_call" | custom-call | flops 4697620480 | bytes 14548992 | tf_op jit(solution)/shard_map/input_grad/pallas_call | solution.py:49
  84.1 1.5 %collective-permute-start.21 = (bf16[160,1024]{1,0:T(8,128)(2,1)S(1)}, bf16[160,1024]{1,0:T(8,128)(2,1)S(1)}, u32[]{:S(2)}, u32[]{:S(2)}) collective-permute-start(bf16[160,1024]{1,0:T(8,128)(2,1)S(1)} %get-tuple-element.85), channel_id=1, source_target_pairs={{0,1},{1,0},{2,3},{3,2},{4,5},{5,4},{6,7},{7,6},{8,9},{9,8},{10,11... | collective-permute-start | bytes 983048 | tf_op jit(solution)/shard_map/ppermute | solution.py:158
  85.6 5.2 %collective-permute-done.18 = bf16[160,1024]{1,0:T(8,128)(2,1)S(1)} collective-permute-done((bf16[160,1024]{1,0:T(8,128)(2,1)S(1)}, bf16[160,1024]{1,0:T(8,128)(2,1)S(1)}, u32[]{:S(2)}, u32[]{:S(2)}) %collective-permute-start.18) | collective-permute-done | bytes 327712 | tf_op jit(solution)/shard_map/ppermute | solution.py:158
  90.8 6.4 %collective-permute-done.16 = bf16[160,1024]{1,0:T(8,128)(2,1)S(1)} collective-permute-done((bf16[160,1024]{1,0:T(8,128)(2,1)S(1)}, bf16[160,1024]{1,0:T(8,128)(2,1)S(1)}, u32[]{:S(2)}, u32[]{:S(2)}) %collective-permute-start.16) | collective-permute-done | bytes 327712 | tf_op jit(solution)/shard_map/ppermute | solution.py:158
  97.4 1.4 %collective-permute-start.22 = (bf16[160,1024]{1,0:T(8,128)(2,1)S(1)}, bf16[160,1024]{1,0:T(8,128)(2,1)S(1)}, u32[]{:S(2)}, u32[]{:S(2)}) collective-permute-start(bf16[160,1024]{1,0:T(8,128)(2,1)S(1)} %add_convert_fusion.2), channel_id=1, source_target_pairs={{0,3},{1,2},{2,1},{3,0},{4,7},{5,6},{6,5},{7,4},{8,11},{9,10},{10,... | collective-permute-start | bytes 983048 | tf_op jit(solution)/shard_map/ppermute | solution.py:158
  98.8 3.0 %collective-permute-done.20.refs_11_ = bf16[160,1024]{1,0:T(8,128)(2,1)S(1)} collective-permute-done((bf16[160,1024]{1,0:T(8,128)(2,1)S(1)}, bf16[160,1024]{1,0:T(8,128)(2,1)S(1)}, u32[]{:S(2)}, u32[]{:S(2)}) %collective-permute-start.20) | collective-permute-done | bytes 327712 | tf_op jit(solution)/shard_map/ppermute | solution.py:152
  101.8 8.9 %weight_grads.2 = (f32[1792,1024]{1,0:T(8,128)}, f32[1792,1024]{1,0:T(8,128)}) custom-call(s32[1]{0:T(128)} %bitcast.turn_ref, bf16[2,160,1792]{2,1,0:T(8,128)(2,1)S(1)} %pad_maximum_fusion.refs_0_, bf16[2,160,1792]{2,1,0:T(8,128)(2,1)} %collective-permute-done.11.refs_1_, bf16[2,160,1792]{2,1,0:T(8,128)(2,1)S(1)} %collective-permute-done.refs_2_, ...), custom_call_target="tpu_custom_call" | custom-call | flops 1 | bytes 1 | tf_op jit(solution)/shard_map/weight_grads/pallas_call | solution.py:114
  111.5 0.9 collective-permute-start.23
  112.3 7.2 %weight_grads.3 = (f32[1792,1024]{1,0:T(8,128)}, f32[1792,1024]{1,0:T(8,128)}) custom-call(s32[1]{0:T(128)} %bitcast.turn_ref, bf16[2,160,1792]{2,1,0:T(8,128)(2,1)S(1)} %pad_maximum_fusion.refs_0_, bf16[2,160,1792]{2,1,0:T(8,128)(2,1)} %collective-permute-done.11.refs_1_, ...), custom_call_target="tpu_custom_call", output_to_operand_aliasing={{0}: (18, {}), {1}: (19, {})} | custom-call | flops 4026531840 | bytes 17039360 | tf_op jit(solution)/shard_map/weight_grads/pallas_call | solution.py:114
  119.5 1.0 collective-permute-done.23
  120.5 0.9 add_convert_fusion
  (62 shorter events, 5.8 us)
Async XLA Ops:
  3.2 24.0 %copy-start.9 = (bf16[1792,1024]{1,0:T(8,128)(2,1)S(1)}, bf16[1792,1024]{1,0:T(8,128)(2,1)}, u32[]{:S(2)}) copy-start(bf16[1792,1024]{1,0:T(8,128)(2,1)} %param.12) | copy-start | bytes 11010052
  3.4 23.9 %copy-start = (bf16[1792,1024]{1,0:T(8,128)(2,1)S(1)}, bf16[1792,1024]{1,0:T(8,128)(2,1)}, u32[]{:S(2)}) copy-start(bf16[1792,1024]{1,0:T(8,128)(2,1)} %refs_16_.3) | copy-start | bytes 11010052
  3.5 31.3 %collective-permute-start = (bf16[2,160,1792]{2,1,0:T(8,128)(2,1)S(1)}, bf16[2,160,1792]{2,1,0:T(8,128)(2,1)S(1)}, u32[]{:S(2)}, u32[]{:S(2)}) collective-permute-start(bf16[2,160,1792]{2,1,0:T(8,128)(2,1)S(1)} %pad_maximum_fusion.refs_0_), channel_id=1, source_target_pairs={{0,8},{4,12},{8,0},{12,4},{1,9},{5,13},{9,1},{13,5},{2,10},{6,14},... | collective-permute-start | bytes 3440648 | tf_op jit(solution)/shard_map/ppermute | solution.py:155
  6.6 28.2 %collective-permute-start.1 = (bf16[2,160,1792]{2,1,0:T(8,128)(2,1)S(1)}, bf16[2,160,1792]{2,1,0:T(8,128)(2,1)S(1)}, u32[]{:S(2)}, u32[]{:S(2)}) collective-permute-start(bf16[2,160,1792]{2,1,0:T(8,128)(2,1)S(1)} %pad_maximum_fusion.1), channel_id=1, source_target_pairs={{0,16},{16,0},{1,17},{17,1},{2,18},{18,2},{3,19},{19,3},{4,20},{20... | collective-permute-start | bytes 3440648 | tf_op jit(solution)/shard_map/ppermute | solution.py:152
  8.3 9.8 %copy-start.10 = (bf16[160,1024]{1,0:T(8,128)(2,1)}, bf16[160,1024]{1,0:T(8,128)(2,1)S(1)}, u32[]{:S(2)}) copy-start(bf16[160,1024]{1,0:T(8,128)(2,1)S(1)} %subtract_convert_fusion.1) | copy-start | bytes 983044
  8.3 9.8 %collective-permute-start.2 = (bf16[160,1024]{1,0:T(8,128)(2,1)S(1)}, bf16[160,1024]{1,0:T(8,128)(2,1)S(1)}, u32[]{:S(2)}, u32[]{:S(2)}) collective-permute-start(bf16[160,1024]{1,0:T(8,128)(2,1)S(1)} %subtract_convert_fusion.1), channel_id=1, source_target_pairs={{0,1},{1,0},{2,3},{3,2},{4,5},{5,4},{6,7},{7,6},{8,9},{9,8},{10,11... | collective-permute-start | bytes 983048 | tf_op jit(solution)/shard_map/ppermute | solution.py:158
  9.9 16.7 %collective-permute-start.3 = (bf16[160,1024]{1,0:T(8,128)(2,1)S(1)}, bf16[160,1024]{1,0:T(8,128)(2,1)S(1)}, u32[]{:S(2)}, u32[]{:S(2)}) collective-permute-start(bf16[160,1024]{1,0:T(8,128)(2,1)S(1)} %subtract_convert_fusion.1), channel_id=1, source_target_pairs={{0,3},{1,2},{2,1},{3,0},{4,7},{5,6},{6,5},{7,4},{8,11},{9,10},{10,... | collective-permute-start | bytes 983048 | tf_op jit(solution)/shard_map/ppermute | solution.py:158
  12.4 26.9 %collective-permute-start.11 = (bf16[2,160,1792]{2,1,0:T(8,128)(2,1)S(1)}, bf16[2,160,1792]{2,1,0:T(8,128)(2,1)}, u32[]{:S(2)}, u32[]{:S(2)}) collective-permute-start(bf16[2,160,1792]{2,1,0:T(8,128)(2,1)S(1)} %pad_maximum_fusion.refs_0_), channel_id=1, source_target_pairs={{0,4},{4,0},{8,12},{12,8},{1,5},{5,1},{9,13},{13,9},{2,6},{6,2},{1... | collective-permute-start | bytes 3440648 | tf_op jit(solution)/shard_map/ppermute | solution.py:155
  18.1 8.5 %copy-start.13 = (bf16[160,1024]{1,0:T(8,128)(2,1)}, bf16[160,1024]{1,0:T(8,128)(2,1)S(1)}, u32[]{:S(2)}) copy-start(bf16[160,1024]{1,0:T(8,128)(2,1)S(1)} %collective-permute-done.2) | copy-start | bytes 983044
  26.6 8.2 %collective-permute-start.4 = (bf16[160,1024]{1,0:T(8,128)(2,1)S(1)}, bf16[160,1024]{1,0:T(8,128)(2,1)S(1)}, u32[]{:S(2)}, u32[]{:S(2)}) collective-permute-start(bf16[160,1024]{1,0:T(8,128)(2,1)S(1)} %collective-permute-done.3), channel_id=1, source_target_pairs={{0,1},{1,0},{2,3},{3,2},{4,5},{5,4},{6,7},{7,6},{8,9},{9,8},{10,11... | collective-permute-start | bytes 983048 | tf_op jit(solution)/shard_map/ppermute | solution.py:158
  35.5 5.4 %collective-permute-start.12 = (bf16[2,160,1792]{2,1,0:T(8,128)(2,1)S(1)}, bf16[2,160,1792]{2,1,0:T(8,128)(2,1)}, u32[]{:S(2)}, u32[]{:S(2)}) collective-permute-start(bf16[2,160,1792]{2,1,0:T(8,128)(2,1)S(1)} %collective-permute-done.refs_2_), channel_id=1, source_target_pairs={{0,4},{4,0},{8,12},{12,8},{1,5},{5,1},{9,13},{13,9},{2,6},{6,2},{1... | collective-permute-start | bytes 3440648 | tf_op jit(solution)/shard_map/ppermute | solution.py:155
  35.5 19.1 %collective-permute-start.9 = (bf16[160,1024]{1,0:T(8,128)(2,1)}, bf16[160,1024]{1,0:T(8,128)(2,1)S(1)}, u32[]{:S(2)}, u32[]{:S(2)}) collective-permute-start(bf16[160,1024]{1,0:T(8,128)(2,1)} %param.7), channel_id=1, source_target_pairs={{0,1},{1,0},{2,3},{3,2},{4,5},{5,4},{6,7},{7,6},{8,9},{9,8},{10,11... | collective-permute-start | bytes 983048 | tf_op jit(solution)/shard_map/ppermute | solution.py:158
  35.8 18.8 %collective-permute-start.10 = (bf16[160,1024]{1,0:T(8,128)(2,1)}, bf16[160,1024]{1,0:T(8,128)(2,1)S(1)}, u32[]{:S(2)}, u32[]{:S(2)}) collective-permute-start(bf16[160,1024]{1,0:T(8,128)(2,1)} %param.7), channel_id=1, source_target_pairs={{0,3},{1,2},{2,1},{3,0},{4,7},{5,6},{6,5},{7,4},{8,11},{9,10},{10,... | collective-permute-start | bytes 983048 | tf_op jit(solution)/shard_map/ppermute | solution.py:158
  37.7 32.0 %collective-permute-start.6 = (bf16[2,160,1792]{2,1,0:T(8,128)(2,1)S(1)}, bf16[2,160,1792]{2,1,0:T(8,128)(2,1)S(1)}, u32[]{:S(2)}, u32[]{:S(2)}) collective-permute-start(bf16[2,160,1792]{2,1,0:T(8,128)(2,1)S(1)} %collective-permute-done.1.refs_0_.refs_4_), channel_id=1, source_target_pairs={{0,8},{4,12},{8,0},{12,4},{1,9},{5,13},{9,1},{13,5},{2,10},{6,14},... | collective-permute-start | bytes 3440648 | tf_op jit(solution)/shard_map/ppermute | solution.py:155
  39.4 30.4 %collective-permute-start.7 = (bf16[3,160,1024]{2,1,0:T(8,128)(2,1)S(1)}, bf16[3,160,1024]{2,1,0:T(8,128)(2,1)S(1)}, u32[]{:S(2)}, u32[]{:S(2)}) collective-permute-start(bf16[3,160,1024]{2,1,0:T(8,128)(2,1)S(1)} %pad_maximum_fusion.2.refs_6_.refs_12_), channel_id=1, source_target_pairs={{0,16},{16,0},{1,17},{17,1},{2,18},{18,2},{3,19},{19,3},{4,20},{20... | collective-permute-start | bytes 2949128 | tf_op jit(solution)/shard_map/ppermute | solution.py:152
  40.9 28.8 %collective-permute-start.8 = (bf16[160,1024]{1,0:T(8,128)(2,1)S(1)}, bf16[160,1024]{1,0:T(8,128)(2,1)S(1)}, u32[]{:S(2)}, u32[]{:S(2)}) collective-permute-start(bf16[160,1024]{1,0:T(8,128)(2,1)S(1)} %copy-done.5), channel_id=1, source_target_pairs={{0,16},{16,0},{1,17},{17,1},{2,18},{18,2},{3,19},{19,3},{4,20},{20... | collective-permute-start | bytes 983048 | tf_op jit(solution)/shard_map/ppermute | solution.py:152
  45.5 24.9 %copy-start.12 = (bf16[160,1024]{1,0:T(8,128)(2,1)S(1)}, bf16[160,1024]{1,0:T(8,128)(2,1)}, u32[]{:S(2)}) copy-start(bf16[160,1024]{1,0:T(8,128)(2,1)} %param.7) | copy-start | bytes 983044
  45.5 29.9 %copy-start.3 = (bf16[1792,1024]{1,0:T(8,128)(2,1)S(1)}, bf16[1792,1024]{1,0:T(8,128)(2,1)}, u32[]{:S(2)}) copy-start(bf16[1792,1024]{1,0:T(8,128)(2,1)} %multiply_convert_fusion.refs_5_) | copy-start | bytes 11010052
  45.5 29.9 %copy-start.7 = (bf16[1792,1024]{1,0:T(8,128)(2,1)S(1)}, bf16[1792,1024]{1,0:T(8,128)(2,1)}, u32[]{:S(2)}) copy-start(bf16[1792,1024]{1,0:T(8,128)(2,1)} %refs_4_.3) | copy-start | bytes 11010052
  54.7 15.1 %collective-permute-start.13 = (bf16[160,1024]{1,0:T(8,128)(2,1)S(1)}, bf16[160,1024]{1,0:T(8,128)(2,1)S(1)}, u32[]{:S(2)}, u32[]{:S(2)}) collective-permute-start(bf16[160,1024]{1,0:T(8,128)(2,1)S(1)} %collective-permute-done.10), channel_id=1, source_target_pairs={{0,1},{1,0},{2,3},{3,2},{4,5},{5,4},{6,7},{7,6},{8,9},{9,8},{10,11... | collective-permute-start | bytes 983048 | tf_op jit(solution)/shard_map/ppermute | solution.py:158
  55.4 15.0 %collective-permute-start.14 = (bf16[160,1024]{1,0:T(8,128)(2,1)S(1)}, bf16[160,1024]{1,0:T(8,128)(2,1)S(1)}, u32[]{:S(2)}, u32[]{:S(2)}) collective-permute-start(bf16[160,1024]{1,0:T(8,128)(2,1)S(1)} %get-tuple-element.69), channel_id=1, source_target_pairs={{0,1},{1,0},{2,3},{3,2},{4,5},{5,4},{6,7},{7,6},{8,9},{9,8},{10,11... | collective-permute-start | bytes 983048 | tf_op jit(solution)/shard_map/ppermute | solution.py:158
  69.7 5.7 %collective-permute-start.5 = (bf16[2,160,1792]{2,1,0:T(8,128)(2,1)S(1)}, bf16[2,160,1792]{2,1,0:T(8,128)(2,1)S(1)}, u32[]{:S(2)}, u32[]{:S(2)}) collective-permute-start(bf16[2,160,1792]{2,1,0:T(8,128)(2,1)S(1)} %collective-permute-done.1.refs_0_.refs_4_), channel_id=1, source_target_pairs={{0,4},{4,0},{8,12},{12,8},{1,5},{5,1},{9,13},{13,9},{2,6},{6,2},{1... | collective-permute-start | bytes 3440648 | tf_op jit(solution)/shard_map/ppermute | solution.py:155
  70.4 5.0 %collective-permute-start.15 = (bf16[2,160,1792]{2,1,0:T(8,128)(2,1)S(1)}, bf16[2,160,1792]{2,1,0:T(8,128)(2,1)S(1)}, u32[]{:S(2)}, u32[]{:S(2)}) collective-permute-start(bf16[2,160,1792]{2,1,0:T(8,128)(2,1)S(1)} %collective-permute-done.6.refs_2_.refs_6_), channel_id=1, source_target_pairs={{0,4},{4,0},{8,12},{12,8},{1,5},{5,1},{9,13},{13,9},{2,6},{6,2},{1... | collective-permute-start | bytes 3440648 | tf_op jit(solution)/shard_map/ppermute | solution.py:155
  70.5 31.3 %collective-permute-start.19 = (bf16[3,160,1024]{2,1,0:T(8,128)(2,1)S(1)}, bf16[3,160,1024]{2,1,0:T(8,128)(2,1)S(1)}, u32[]{:S(2)}, u32[]{:S(2)}) collective-permute-start(bf16[3,160,1024]{2,1,0:T(8,128)(2,1)S(1)} %pad_maximum_fusion.3.refs_8_), channel_id=1, source_target_pairs={{0,16},{16,0},{1,17},{17,1},{2,18},{18,2},{3,19},{19,3},{4,20},{20... | collective-permute-start | bytes 2949128 | tf_op jit(solution)/shard_map/ppermute | solution.py:152
  72.1 12.0 %collective-permute-start.17 = (bf16[160,1024]{1,0:T(8,128)(2,1)S(1)}, bf16[160,1024]{1,0:T(8,128)(2,1)S(1)}, u32[]{:S(2)}, u32[]{:S(2)}) collective-permute-start(bf16[160,1024]{1,0:T(8,128)(2,1)S(1)} %get-tuple-element.75), channel_id=1, source_target_pairs={{0,1},{1,0},{2,3},{3,2},{4,5},{5,4},{6,7},{7,6},{8,9},{9,8},{10,11... | collective-permute-start | bytes 983048 | tf_op jit(solution)/shard_map/ppermute | solution.py:158
  72.9 18.0 %collective-permute-start.18 = (bf16[160,1024]{1,0:T(8,128)(2,1)S(1)}, bf16[160,1024]{1,0:T(8,128)(2,1)S(1)}, u32[]{:S(2)}, u32[]{:S(2)}) collective-permute-start(bf16[160,1024]{1,0:T(8,128)(2,1)S(1)} %add_convert_fusion.3), channel_id=1, source_target_pairs={{0,3},{1,2},{2,1},{3,0},{4,7},{5,6},{6,5},{7,4},{8,11},{9,10},{10,... | collective-permute-start | bytes 983048 | tf_op jit(solution)/shard_map/ppermute | solution.py:158
  75.4 26.4 %copy-start.1 = (bf16[1792,1024]{1,0:T(8,128)(2,1)S(1)}, bf16[1792,1024]{1,0:T(8,128)(2,1)}, u32[]{:S(2)}) copy-start(bf16[1792,1024]{1,0:T(8,128)(2,1)} %refs_16_.3) | copy-start | bytes 11010052
  83.1 14.1 %collective-permute-start.16 = (bf16[160,1024]{1,0:T(8,128)(2,1)S(1)}, bf16[160,1024]{1,0:T(8,128)(2,1)S(1)}, u32[]{:S(2)}, u32[]{:S(2)}) collective-permute-start(bf16[160,1024]{1,0:T(8,128)(2,1)S(1)} %get-tuple-element.73), channel_id=1, source_target_pairs={{0,1},{1,0},{2,3},{3,2},{4,5},{5,4},{6,7},{7,6},{8,9},{9,8},{10,11... | collective-permute-start | bytes 983048 | tf_op jit(solution)/shard_map/ppermute | solution.py:158
  83.5 18.3 %collective-permute-start.20 = (bf16[160,1024]{1,0:T(8,128)(2,1)S(1)}, bf16[160,1024]{1,0:T(8,128)(2,1)S(1)}, u32[]{:S(2)}, u32[]{:S(2)}) collective-permute-start(bf16[160,1024]{1,0:T(8,128)(2,1)S(1)} %collective-permute-done.13.refs_9_), channel_id=1, source_target_pairs={{0,16},{16,0},{1,17},{17,1},{2,18},{18,2},{3,19},{19,3},{4,20},{20... | collective-permute-start | bytes 983048 | tf_op jit(solution)/shard_map/ppermute | solution.py:152
  84.1 26.5 %collective-permute-start.21 = (bf16[160,1024]{1,0:T(8,128)(2,1)S(1)}, bf16[160,1024]{1,0:T(8,128)(2,1)S(1)}, u32[]{:S(2)}, u32[]{:S(2)}) collective-permute-start(bf16[160,1024]{1,0:T(8,128)(2,1)S(1)} %get-tuple-element.85), channel_id=1, source_target_pairs={{0,1},{1,0},{2,3},{3,2},{4,5},{5,4},{6,7},{7,6},{8,9},{9,8},{10,11... | collective-permute-start | bytes 983048 | tf_op jit(solution)/shard_map/ppermute | solution.py:158
  97.4 13.9 %collective-permute-start.22 = (bf16[160,1024]{1,0:T(8,128)(2,1)S(1)}, bf16[160,1024]{1,0:T(8,128)(2,1)S(1)}, u32[]{:S(2)}, u32[]{:S(2)}) collective-permute-start(bf16[160,1024]{1,0:T(8,128)(2,1)S(1)} %add_convert_fusion.2), channel_id=1, source_target_pairs={{0,3},{1,2},{2,1},{3,0},{4,7},{5,6},{6,5},{7,4},{8,11},{9,10},{10,... | collective-permute-start | bytes 983048 | tf_op jit(solution)/shard_map/ppermute | solution.py:158
  111.5 9.0 %collective-permute-start.23 = (bf16[160,1024]{1,0:T(8,128)(2,1)S(1)}, bf16[160,1024]{1,0:T(8,128)(2,1)S(1)}, u32[]{:S(2)}, u32[]{:S(2)}) collective-permute-start(bf16[160,1024]{1,0:T(8,128)(2,1)S(1)} %add_convert_fusion.1), channel_id=1, source_target_pairs={{0,16},{16,0},{1,17},{17,1},{2,18},{18,2},{3,19},{19,3},{4,20},{20... | collective-permute-start | bytes 983048 | tf_op jit(solution)/shard_map/ppermute | solution.py:152
  (7 other events, 18.6 us)

commit v4 on v3

--- a/solution.py
+++ b/solution.py
@@ -9,6 +9,7 @@
 
 VMEM_LIMIT = 34 * 1024 * 1024
 VMEM_LIMIT_GRAD = 18 * 1024 * 1024
+OWN_LIMIT = 50 * 1024 * 1024
 ORDER = (0, 1, 3, 2)
 
 
@@ -39,7 +40,7 @@
         outs[k][...] = (part_a[at] + part_b[at] * sign).astype(outs[k].dtype)
 
 
-def partial_input_grad(turn, pieces, mean_weight, perturbed, signs, weight):
+def partial_input_grad(turn, pieces, mean_weight, perturbed, signs, weight, limit):
     hidden, feats = mean_weight.shape
     n_piece, rows = len(pieces), pieces[0].shape[1]
     tile = min(256, feats)
@@ -60,7 +61,7 @@
             ],
         ),
         out_shape=[jax.ShapeDtypeStruct((rows, feats), jnp.bfloat16)] * n_piece,
-        compiler_params=pltpu.CompilerParams(vmem_limit_bytes=VMEM_LIMIT_GRAD),
+        compiler_params=pltpu.CompilerParams(vmem_limit_bytes=limit),
         cost_estimate=pl.CostEstimate(
             flops=int(weight * n_piece * rows * hidden * feats),
             bytes_accessed=4 * (n_piece * rows * (hidden + feats) + hidden * feats),
@@ -159,12 +160,12 @@
 
     def half(step):
         start = ((depth + step) % n_depth) * hidden
-        return jnp.stack([lax.dynamic_slice_in_dim(a, start, hidden, 1) for a in (out_grads, signed_grads)])
+        grads, bits = (lax.dynamic_slice_in_dim(a, start, hidden, 1) for a in (out_grads, out_bits))
+        return jnp.stack([grads, grads * (1 - 2 * bits).astype(jnp.bfloat16)])
 
     def tie(*values):
         return lax.optimization_barrier(values)
 
-    signed_grads = out_grads * (1 - 2 * out_bits).astype(jnp.bfloat16)
     mine, others = half(0), [half(j) for j in range(1, n_depth)]
     others, in_bits = tie(others, in_bits)
     in_sign = (1 - 2 * in_bits).astype(jnp.bfloat16)
@@ -179,7 +180,7 @@
     pieces = [[mine, swap(mine, 1), across, swap(across, 1)]]
 
     slab_sign = [[head, tail]] + [[hop(head, j), hop(tail, j)] for j in range(1, n_depth)]
-    own = partial_input_grad(turn, pieces[0], mean_weight, perturbed, slab_sign[0], 64)
+    own = partial_input_grad(turn, pieces[0], mean_weight, perturbed, slab_sign[0], 64, OWN_LIMIT)
     blocks = [inputs, cross(inputs, 1), None, cross(inputs, 3)]
     blocks[1], blocks[3], own = tie(blocks[1], blocks[3], own)
     blocks[2] = cross(blocks[3], 1)
@@ -198,7 +199,7 @@
     for j in range(1, n_depth):
         hopped = [hop(x, j) for x in blocks]
         pieces.append([others[j - 1], swap(others[j - 1], 1), across[j - 1], swap(across[j - 1], 1)])
-        part = partial_input_grad(turn, pieces[j], mean_weight, perturbed, slab_sign[j], 4)
+        part = partial_input_grad(turn, pieces[j], mean_weight, perturbed, slab_sign[j], 4, VMEM_LIMIT_GRAD)
         passed = cross(part[2], 1)
         if j == 1:
             passed, owned = tie(passed, owned)

time: 122 us -> 120 us (0.984)
  waiting for transfers between devices: 48.1 us -> 44.5 us
  starting transfers between devices: 25.5 us -> 27.6 us
  Pallas kernels: 32.8 us -> 34.2 us
  local copies, waits for them, and re-layouts: 5.01 us -> 3.77 us
    ppermute x12, waiting for transfers between devices: 31.1 us -> 27 us  [cross(): return lax.ppermute(value, 'col', [(i, i ^ bits) for i in range(n_col)])]
    another operation x2 -> x3, other arithmetic: 0.21 us -> 2.74 us  [half(): return jnp.stack([grads, grads * (1 - 2 * bits).astype(jnp.bfloat16)])]
    mul x1 -> x0, other arithmetic: 2.5 us -> none  [local(): signed_grads = out_grads * (1 - 2 * out_bits).astype(jnp.bfloat16)]
    pallas_call x2, Pallas kernels: 16.8 us -> 18.1 us  [partial_input_grad(): pl.pallas_call(functools.partial(grad_kernel, n_piece), grid_spec=pltpu.P...]
    unnamed x30 -> x36, local copies, waits for them, and re-layouts: 4.85 us -> 3.77 us
  transfers between devices with their start and end apart: 24 -> 24, of which waited for: 10 -> 10; matrix products, arithmetic and copies ran while one was open for 4% -> 5% of each run, Pallas kernels for 27% -> 28%
where the time goes in v4:
time: 120 us
  waiting for transfers between devices  44.5 us (37%)
  Pallas kernels  34.2 us (29%)
  starting transfers between devices  27.6 us (23%)
  other arithmetic  9.18 us (8%)
  local copies, waits for them, and re-layouts  3.77 us (3%)
    ppermute x12, waiting for transfers between devices, cross(): return lax.ppermute(value, 'col', [(i, i ^ bits) for i in range(n_col)])  27 us
    pallas_call x2, Pallas kernels, partial_input_grad(): pl.pallas_call(functools.partial(grad_kernel, n_piece), grid_spec=pltpu.P...  18.1 us
    ppermute x6, waiting for transfers between devices, hop(): lax.ppermute(value, 'depth', [(i, (i + step) % n_depth) for i in range(n_...  17.5 us
    pallas_call x2, Pallas kernels, weight_grads(): pl.pallas_call(functools.partial(weight_kernel, n_slab, n_piece, scale),...  16 us
    ppermute x12, starting transfers between devices, cross(): return lax.ppermute(value, 'col', [(i, i ^ bits) for i in range(n_col)])  15.6 us
    ppermute x6, starting transfers between devices, hop(): lax.ppermute(value, 'depth', [(i, (i + step) % n_depth) for i in range(n_...  7.88 us
    ppermute x6, starting transfers between devices, swap(): return lax.ppermute(value, 'row', [(i, i ^ bit) for i in range(n_row)])  4.1 us
    unnamed x36, local copies, waits for them, and re-layouts  3.77 us
  transfers between devices with their start and end apart: 24, of which 10 were waited for; matrix products, arithmetic and copies ran while one was open for 5% of the time, Pallas kernels for 28%

profile of v4, /device:TPU:0, one launch (start us, length us, event | category | flops | bytes accessed | tf_op | source)
XLA Modules:
  0.0 120.1 jit_solution(15500967177563743248)
XLA Ops:
  0.7 2.5 %fusion.3 = (bf16[1,160,1792]{2,1,0:T(8,128)(2,1)S(1)}, bf16[1,160,1792]{2,1,0:T(8,128)(2,1)S(1)}, bf16[1,160,1792]{2,1,0:T(8,128)(2,1)S(1)}, bf16[1,160,1792]{2,1,0:T(8,128)(2,1)S(1)}) fusion(s32[160,3584]{1,0:T(8,128)} %param.10, s32[]{:T(128)S(6)} %select_n.22, bf16[160,3584]{1,0:T(8,128)(2,1)} %param.9, s32[]{:T(128)S(6)} %select_n.20), kind=kLoop, calls=%fused_computation.15 | loop fusion | flops 4014080 | bytes 5734408 | tf_op jit(solution)/shard_map/stack | solution.py:164
  3.3 3.0 %collective-permute-start = (bf16[2,160,1792]{2,1,0:T(8,128)(2,1)S(1)}, bf16[2,160,1792]{2,1,0:T(8,128)(2,1)S(1)}, u32[]{:S(2)}, u32[]{:S(2)}) collective-permute-start(bf16[2,160,1792]{2,1,0:T(8,128)(2,1)S(1)} %pad_maximum_fusion.refs_0_), channel_id=1, source_target_pairs={{0,8},{4,12},{8,0},{12,4},{1,9},{5,13},{9,1},{13,5},{2,10},{6,14},... | collective-permute-start | bytes 3440648 | tf_op jit(solution)/shard_map/ppermute | solution.py:156
  6.5 1.6 %collective-permute-start.1 = (bf16[2,160,1792]{2,1,0:T(8,128)(2,1)S(1)}, bf16[2,160,1792]{2,1,0:T(8,128)(2,1)S(1)}, u32[]{:S(2)}, u32[]{:S(2)}) collective-permute-start(bf16[2,160,1792]{2,1,0:T(8,128)(2,1)S(1)} %pad_maximum_fusion.1), channel_id=1, source_target_pairs={{0,16},{16,0},{1,17},{17,1},{2,18},{18,2},{3,19},{19,3},{4,20},{20... | collective-permute-start | bytes 3440648 | tf_op jit(solution)/shard_map/ppermute | solution.py:153
  8.1 1.6 %collective-permute-start.2 = (bf16[160,1024]{1,0:T(8,128)(2,1)S(1)}, bf16[160,1024]{1,0:T(8,128)(2,1)S(1)}, u32[]{:S(2)}, u32[]{:S(2)}) collective-permute-start(bf16[160,1024]{1,0:T(8,128)(2,1)S(1)} %subtract_convert_fusion.2), channel_id=1, source_target_pairs={{0,1},{1,0},{2,3},{3,2},{4,5},{5,4},{6,7},{7,6},{8,9},{9,8},{10,11... | collective-permute-start | bytes 983048 | tf_op jit(solution)/shard_map/ppermute | solution.py:159
  9.8 2.5 %collective-permute-start.3 = (bf16[160,1024]{1,0:T(8,128)(2,1)S(1)}, bf16[160,1024]{1,0:T(8,128)(2,1)S(1)}, u32[]{:S(2)}, u32[]{:S(2)}) collective-permute-start(bf16[160,1024]{1,0:T(8,128)(2,1)S(1)} %subtract_convert_fusion.2), channel_id=1, source_target_pairs={{0,3},{1,2},{2,1},{3,0},{4,7},{5,6},{6,5},{7,4},{8,11},{9,10},{10,... | collective-permute-start | bytes 983048 | tf_op jit(solution)/shard_map/ppermute | solution.py:159
  12.2 5.7 %collective-permute-done.2 = bf16[160,1024]{1,0:T(8,128)(2,1)S(1)} collective-permute-done((bf16[160,1024]{1,0:T(8,128)(2,1)S(1)}, bf16[160,1024]{1,0:T(8,128)(2,1)S(1)}, u32[]{:S(2)}, u32[]{:S(2)}) %collective-permute-start.2) | collective-permute-done | bytes 327712 | tf_op jit(solution)/shard_map/ppermute | solution.py:159
  17.9 8.3 %collective-permute-done.3 = bf16[160,1024]{1,0:T(8,128)(2,1)S(1)} collective-permute-done((bf16[160,1024]{1,0:T(8,128)(2,1)S(1)}, bf16[160,1024]{1,0:T(8,128)(2,1)S(1)}, u32[]{:S(2)}, u32[]{:S(2)}) %collective-permute-start.3) | collective-permute-done | bytes 327712 | tf_op jit(solution)/shard_map/ppermute | solution.py:159
  26.8 3.7 %multiply_convert_fusion.refs_5_ = bf16[1792,1024]{1,0:T(8,128)(2,1)} fusion(bf16[1792,1024]{1,0:T(8,128)(2,1)S(1)} %copy-done, bf16[1792,1024]{1,0:T(8,128)(2,1)S(1)} %copy-done.12), kind=kLoop, calls=%fused_computation | loop fusion | flops 7340032 | bytes 11010048 | tf_op jit(solution)/shard_map/convert_element_type | solution.py:172
  30.5 3.6 %collective-permute-done.4.refs_7_.refs_13_ = bf16[160,1024]{1,0:T(8,128)(2,1)S(1)} collective-permute-done((bf16[160,1024]{1,0:T(8,128)(2,1)S(1)}, bf16[160,1024]{1,0:T(8,128)(2,1)S(1)}, u32[]{:S(2)}, u32[]{:S(2)}) %collective-permute-start.4) | collective-permute-done | bytes 327712 | tf_op jit(solution)/shard_map/ppermute | solution.py:159
  35.2 2.2 %collective-permute-start.10 = (bf16[160,1024]{1,0:T(8,128)(2,1)}, bf16[160,1024]{1,0:T(8,128)(2,1)S(1)}, u32[]{:S(2)}, u32[]{:S(2)}) collective-permute-start(bf16[160,1024]{1,0:T(8,128)(2,1)} %param.7), channel_id=1, source_target_pairs={{0,3},{1,2},{2,1},{3,0},{4,7},{5,6},{6,5},{7,4},{8,11},{9,10},{10,... | collective-permute-start | bytes 983048 | tf_op jit(solution)/shard_map/ppermute | solution.py:159
  37.9 1.3 %pad_maximum_fusion.2.refs_6_.refs_12_ = bf16[3,160,1024]{2,1,0:T(8,128)(2,1)S(1)} fusion(bf16[1,160,1024]{2,1,0:T(8,128)(2,1)} %bitcast.20, bf16[1,160,1024]{2,1,0:T(8,128)(2,1)} %bitcast.19, bf16[1,160,1024]{2,1,0:T(8,128)(2,1)} %bitcast.15), kind=kLoop, calls=%fused_computation.5 | loop fusion | flops 983040 | bytes 1966080 | tf_op jit(solution)/shard_map/stack | solution.py:179
  39.2 1.6 %collective-permute-start.7 = (bf16[3,160,1024]{2,1,0:T(8,128)(2,1)S(1)}, bf16[3,160,1024]{2,1,0:T(8,128)(2,1)S(1)}, u32[]{:S(2)}, u32[]{:S(2)}) collective-permute-start(bf16[3,160,1024]{2,1,0:T(8,128)(2,1)S(1)} %pad_maximum_fusion.2.refs_6_.refs_12_), channel_id=1, source_target_pairs={{0,16},{16,0},{1,17},{17,1},{2,18},{18,2},{3,19},{19,3},{4,20},{20... | collective-permute-start | bytes 2949128 | tf_op jit(solution)/shard_map/ppermute | solution.py:153
  41.3 10.5 %input_grad.2 = (bf16[160,1024]{1,0:T(8,128)(2,1)S(1)}, bf16[160,1024]{1,0:T(8,128)(2,1)}, bf16[160,1024]{1,0:T(8,128)(2,1)S(1)}, bf16[160,1024]{1,0:T(8,128)(2,1)S(1)}) custom-call(s32[1]{0:T(128)} %bitcast.turn_ref, bf16[2,160,1792]{2,1,0:T(8,128)(2,1)S(1)} %pad_maximum_fusion.refs_0_, bf16[2,160,1792]{2,1,0:T(8,128)(2,1)} %collective-permute-done.11.refs_1_, ...), custom_call_target="tpu_custom_call" | custom-call | flops 75161927680 | bytes 14548992 | tf_op jit(solution)/shard_map/input_grad/pallas_call | solution.py:50
  51.8 1.0 collective-permute-done.10
  52.8 1.2 %collective-permute-start.13 = (bf16[160,1024]{1,0:T(8,128)(2,1)S(1)}, bf16[160,1024]{1,0:T(8,128)(2,1)S(1)}, u32[]{:S(2)}, u32[]{:S(2)}) collective-permute-start(bf16[160,1024]{1,0:T(8,128)(2,1)S(1)} %collective-permute-done.10), channel_id=1, source_target_pairs={{0,1},{1,0},{2,3},{3,2},{4,5},{5,4},{6,7},{7,6},{8,9},{9,8},{10,11... | collective-permute-start | bytes 983048 | tf_op jit(solution)/shard_map/ppermute | solution.py:159
  54.0 0.8 collective-permute-start.14
  54.8 14.7 %collective-permute-done.8.refs_7_.refs_15_ = bf16[160,1024]{1,0:T(8,128)(2,1)S(1)} collective-permute-done((bf16[160,1024]{1,0:T(8,128)(2,1)S(1)}, bf16[160,1024]{1,0:T(8,128)(2,1)S(1)}, u32[]{:S(2)}, u32[]{:S(2)}) %collective-permute-start.8) | collective-permute-done | bytes 327712 | tf_op jit(solution)/shard_map/ppermute | solution.py:153
  70.3 1.6 %collective-permute-start.19 = (bf16[3,160,1024]{2,1,0:T(8,128)(2,1)S(1)}, bf16[3,160,1024]{2,1,0:T(8,128)(2,1)S(1)}, u32[]{:S(2)}, u32[]{:S(2)}) collective-permute-start(bf16[3,160,1024]{2,1,0:T(8,128)(2,1)S(1)} %pad_maximum_fusion.3.refs_8_), channel_id=1, source_target_pairs={{0,16},{16,0},{1,17},{17,1},{2,18},{18,2},{3,19},{19,3},{4,20},{20... | collective-permute-start | bytes 2949128 | tf_op jit(solution)/shard_map/ppermute | solution.py:153
  72.6 1.9 %collective-permute-start.18 = (bf16[160,1024]{1,0:T(8,128)(2,1)S(1)}, bf16[160,1024]{1,0:T(8,128)(2,1)S(1)}, u32[]{:S(2)}, u32[]{:S(2)}) collective-permute-start(bf16[160,1024]{1,0:T(8,128)(2,1)S(1)} %add_convert_fusion.3), channel_id=1, source_target_pairs={{0,3},{1,2},{2,1},{3,0},{4,7},{5,6},{6,5},{7,4},{8,11},{9,10},{10,... | collective-permute-start | bytes 983048 | tf_op jit(solution)/shard_map/ppermute | solution.py:159
  74.6 1.0 copy-done.8
  75.5 2.0 %copy-done.11 = bf16[1792,1024]{1,0:T(8,128)(2,1)S(1)} copy-done((bf16[1792,1024]{1,0:T(8,128)(2,1)S(1)}, bf16[1792,1024]{1,0:T(8,128)(2,1)}, u32[]{:S(2)}) %copy-start.11) | copy-done | bytes 3670040
  77.6 7.7 %input_grad.3 = (bf16[160,1024]{1,0:T(8,128)(2,1)S(1)}, bf16[160,1024]{1,0:T(8,128)(2,1)S(1)}, bf16[160,1024]{1,0:T(8,128)(2,1)S(1)}, bf16[160,1024]{1,0:T(8,128)(2,1)S(1)}) custom-call(s32[1]{0:T(128)} %bitcast.turn_ref, bf16[2,160,1792]{2,1,0:T(8,128)(2,1)S(1)} %collective-permute-done.1.refs_0_.refs_4_, ...), custom_call_target="tpu_custom_call" | custom-call | flops 4697620480 | bytes 14548992 | tf_op jit(solution)/shard_map/input_grad/pallas_call | solution.py:50
  85.6 1.3 %collective-permute-start.20 = (bf16[160,1024]{1,0:T(8,128)(2,1)S(1)}, bf16[160,1024]{1,0:T(8,128)(2,1)S(1)}, u32[]{:S(2)}, u32[]{:S(2)}) collective-permute-start(bf16[160,1024]{1,0:T(8,128)(2,1)S(1)} %collective-permute-done.13.refs_9_), channel_id=1, source_target_pairs={{0,16},{16,0},{1,17},{17,1},{2,18},{18,2},{3,19},{19,3},{4,20},{20... | collective-permute-start | bytes 983048 | tf_op jit(solution)/shard_map/ppermute | solution.py:153
  86.9 1.3 %collective-permute-start.21 = (bf16[160,1024]{1,0:T(8,128)(2,1)S(1)}, bf16[160,1024]{1,0:T(8,128)(2,1)S(1)}, u32[]{:S(2)}, u32[]{:S(2)}) collective-permute-start(bf16[160,1024]{1,0:T(8,128)(2,1)S(1)} %get-tuple-element.85), channel_id=1, source_target_pairs={{0,1},{1,0},{2,3},{3,2},{4,5},{5,4},{6,7},{7,6},{8,9},{9,8},{10,11... | collective-permute-start | bytes 983048 | tf_op jit(solution)/shard_map/ppermute | solution.py:159
  88.3 1.6 %collective-permute-done.18 = bf16[160,1024]{1,0:T(8,128)(2,1)S(1)} collective-permute-done((bf16[160,1024]{1,0:T(8,128)(2,1)S(1)}, bf16[160,1024]{1,0:T(8,128)(2,1)S(1)}, u32[]{:S(2)}, u32[]{:S(2)}) %collective-permute-start.18) | collective-permute-done | bytes 327712 | tf_op jit(solution)/shard_map/ppermute | solution.py:159
  89.9 6.6 %collective-permute-done.16 = bf16[160,1024]{1,0:T(8,128)(2,1)S(1)} collective-permute-done((bf16[160,1024]{1,0:T(8,128)(2,1)S(1)}, bf16[160,1024]{1,0:T(8,128)(2,1)S(1)}, u32[]{:S(2)}, u32[]{:S(2)}) %collective-permute-start.16) | collective-permute-done | bytes 327712 | tf_op jit(solution)/shard_map/ppermute | solution.py:159
  96.5 2.0 %collective-permute-start.22 = (bf16[160,1024]{1,0:T(8,128)(2,1)S(1)}, bf16[160,1024]{1,0:T(8,128)(2,1)S(1)}, u32[]{:S(2)}, u32[]{:S(2)}) collective-permute-start(bf16[160,1024]{1,0:T(8,128)(2,1)S(1)} %add_convert_fusion.2), channel_id=1, source_target_pairs={{0,3},{1,2},{2,1},{3,0},{4,7},{5,6},{6,5},{7,4},{8,11},{9,10},{10,... | collective-permute-start | bytes 983048 | tf_op jit(solution)/shard_map/ppermute | solution.py:159
  98.6 2.4 %collective-permute-done.20.refs_11_ = bf16[160,1024]{1,0:T(8,128)(2,1)S(1)} collective-permute-done((bf16[160,1024]{1,0:T(8,128)(2,1)S(1)}, bf16[160,1024]{1,0:T(8,128)(2,1)S(1)}, u32[]{:S(2)}, u32[]{:S(2)}) %collective-permute-start.20) | collective-permute-done | bytes 327712 | tf_op jit(solution)/shard_map/ppermute | solution.py:153
  101.0 8.9 %weight_grads.2 = (f32[1792,1024]{1,0:T(8,128)}, f32[1792,1024]{1,0:T(8,128)}) custom-call(s32[1]{0:T(128)} %bitcast.turn_ref, bf16[2,160,1792]{2,1,0:T(8,128)(2,1)S(1)} %pad_maximum_fusion.refs_0_, bf16[2,160,1792]{2,1,0:T(8,128)(2,1)} %collective-permute-done.11.refs_1_, bf16[2,160,1792]{2,1,0:T(8,128)(2,1)S(1)} %copy-done.3, ...), custom_call_target="tpu_custom_call" | custom-call | flops 1 | bytes 1 | tf_op jit(solution)/shard_map/weight_grads/pallas_call | solution.py:115
  110.3 1.3 %collective-permute-start.23 = (bf16[160,1024]{1,0:T(8,128)(2,1)S(1)}, bf16[160,1024]{1,0:T(8,128)(2,1)S(1)}, u32[]{:S(2)}, u32[]{:S(2)}) collective-permute-start(bf16[160,1024]{1,0:T(8,128)(2,1)S(1)} %add_convert_fusion.1), channel_id=1, source_target_pairs={{0,16},{16,0},{1,17},{17,1},{2,18},{18,2},{3,19},{19,3},{4,20},{20... | collective-permute-start | bytes 983048 | tf_op jit(solution)/shard_map/ppermute | solution.py:153
  111.7 7.2 %weight_grads.3 = (f32[1792,1024]{1,0:T(8,128)}, f32[1792,1024]{1,0:T(8,128)}) custom-call(s32[1]{0:T(128)} %bitcast.turn_ref, bf16[2,160,1792]{2,1,0:T(8,128)(2,1)S(1)} %pad_maximum_fusion.refs_0_, bf16[2,160,1792]{2,1,0:T(8,128)(2,1)} %collective-permute-done.11.refs_1_, ...), custom_call_target="tpu_custom_call", output_to_operand_aliasing={{0}: (18, {}), {1}: (19, {})} | custom-call | flops 4026531840 | bytes 17039360 | tf_op jit(solution)/shard_map/weight_grads/pallas_call | solution.py:115
  119.1 0.9 add_convert_fusion
  (67 shorter events, 5.6 us)
Async XLA Ops:
  0.7 26.2 %copy-start.12 = (bf16[1792,1024]{1,0:T(8,128)(2,1)S(1)}, bf16[1792,1024]{1,0:T(8,128)(2,1)}, u32[]{:S(2)}) copy-start(bf16[1792,1024]{1,0:T(8,128)(2,1)} %param.12) | copy-start | bytes 11010052
  3.2 23.6 %copy-start = (bf16[1792,1024]{1,0:T(8,128)(2,1)S(1)}, bf16[1792,1024]{1,0:T(8,128)(2,1)}, u32[]{:S(2)}) copy-start(bf16[1792,1024]{1,0:T(8,128)(2,1)} %refs_16_.3) | copy-start | bytes 11010052
  3.3 30.8 %collective-permute-start = (bf16[2,160,1792]{2,1,0:T(8,128)(2,1)S(1)}, bf16[2,160,1792]{2,1,0:T(8,128)(2,1)S(1)}, u32[]{:S(2)}, u32[]{:S(2)}) collective-permute-start(bf16[2,160,1792]{2,1,0:T(8,128)(2,1)S(1)} %pad_maximum_fusion.refs_0_), channel_id=1, source_target_pairs={{0,8},{4,12},{8,0},{12,4},{1,9},{5,13},{9,1},{13,5},{2,10},{6,14},... | collective-permute-start | bytes 3440648 | tf_op jit(solution)/shard_map/ppermute | solution.py:156
  6.5 27.7 %collective-permute-start.1 = (bf16[2,160,1792]{2,1,0:T(8,128)(2,1)S(1)}, bf16[2,160,1792]{2,1,0:T(8,128)(2,1)S(1)}, u32[]{:S(2)}, u32[]{:S(2)}) collective-permute-start(bf16[2,160,1792]{2,1,0:T(8,128)(2,1)S(1)} %pad_maximum_fusion.1), channel_id=1, source_target_pairs={{0,16},{16,0},{1,17},{17,1},{2,18},{18,2},{3,19},{19,3},{4,20},{20... | collective-permute-start | bytes 3440648 | tf_op jit(solution)/shard_map/ppermute | solution.py:153
  8.1 9.8 %collective-permute-start.2 = (bf16[160,1024]{1,0:T(8,128)(2,1)S(1)}, bf16[160,1024]{1,0:T(8,128)(2,1)S(1)}, u32[]{:S(2)}, u32[]{:S(2)}) collective-permute-start(bf16[160,1024]{1,0:T(8,128)(2,1)S(1)} %subtract_convert_fusion.2), channel_id=1, source_target_pairs={{0,1},{1,0},{2,3},{3,2},{4,5},{5,4},{6,7},{7,6},{8,9},{9,8},{10,11... | collective-permute-start | bytes 983048 | tf_op jit(solution)/shard_map/ppermute | solution.py:159
  9.8 16.5 %collective-permute-start.3 = (bf16[160,1024]{1,0:T(8,128)(2,1)S(1)}, bf16[160,1024]{1,0:T(8,128)(2,1)S(1)}, u32[]{:S(2)}, u32[]{:S(2)}) collective-permute-start(bf16[160,1024]{1,0:T(8,128)(2,1)S(1)} %subtract_convert_fusion.2), channel_id=1, source_target_pairs={{0,3},{1,2},{2,1},{3,0},{4,7},{5,6},{6,5},{7,4},{8,11},{9,10},{10,... | collective-permute-start | bytes 983048 | tf_op jit(solution)/shard_map/ppermute | solution.py:159
  12.2 26.9 %collective-permute-start.11 = (bf16[2,160,1792]{2,1,0:T(8,128)(2,1)S(1)}, bf16[2,160,1792]{2,1,0:T(8,128)(2,1)}, u32[]{:S(2)}, u32[]{:S(2)}) collective-permute-start(bf16[2,160,1792]{2,1,0:T(8,128)(2,1)S(1)} %pad_maximum_fusion.refs_0_), channel_id=1, source_target_pairs={{0,4},{4,0},{8,12},{12,8},{1,5},{5,1},{9,13},{13,9},{2,6},{6,2},{1... | collective-permute-start | bytes 3440648 | tf_op jit(solution)/shard_map/ppermute | solution.py:156
  17.9 12.6 %copy-start.16 = (bf16[160,1024]{1,0:T(8,128)(2,1)}, bf16[160,1024]{1,0:T(8,128)(2,1)S(1)}, u32[]{:S(2)}) copy-start(bf16[160,1024]{1,0:T(8,128)(2,1)S(1)} %collective-permute-done.2) | copy-start | bytes 983044
  26.2 7.9 %collective-permute-start.4 = (bf16[160,1024]{1,0:T(8,128)(2,1)S(1)}, bf16[160,1024]{1,0:T(8,128)(2,1)S(1)}, u32[]{:S(2)}, u32[]{:S(2)}) collective-permute-start(bf16[160,1024]{1,0:T(8,128)(2,1)S(1)} %collective-permute-done.3), channel_id=1, source_target_pairs={{0,1},{1,0},{2,3},{3,2},{4,5},{5,4},{6,7},{7,6},{8,9},{9,8},{10,11... | collective-permute-start | bytes 983048 | tf_op jit(solution)/shard_map/ppermute | solution.py:159
  34.9 5.9 %collective-permute-start.12 = (bf16[2,160,1792]{2,1,0:T(8,128)(2,1)S(1)}, bf16[2,160,1792]{2,1,0:T(8,128)(2,1)}, u32[]{:S(2)}, u32[]{:S(2)}) collective-permute-start(bf16[2,160,1792]{2,1,0:T(8,128)(2,1)S(1)} %collective-permute-done.refs_2_), channel_id=1, source_target_pairs={{0,4},{4,0},{8,12},{12,8},{1,5},{5,1},{9,13},{13,9},{2,6},{6,2},{1... | collective-permute-start | bytes 3440648 | tf_op jit(solution)/shard_map/ppermute | solution.py:156
  34.9 16.9 %collective-permute-start.9 = (bf16[160,1024]{1,0:T(8,128)(2,1)}, bf16[160,1024]{1,0:T(8,128)(2,1)S(1)}, u32[]{:S(2)}, u32[]{:S(2)}) collective-permute-start(bf16[160,1024]{1,0:T(8,128)(2,1)} %param.7), channel_id=1, source_target_pairs={{0,1},{1,0},{2,3},{3,2},{4,5},{5,4},{6,7},{7,6},{8,9},{9,8},{10,11... | collective-permute-start | bytes 983048 | tf_op jit(solution)/shard_map/ppermute | solution.py:159
  35.2 17.6 %collective-permute-start.10 = (bf16[160,1024]{1,0:T(8,128)(2,1)}, bf16[160,1024]{1,0:T(8,128)(2,1)S(1)}, u32[]{:S(2)}, u32[]{:S(2)}) collective-permute-start(bf16[160,1024]{1,0:T(8,128)(2,1)} %param.7), channel_id=1, source_target_pairs={{0,3},{1,2},{2,1},{3,0},{4,7},{5,6},{6,5},{7,4},{8,11},{9,10},{10,... | collective-permute-start | bytes 983048 | tf_op jit(solution)/shard_map/ppermute | solution.py:159
  37.4 32.2 %collective-permute-start.6 = (bf16[2,160,1792]{2,1,0:T(8,128)(2,1)S(1)}, bf16[2,160,1792]{2,1,0:T(8,128)(2,1)S(1)}, u32[]{:S(2)}, u32[]{:S(2)}) collective-permute-start(bf16[2,160,1792]{2,1,0:T(8,128)(2,1)S(1)} %collective-permute-done.1.refs_0_.refs_4_), channel_id=1, source_target_pairs={{0,8},{4,12},{8,0},{12,4},{1,9},{5,13},{9,1},{13,5},{2,10},{6,14},... | collective-permute-start | bytes 3440648 | tf_op jit(solution)/shard_map/ppermute | solution.py:156
  39.2 30.4 %collective-permute-start.7 = (bf16[3,160,1024]{2,1,0:T(8,128)(2,1)S(1)}, bf16[3,160,1024]{2,1,0:T(8,128)(2,1)S(1)}, u32[]{:S(2)}, u32[]{:S(2)}) collective-permute-start(bf16[3,160,1024]{2,1,0:T(8,128)(2,1)S(1)} %pad_maximum_fusion.2.refs_6_.refs_12_), channel_id=1, source_target_pairs={{0,16},{16,0},{1,17},{17,1},{2,18},{18,2},{3,19},{19,3},{4,20},{20... | collective-permute-start | bytes 2949128 | tf_op jit(solution)/shard_map/ppermute | solution.py:153
  40.8 28.8 %collective-permute-start.8 = (bf16[160,1024]{1,0:T(8,128)(2,1)S(1)}, bf16[160,1024]{1,0:T(8,128)(2,1)S(1)}, u32[]{:S(2)}, u32[]{:S(2)}) collective-permute-start(bf16[160,1024]{1,0:T(8,128)(2,1)S(1)} %copy-done.6), channel_id=1, source_target_pairs={{0,16},{16,0},{1,17},{17,1},{2,18},{18,2},{3,19},{19,3},{4,20},{20... | collective-permute-start | bytes 983048 | tf_op jit(solution)/shard_map/ppermute | solution.py:153
  41.3 28.8 %copy-start.15 = (bf16[160,1024]{1,0:T(8,128)(2,1)S(1)}, bf16[160,1024]{1,0:T(8,128)(2,1)}, u32[]{:S(2)}) copy-start(bf16[160,1024]{1,0:T(8,128)(2,1)} %param.7) | copy-start | bytes 983044
  41.3 33.2 %copy-start.4 = (bf16[1792,1024]{1,0:T(8,128)(2,1)S(1)}, bf16[1792,1024]{1,0:T(8,128)(2,1)}, u32[]{:S(2)}) copy-start(bf16[1792,1024]{1,0:T(8,128)(2,1)} %multiply_convert_fusion.refs_5_) | copy-start | bytes 11010052
  51.8 20.8 %copy-start.9 = (bf16[160,1024]{1,0:T(8,128)(2,1)}, bf16[160,1024]{1,0:T(8,128)(2,1)S(1)}, u32[]{:S(2)}) copy-start(bf16[160,1024]{1,0:T(8,128)(2,1)S(1)} %get-tuple-element.78) | copy-start | bytes 983044
  52.8 16.8 %collective-permute-start.13 = (bf16[160,1024]{1,0:T(8,128)(2,1)S(1)}, bf16[160,1024]{1,0:T(8,128)(2,1)S(1)}, u32[]{:S(2)}, u32[]{:S(2)}) collective-permute-start(bf16[160,1024]{1,0:T(8,128)(2,1)S(1)} %collective-permute-done.10), channel_id=1, source_target_pairs={{0,1},{1,0},{2,3},{3,2},{4,5},{5,4},{6,7},{7,6},{8,9},{9,8},{10,11... | collective-permute-start | bytes 983048 | tf_op jit(solution)/shard_map/ppermute | solution.py:159
  54.0 15.6 %collective-permute-start.14 = (bf16[160,1024]{1,0:T(8,128)(2,1)S(1)}, bf16[160,1024]{1,0:T(8,128)(2,1)S(1)}, u32[]{:S(2)}, u32[]{:S(2)}) collective-permute-start(bf16[160,1024]{1,0:T(8,128)(2,1)S(1)} %get-tuple-element.69), channel_id=1, source_target_pairs={{0,1},{1,0},{2,3},{3,2},{4,5},{5,4},{6,7},{7,6},{8,9},{9,8},{10,11... | collective-permute-start | bytes 983048 | tf_op jit(solution)/shard_map/ppermute | solution.py:159
  69.5 5.0 %collective-permute-start.5 = (bf16[2,160,1792]{2,1,0:T(8,128)(2,1)S(1)}, bf16[2,160,1792]{2,1,0:T(8,128)(2,1)S(1)}, u32[]{:S(2)}, u32[]{:S(2)}) collective-permute-start(bf16[2,160,1792]{2,1,0:T(8,128)(2,1)S(1)} %collective-permute-done.1.refs_0_.refs_4_), channel_id=1, source_target_pairs={{0,4},{4,0},{8,12},{12,8},{1,5},{5,1},{9,13},{13,9},{2,6},{6,2},{1... | collective-permute-start | bytes 3440648 | tf_op jit(solution)/shard_map/ppermute | solution.py:156
  69.6 5.0 %collective-permute-start.15 = (bf16[2,160,1792]{2,1,0:T(8,128)(2,1)S(1)}, bf16[2,160,1792]{2,1,0:T(8,128)(2,1)S(1)}, u32[]{:S(2)}, u32[]{:S(2)}) collective-permute-start(bf16[2,160,1792]{2,1,0:T(8,128)(2,1)S(1)} %collective-permute-done.6.refs_2_.refs_6_), channel_id=1, source_target_pairs={{0,4},{4,0},{8,12},{12,8},{1,5},{5,1},{9,13},{13,9},{2,6},{6,2},{1... | collective-permute-start | bytes 3440648 | tf_op jit(solution)/shard_map/ppermute | solution.py:156
  70.3 30.8 %collective-permute-start.19 = (bf16[3,160,1024]{2,1,0:T(8,128)(2,1)S(1)}, bf16[3,160,1024]{2,1,0:T(8,128)(2,1)S(1)}, u32[]{:S(2)}, u32[]{:S(2)}) collective-permute-start(bf16[3,160,1024]{2,1,0:T(8,128)(2,1)S(1)} %pad_maximum_fusion.3.refs_8_), channel_id=1, source_target_pairs={{0,16},{16,0},{1,17},{17,1},{2,18},{18,2},{3,19},{19,3},{4,20},{20... | collective-permute-start | bytes 2949128 | tf_op jit(solution)/shard_map/ppermute | solution.py:153
  71.8 15.1 %collective-permute-start.17 = (bf16[160,1024]{1,0:T(8,128)(2,1)}, bf16[160,1024]{1,0:T(8,128)(2,1)S(1)}, u32[]{:S(2)}, u32[]{:S(2)}) collective-permute-start(bf16[160,1024]{1,0:T(8,128)(2,1)} %get-tuple-element.75), channel_id=1, source_target_pairs={{0,1},{1,0},{2,3},{3,2},{4,5},{5,4},{6,7},{7,6},{8,9},{9,8},{10,11... | collective-permute-start | bytes 983048 | tf_op jit(solution)/shard_map/ppermute | solution.py:159
  72.6 17.3 %collective-permute-start.18 = (bf16[160,1024]{1,0:T(8,128)(2,1)S(1)}, bf16[160,1024]{1,0:T(8,128)(2,1)S(1)}, u32[]{:S(2)}, u32[]{:S(2)}) collective-permute-start(bf16[160,1024]{1,0:T(8,128)(2,1)S(1)} %add_convert_fusion.3), channel_id=1, source_target_pairs={{0,3},{1,2},{2,1},{3,0},{4,7},{5,6},{6,5},{7,4},{8,11},{9,10},{10,... | collective-permute-start | bytes 983048 | tf_op jit(solution)/shard_map/ppermute | solution.py:159
  77.6 23.5 %copy-start.1 = (bf16[1792,1024]{1,0:T(8,128)(2,1)S(1)}, bf16[1792,1024]{1,0:T(8,128)(2,1)}, u32[]{:S(2)}) copy-start(bf16[1792,1024]{1,0:T(8,128)(2,1)} %refs_16_.3) | copy-start | bytes 11010052
  77.6 23.5 %copy-start.3 = (bf16[2,160,1792]{2,1,0:T(8,128)(2,1)S(1)}, bf16[2,160,1792]{2,1,0:T(8,128)(2,1)}, u32[]{:S(2)}) copy-start(bf16[2,160,1792]{2,1,0:T(8,128)(2,1)} %copy-done.2) | copy-start | bytes 3440644
  85.2 11.2 %collective-permute-start.16 = (bf16[160,1024]{1,0:T(8,128)(2,1)S(1)}, bf16[160,1024]{1,0:T(8,128)(2,1)S(1)}, u32[]{:S(2)}, u32[]{:S(2)}) collective-permute-start(bf16[160,1024]{1,0:T(8,128)(2,1)S(1)} %get-tuple-element.73), channel_id=1, source_target_pairs={{0,1},{1,0},{2,3},{3,2},{4,5},{5,4},{6,7},{7,6},{8,9},{9,8},{10,11... | collective-permute-start | bytes 983048 | tf_op jit(solution)/shard_map/ppermute | solution.py:159
  85.6 15.4 %collective-permute-start.20 = (bf16[160,1024]{1,0:T(8,128)(2,1)S(1)}, bf16[160,1024]{1,0:T(8,128)(2,1)S(1)}, u32[]{:S(2)}, u32[]{:S(2)}) collective-permute-start(bf16[160,1024]{1,0:T(8,128)(2,1)S(1)} %collective-permute-done.13.refs_9_), channel_id=1, source_target_pairs={{0,16},{16,0},{1,17},{17,1},{2,18},{18,2},{3,19},{19,3},{4,20},{20... | collective-permute-start | bytes 983048 | tf_op jit(solution)/shard_map/ppermute | solution.py:153
  86.9 23.0 %collective-permute-start.21 = (bf16[160,1024]{1,0:T(8,128)(2,1)S(1)}, bf16[160,1024]{1,0:T(8,128)(2,1)S(1)}, u32[]{:S(2)}, u32[]{:S(2)}) collective-permute-start(bf16[160,1024]{1,0:T(8,128)(2,1)S(1)} %get-tuple-element.85), channel_id=1, source_target_pairs={{0,1},{1,0},{2,3},{3,2},{4,5},{5,4},{6,7},{7,6},{8,9},{9,8},{10,11... | collective-permute-start | bytes 983048 | tf_op jit(solution)/shard_map/ppermute | solution.py:159
  96.5 13.6 %collective-permute-start.22 = (bf16[160,1024]{1,0:T(8,128)(2,1)S(1)}, bf16[160,1024]{1,0:T(8,128)(2,1)S(1)}, u32[]{:S(2)}, u32[]{:S(2)}) collective-permute-start(bf16[160,1024]{1,0:T(8,128)(2,1)S(1)} %add_convert_fusion.2), channel_id=1, source_target_pairs={{0,3},{1,2},{2,1},{3,0},{4,7},{5,6},{6,5},{7,4},{8,11},{9,10},{10,... | collective-permute-start | bytes 983048 | tf_op jit(solution)/shard_map/ppermute | solution.py:159
  110.3 8.8 %collective-permute-start.23 = (bf16[160,1024]{1,0:T(8,128)(2,1)S(1)}, bf16[160,1024]{1,0:T(8,128)(2,1)S(1)}, u32[]{:S(2)}, u32[]{:S(2)}) collective-permute-start(bf16[160,1024]{1,0:T(8,128)(2,1)S(1)} %add_convert_fusion.1), channel_id=1, source_target_pairs={{0,16},{16,0},{1,17},{17,1},{2,18},{18,2},{3,19},{19,3},{4,20},{20... | collective-permute-start | bytes 983048 | tf_op jit(solution)/shard_map/ppermute | solution.py:153
  (10 other events, 44.4 us)

commit v5 on v4

--- a/solution.py
+++ b/solution.py
@@ -177,17 +177,18 @@
     signs[2] = cross(signs[3], 1)
     across, others, perturbed, signs, inputs = tie(swap(mine, 2), others, perturbed, signs, inputs)
     head, tail = jnp.stack([signs[0], signs[1], signs[3]]), signs[2]
+    head, late_inputs = tie(head, inputs)
     pieces = [[mine, swap(mine, 1), across, swap(across, 1)]]
 
     slab_sign = [[head, tail]] + [[hop(head, j), hop(tail, j)] for j in range(1, n_depth)]
     own = partial_input_grad(turn, pieces[0], mean_weight, perturbed, slab_sign[0], 64, OWN_LIMIT)
-    blocks = [inputs, cross(inputs, 1), None, cross(inputs, 3)]
-    blocks[1], blocks[3], own = tie(blocks[1], blocks[3], own)
-    blocks[2] = cross(blocks[3], 1)
+    blocks = [inputs, cross(inputs, 1), None, cross(late_inputs, 3)]
+    blocks[1], own = tie(blocks[1], own)
     passed = cross(own[2], 1)
     across = [swap(other, 2) for other in others]
-    across, slab_sign, blocks[2], passed = tie(across, slab_sign, blocks[2], passed)
-    blocks = [jnp.stack([blocks[0], blocks[1], blocks[3]]), blocks[2]]
+    across, slab_sign, blocks[1], blocks[3], passed = tie(across, slab_sign, blocks[1], blocks[3], passed)
+    three, blocks[3] = tie(jnp.stack([blocks[0], blocks[1], blocks[3]]), blocks[3])
+    blocks = [three, cross(blocks[3], 1)]
 
     def scatter(part, passed):
         joined = (part[3].astype(jnp.float32) + passed.astype(jnp.float32)).astype(jnp.bfloat16)
@@ -202,7 +203,7 @@
         part = partial_input_grad(turn, pieces[j], mean_weight, perturbed, slab_sign[j], 4, VMEM_LIMIT_GRAD)
         passed = cross(part[2], 1)
         if j == 1:
-            passed, owned = tie(passed, owned)
+            passed, owned[2], blocks[1] = tie(passed, owned[2], blocks[1])
             total = sum(x.astype(jnp.float32) for x in owned)
         parts = scatter(part, passed)
         parts[0], hopped = tie(parts[0], hopped)

time: 120 us -> 120 us (level)
    unnamed x36 -> x40, local copies, waits for them, and re-layouts: 3.77 us -> 3.77 us
where the time goes in v5:
time: 120 us; the launch traced here: 119 us
  waiting for transfers between devices  45.5 us (38%)
  Pallas kernels  33.4 us (28%)
  starting transfers between devices  26.7 us (22%)
  other arithmetic  9.18 us (8%)
  local copies, waits for them, and re-layouts  3.77 us (3%)
    ppermute x12, waiting for transfers between devices, cross(): return lax.ppermute(value, 'col', [(i, i ^ bits) for i in range(n_col)])  27.7 us
    ppermute x6, waiting for transfers between devices, hop(): lax.ppermute(value, 'depth', [(i, (i + step) % n_depth) for i in range(n_...  17.7 us
    pallas_call x2, Pallas kernels, partial_input_grad(): pl.pallas_call(functools.partial(grad_kernel, n_piece), grid_spec=pltpu.P...  17.4 us
    pallas_call x2, Pallas kernels, weight_grads(): pl.pallas_call(functools.partial(weight_kernel, n_slab, n_piece, scale),...  16 us
    ppermute x12, starting transfers between devices, cross(): return lax.ppermute(value, 'col', [(i, i ^ bits) for i in range(n_col)])  14.9 us
    ppermute x6, starting transfers between devices, hop(): lax.ppermute(value, 'depth', [(i, (i + step) % n_depth) for i in range(n_...  7.71 us
    ppermute x6, starting transfers between devices, swap(): return lax.ppermute(value, 'row', [(i, i ^ bit) for i in range(n_row)])  4.1 us
    unnamed x40, local copies, waits for them, and re-layouts  3.77 us
  transfers between devices with their start and end apart: 24, of which 10 were waited for; matrix products, arithmetic and copies ran while one was open for 5% of the time, Pallas kernels for 28%

profile of v5, /device:TPU:0, one launch (start us, length us, event | category | flops | bytes accessed | tf_op | source)
XLA Modules:
  0.0 119.4 jit_solution(7699668665583469677)
XLA Ops:
  0.7 2.5 %fusion.3 = (bf16[1,160,1792]{2,1,0:T(8,128)(2,1)S(1)}, bf16[1,160,1792]{2,1,0:T(8,128)(2,1)S(1)}, bf16[1,160,1792]{2,1,0:T(8,128)(2,1)S(1)}, bf16[1,160,1792]{2,1,0:T(8,128)(2,1)S(1)}) fusion(s32[160,3584]{1,0:T(8,128)} %param.10, s32[]{:T(128)S(6)} %select_n.22, bf16[160,3584]{1,0:T(8,128)(2,1)} %param.9, s32[]{:T(128)S(6)} %select_n.20), kind=kLoop, calls=%fused_computation.15 | loop fusion | flops 4014080 | bytes 5734408 | tf_op jit(solution)/shard_map/stack | solution.py:164
  3.3 3.0 %collective-permute-start = (bf16[2,160,1792]{2,1,0:T(8,128)(2,1)S(1)}, bf16[2,160,1792]{2,1,0:T(8,128)(2,1)S(1)}, u32[]{:S(2)}, u32[]{:S(2)}) collective-permute-start(bf16[2,160,1792]{2,1,0:T(8,128)(2,1)S(1)} %pad_maximum_fusion.refs_0_), channel_id=1, source_target_pairs={{0,8},{4,12},{8,0},{12,4},{1,9},{5,13},{9,1},{13,5},{2,10},{6,14},... | collective-permute-start | bytes 3440648 | tf_op jit(solution)/shard_map/ppermute | solution.py:156
  6.5 1.6 %collective-permute-start.1 = (bf16[2,160,1792]{2,1,0:T(8,128)(2,1)S(1)}, bf16[2,160,1792]{2,1,0:T(8,128)(2,1)S(1)}, u32[]{:S(2)}, u32[]{:S(2)}) collective-permute-start(bf16[2,160,1792]{2,1,0:T(8,128)(2,1)S(1)} %pad_maximum_fusion.1), channel_id=1, source_target_pairs={{0,16},{16,0},{1,17},{17,1},{2,18},{18,2},{3,19},{19,3},{4,20},{20... | collective-permute-start | bytes 3440648 | tf_op jit(solution)/shard_map/ppermute | solution.py:153
  8.1 1.6 %collective-permute-start.2 = (bf16[160,1024]{1,0:T(8,128)(2,1)S(1)}, bf16[160,1024]{1,0:T(8,128)(2,1)S(1)}, u32[]{:S(2)}, u32[]{:S(2)}) collective-permute-start(bf16[160,1024]{1,0:T(8,128)(2,1)S(1)} %subtract_convert_fusion.2), channel_id=1, source_target_pairs={{0,1},{1,0},{2,3},{3,2},{4,5},{5,4},{6,7},{7,6},{8,9},{9,8},{10,11... | collective-permute-start | bytes 983048 | tf_op jit(solution)/shard_map/ppermute | solution.py:159
  9.8 2.5 %collective-permute-start.3 = (bf16[160,1024]{1,0:T(8,128)(2,1)S(1)}, bf16[160,1024]{1,0:T(8,128)(2,1)S(1)}, u32[]{:S(2)}, u32[]{:S(2)}) collective-permute-start(bf16[160,1024]{1,0:T(8,128)(2,1)S(1)} %subtract_convert_fusion.2), channel_id=1, source_target_pairs={{0,3},{1,2},{2,1},{3,0},{4,7},{5,6},{6,5},{7,4},{8,11},{9,10},{10,... | collective-permute-start | bytes 983048 | tf_op jit(solution)/shard_map/ppermute | solution.py:159
  12.2 5.7 %collective-permute-done.2 = bf16[160,1024]{1,0:T(8,128)(2,1)S(1)} collective-permute-done((bf16[160,1024]{1,0:T(8,128)(2,1)S(1)}, bf16[160,1024]{1,0:T(8,128)(2,1)S(1)}, u32[]{:S(2)}, u32[]{:S(2)}) %collective-permute-start.2) | collective-permute-done | bytes 327712 | tf_op jit(solution)/shard_map/ppermute | solution.py:159
  17.9 8.3 %collective-permute-done.3 = bf16[160,1024]{1,0:T(8,128)(2,1)S(1)} collective-permute-done((bf16[160,1024]{1,0:T(8,128)(2,1)S(1)}, bf16[160,1024]{1,0:T(8,128)(2,1)S(1)}, u32[]{:S(2)}, u32[]{:S(2)}) %collective-permute-start.3) | collective-permute-done | bytes 327712 | tf_op jit(solution)/shard_map/ppermute | solution.py:159
  26.8 3.7 %multiply_convert_fusion.refs_5_ = bf16[1792,1024]{1,0:T(8,128)(2,1)} fusion(bf16[1792,1024]{1,0:T(8,128)(2,1)S(1)} %copy-done, bf16[1792,1024]{1,0:T(8,128)(2,1)S(1)} %copy-done.14), kind=kLoop, calls=%fused_computation | loop fusion | flops 7340032 | bytes 11010048 | tf_op jit(solution)/shard_map/convert_element_type | solution.py:172
  30.5 3.6 %collective-permute-done.4.refs_7_.refs_13_ = bf16[160,1024]{1,0:T(8,128)(2,1)S(1)} collective-permute-done((bf16[160,1024]{1,0:T(8,128)(2,1)S(1)}, bf16[160,1024]{1,0:T(8,128)(2,1)S(1)}, u32[]{:S(2)}, u32[]{:S(2)}) %collective-permute-start.4) | collective-permute-done | bytes 327712 | tf_op jit(solution)/shard_map/ppermute | solution.py:159
  35.7 1.3 %pad_maximum_fusion.2.refs_6_.refs_12_ = bf16[3,160,1024]{2,1,0:T(8,128)(2,1)S(1)} fusion(bf16[1,160,1024]{2,1,0:T(8,128)(2,1)} %bitcast.20, bf16[1,160,1024]{2,1,0:T(8,128)(2,1)} %bitcast.19, bf16[1,160,1024]{2,1,0:T(8,128)(2,1)} %bitcast.15), kind=kLoop, calls=%fused_computation.5 | loop fusion | flops 983040 | bytes 1966080 | tf_op jit(solution)/shard_map/stack | solution.py:179
  36.9 1.6 %collective-permute-start.11 = (bf16[3,160,1024]{2,1,0:T(8,128)(2,1)S(1)}, bf16[3,160,1024]{2,1,0:T(8,128)(2,1)S(1)}, u32[]{:S(2)}, u32[]{:S(2)}) collective-permute-start(bf16[3,160,1024]{2,1,0:T(8,128)(2,1)S(1)} %pad_maximum_fusion.2.refs_6_.refs_12_), channel_id=1, source_target_pairs={{0,16},{16,0},{1,17},{17,1},{2,18},{18,2},{3,19},{19,3},{4,20},{20... | collective-permute-start | bytes 2949128 | tf_op jit(solution)/shard_map/ppermute | solution.py:153
  39.0 2.3 %collective-permute-start.13 = (bf16[160,1024]{1,0:T(8,128)(2,1)S(1)}, bf16[160,1024]{1,0:T(8,128)(2,1)S(1)}, u32[]{:S(2)}, u32[]{:S(2)}) collective-permute-start(bf16[160,1024]{1,0:T(8,128)(2,1)S(1)} %copy-done.17), channel_id=1, source_target_pairs={{0,3},{1,2},{2,1},{3,0},{4,7},{5,6},{6,5},{7,4},{8,11},{9,10},{10,... | collective-permute-start | bytes 983048 | tf_op jit(solution)/shard_map/ppermute | solution.py:159
  41.3 9.7 %input_grad.2 = (bf16[160,1024]{1,0:T(8,128)(2,1)S(1)}, bf16[160,1024]{1,0:T(8,128)(2,1)S(1)}, bf16[160,1024]{1,0:T(8,128)(2,1)S(1)}, bf16[160,1024]{1,0:T(8,128)(2,1)S(1)}) custom-call(s32[1]{0:T(128)} %bitcast.4.turn_ref, bf16[2,160,1792]{2,1,0:T(8,128)(2,1)S(1)} %pad_maximum_fusion.refs_0_, bf16[2,160,1792]{2,1,0:T(8,128)(2,1)} %collective-permute-done.6.refs_1_, ...), custom_call_target="tpu_custom_call" | custom-call | flops 75161927680 | bytes 14548992 | tf_op jit(solution)/shard_map/input_grad/pallas_call | solution.py:50
  51.1 0.7 collective-permute-start.14
  51.8 15.8 %collective-permute-done.12.refs_7_.refs_15_ = bf16[160,1024]{1,0:T(8,128)(2,1)S(1)} collective-permute-done((bf16[160,1024]{1,0:T(8,128)(2,1)S(1)}, bf16[160,1024]{1,0:T(8,128)(2,1)S(1)}, u32[]{:S(2)}, u32[]{:S(2)}) %collective-permute-start.12) | collective-permute-done | bytes 327712 | tf_op jit(solution)/shard_map/ppermute | solution.py:153
  68.3 1.6 %collective-permute-start.19 = (bf16[3,160,1024]{2,1,0:T(8,128)(2,1)S(1)}, bf16[3,160,1024]{2,1,0:T(8,128)(2,1)S(1)}, u32[]{:S(2)}, u32[]{:S(2)}) collective-permute-start(bf16[3,160,1024]{2,1,0:T(8,128)(2,1)S(1)} %pad_maximum_fusion.3.refs_8_), channel_id=1, source_target_pairs={{0,16},{16,0},{1,17},{17,1},{2,18},{18,2},{3,19},{19,3},{4,20},{20... | collective-permute-start | bytes 2949128 | tf_op jit(solution)/shard_map/ppermute | solution.py:153
  69.9 1.7 %collective-permute-start.18 = (bf16[160,1024]{1,0:T(8,128)(2,1)S(1)}, bf16[160,1024]{1,0:T(8,128)(2,1)S(1)}, u32[]{:S(2)}, u32[]{:S(2)}) collective-permute-start(bf16[160,1024]{1,0:T(8,128)(2,1)S(1)} %collective-permute-done.13), channel_id=1, source_target_pairs={{0,1},{1,0},{2,3},{3,2},{4,5},{5,4},{6,7},{7,6},{8,9},{9,8},{10,11... | collective-permute-start | bytes 983048 | tf_op jit(solution)/shard_map/ppermute | solution.py:159
  71.8 2.1 %collective-permute-start.17 = (bf16[160,1024]{1,0:T(8,128)(2,1)S(1)}, bf16[160,1024]{1,0:T(8,128)(2,1)S(1)}, u32[]{:S(2)}, u32[]{:S(2)}) collective-permute-start(bf16[160,1024]{1,0:T(8,128)(2,1)S(1)} %add_convert_fusion.3), channel_id=1, source_target_pairs={{0,3},{1,2},{2,1},{3,0},{4,7},{5,6},{6,5},{7,4},{8,11},{9,10},{10,... | collective-permute-start | bytes 983048 | tf_op jit(solution)/shard_map/ppermute | solution.py:159
  73.9 1.0 copy-done.8
  74.9 2.0 %copy-done.11 = bf16[1792,1024]{1,0:T(8,128)(2,1)S(1)} copy-done((bf16[1792,1024]{1,0:T(8,128)(2,1)S(1)}, bf16[1792,1024]{1,0:T(8,128)(2,1)}, u32[]{:S(2)}) %copy-start.11) | copy-done | bytes 3670040
  76.9 7.7 %input_grad.3 = (bf16[160,1024]{1,0:T(8,128)(2,1)S(1)}, bf16[160,1024]{1,0:T(8,128)(2,1)S(1)}, bf16[160,1024]{1,0:T(8,128)(2,1)S(1)}, bf16[160,1024]{1,0:T(8,128)(2,1)S(1)}) custom-call(s32[1]{0:T(128)} %bitcast.4.turn_ref, bf16[2,160,1792]{2,1,0:T(8,128)(2,1)S(1)} %collective-permute-done.1.refs_0_.refs_4_, ...), custom_call_target="tpu_custom_call" | custom-call | flops 4697620480 | bytes 14548992 | tf_op jit(solution)/shard_map/input_grad/pallas_call | solution.py:50
  84.7 1.4 %collective-permute-start.20 = (bf16[160,1024]{1,0:T(8,128)(2,1)S(1)}, bf16[160,1024]{1,0:T(8,128)(2,1)S(1)}, u32[]{:S(2)}, u32[]{:S(2)}) collective-permute-start(bf16[160,1024]{1,0:T(8,128)(2,1)S(1)} %collective-permute-done.18.refs_9_), channel_id=1, source_target_pairs={{0,16},{16,0},{1,17},{17,1},{2,18},{18,2},{3,19},{19,3},{4,20},{20... | collective-permute-start | bytes 983048 | tf_op jit(solution)/shard_map/ppermute | solution.py:153
  86.1 1.1 collective-permute-start.21
  87.2 1.4 %collective-permute-done.17 = bf16[160,1024]{1,0:T(8,128)(2,1)S(1)} collective-permute-done((bf16[160,1024]{1,0:T(8,128)(2,1)S(1)}, bf16[160,1024]{1,0:T(8,128)(2,1)S(1)}, u32[]{:S(2)}, u32[]{:S(2)}) %collective-permute-start.17) | collective-permute-done | bytes 327712 | tf_op jit(solution)/shard_map/ppermute | solution.py:159
  88.7 6.9 %collective-permute-done.16 = bf16[160,1024]{1,0:T(8,128)(2,1)S(1)} collective-permute-done((bf16[160,1024]{1,0:T(8,128)(2,1)S(1)}, bf16[160,1024]{1,0:T(8,128)(2,1)S(1)}, u32[]{:S(2)}, u32[]{:S(2)}) %collective-permute-start.16) | collective-permute-done | bytes 327712 | tf_op jit(solution)/shard_map/ppermute | solution.py:159
  95.6 1.9 %collective-permute-start.22 = (bf16[160,1024]{1,0:T(8,128)(2,1)S(1)}, bf16[160,1024]{1,0:T(8,128)(2,1)S(1)}, u32[]{:S(2)}, u32[]{:S(2)}) collective-permute-start(bf16[160,1024]{1,0:T(8,128)(2,1)S(1)} %add_convert_fusion.2), channel_id=1, source_target_pairs={{0,3},{1,2},{2,1},{3,0},{4,7},{5,6},{6,5},{7,4},{8,11},{9,10},{10,... | collective-permute-start | bytes 983048 | tf_op jit(solution)/shard_map/ppermute | solution.py:159
  97.5 1.6 %collective-permute-done.20.refs_11_ = bf16[160,1024]{1,0:T(8,128)(2,1)S(1)} collective-permute-done((bf16[160,1024]{1,0:T(8,128)(2,1)S(1)}, bf16[160,1024]{1,0:T(8,128)(2,1)S(1)}, u32[]{:S(2)}, u32[]{:S(2)}) %collective-permute-start.20) | collective-permute-done | bytes 327712 | tf_op jit(solution)/shard_map/ppermute | solution.py:153
  99.1 8.9 %weight_grads.2 = (f32[1792,1024]{1,0:T(8,128)}, f32[1792,1024]{1,0:T(8,128)}) custom-call(s32[1]{0:T(128)} %bitcast.4.turn_ref, bf16[2,160,1792]{2,1,0:T(8,128)(2,1)S(1)} %pad_maximum_fusion.refs_0_, bf16[2,160,1792]{2,1,0:T(8,128)(2,1)} %collective-permute-done.6.refs_1_, bf16[2,160,1792]{2,1,0:T(8,128)(2,1)S(1)} %copy-done.3, ...), custom_call_target="tpu_custom_call" | custom-call | flops 1 | bytes 1 | tf_op jit(solution)/shard_map/weight_grads/pallas_call | solution.py:115
  108.0 1.4 %collective-permute-done.21 = bf16[160,1024]{1,0:T(8,128)(2,1)S(1)} collective-permute-done((bf16[160,1024]{1,0:T(8,128)(2,1)S(1)}, bf16[160,1024]{1,0:T(8,128)(2,1)S(1)}, u32[]{:S(2)}, u32[]{:S(2)}) %collective-permute-start.21) | collective-permute-done | bytes 327712 | tf_op jit(solution)/shard_map/ppermute | solution.py:159
  109.9 1.0 collective-permute-start.23
  111.0 7.1 %weight_grads.3 = (f32[1792,1024]{1,0:T(8,128)}, f32[1792,1024]{1,0:T(8,128)}) custom-call(s32[1]{0:T(128)} %bitcast.4.turn_ref, bf16[2,160,1792]{2,1,0:T(8,128)(2,1)S(1)} %pad_maximum_fusion.refs_0_, bf16[2,160,1792]{2,1,0:T(8,128)(2,1)} %collective-permute-done.6.refs_1_, ...), custom_call_target="tpu_custom_call", output_to_operand_aliasing={{0}: (18, {}), {1}: (19, {})} | custom-call | flops 4026531840 | bytes 17039360 | tf_op jit(solution)/shard_map/weight_grads/pallas_call | solution.py:115
  118.5 0.9 add_convert_fusion
  (71 shorter events, 4.8 us)
Async XLA Ops:
  0.7 26.2 %copy-start.14 = (bf16[1792,1024]{1,0:T(8,128)(2,1)S(1)}, bf16[1792,1024]{1,0:T(8,128)(2,1)}, u32[]{:S(2)}) copy-start(bf16[1792,1024]{1,0:T(8,128)(2,1)} %param.12) | copy-start | bytes 11010052
  3.2 23.6 %copy-start = (bf16[1792,1024]{1,0:T(8,128)(2,1)S(1)}, bf16[1792,1024]{1,0:T(8,128)(2,1)}, u32[]{:S(2)}) copy-start(bf16[1792,1024]{1,0:T(8,128)(2,1)} %refs_16_.3) | copy-start | bytes 11010052
  3.3 30.8 %collective-permute-start = (bf16[2,160,1792]{2,1,0:T(8,128)(2,1)S(1)}, bf16[2,160,1792]{2,1,0:T(8,128)(2,1)S(1)}, u32[]{:S(2)}, u32[]{:S(2)}) collective-permute-start(bf16[2,160,1792]{2,1,0:T(8,128)(2,1)S(1)} %pad_maximum_fusion.refs_0_), channel_id=1, source_target_pairs={{0,8},{4,12},{8,0},{12,4},{1,9},{5,13},{9,1},{13,5},{2,10},{6,14},... | collective-permute-start | bytes 3440648 | tf_op jit(solution)/shard_map/ppermute | solution.py:156
  6.5 27.7 %collective-permute-start.1 = (bf16[2,160,1792]{2,1,0:T(8,128)(2,1)S(1)}, bf16[2,160,1792]{2,1,0:T(8,128)(2,1)S(1)}, u32[]{:S(2)}, u32[]{:S(2)}) collective-permute-start(bf16[2,160,1792]{2,1,0:T(8,128)(2,1)S(1)} %pad_maximum_fusion.1), channel_id=1, source_target_pairs={{0,16},{16,0},{1,17},{17,1},{2,18},{18,2},{3,19},{19,3},{4,20},{20... | collective-permute-start | bytes 3440648 | tf_op jit(solution)/shard_map/ppermute | solution.py:153
  8.1 9.8 %collective-permute-start.2 = (bf16[160,1024]{1,0:T(8,128)(2,1)S(1)}, bf16[160,1024]{1,0:T(8,128)(2,1)S(1)}, u32[]{:S(2)}, u32[]{:S(2)}) collective-permute-start(bf16[160,1024]{1,0:T(8,128)(2,1)S(1)} %subtract_convert_fusion.2), channel_id=1, source_target_pairs={{0,1},{1,0},{2,3},{3,2},{4,5},{5,4},{6,7},{7,6},{8,9},{9,8},{10,11... | collective-permute-start | bytes 983048 | tf_op jit(solution)/shard_map/ppermute | solution.py:159
  9.8 16.5 %collective-permute-start.3 = (bf16[160,1024]{1,0:T(8,128)(2,1)S(1)}, bf16[160,1024]{1,0:T(8,128)(2,1)S(1)}, u32[]{:S(2)}, u32[]{:S(2)}) collective-permute-start(bf16[160,1024]{1,0:T(8,128)(2,1)S(1)} %subtract_convert_fusion.2), channel_id=1, source_target_pairs={{0,3},{1,2},{2,1},{3,0},{4,7},{5,6},{6,5},{7,4},{8,11},{9,10},{10,... | collective-permute-start | bytes 983048 | tf_op jit(solution)/shard_map/ppermute | solution.py:159
  12.2 26.3 %collective-permute-start.6 = (bf16[2,160,1792]{2,1,0:T(8,128)(2,1)S(1)}, bf16[2,160,1792]{2,1,0:T(8,128)(2,1)}, u32[]{:S(2)}, u32[]{:S(2)}) collective-permute-start(bf16[2,160,1792]{2,1,0:T(8,128)(2,1)S(1)} %pad_maximum_fusion.refs_0_), channel_id=1, source_target_pairs={{0,4},{4,0},{8,12},{12,8},{1,5},{5,1},{9,13},{13,9},{2,6},{6,2},{1... | collective-permute-start | bytes 3440648 | tf_op jit(solution)/shard_map/ppermute | solution.py:156
  26.2 7.9 %collective-permute-start.4 = (bf16[160,1024]{1,0:T(8,128)(2,1)S(1)}, bf16[160,1024]{1,0:T(8,128)(2,1)S(1)}, u32[]{:S(2)}, u32[]{:S(2)}) collective-permute-start(bf16[160,1024]{1,0:T(8,128)(2,1)S(1)} %collective-permute-done.3), channel_id=1, source_target_pairs={{0,1},{1,0},{2,3},{3,2},{4,5},{5,4},{6,7},{7,6},{8,9},{9,8},{10,11... | collective-permute-start | bytes 983048 | tf_op jit(solution)/shard_map/ppermute | solution.py:159
  34.9 4.2 %collective-permute-start.7 = (bf16[2,160,1792]{2,1,0:T(8,128)(2,1)S(1)}, bf16[2,160,1792]{2,1,0:T(8,128)(2,1)}, u32[]{:S(2)}, u32[]{:S(2)}) collective-permute-start(bf16[2,160,1792]{2,1,0:T(8,128)(2,1)S(1)} %collective-permute-done.refs_2_), channel_id=1, source_target_pairs={{0,4},{4,0},{8,12},{12,8},{1,5},{5,1},{9,13},{13,9},{2,6},{6,2},{1... | collective-permute-start | bytes 3440648 | tf_op jit(solution)/shard_map/ppermute | solution.py:156
  34.9 32.8 %collective-permute-start.10 = (bf16[2,160,1792]{2,1,0:T(8,128)(2,1)S(1)}, bf16[2,160,1792]{2,1,0:T(8,128)(2,1)S(1)}, u32[]{:S(2)}, u32[]{:S(2)}) collective-permute-start(bf16[2,160,1792]{2,1,0:T(8,128)(2,1)S(1)} %collective-permute-done.1.refs_0_.refs_4_), channel_id=1, source_target_pairs={{0,8},{4,12},{8,0},{12,4},{1,9},{5,13},{9,1},{13,5},{2,10},{6,14},... | collective-permute-start | bytes 3440648 | tf_op jit(solution)/shard_map/ppermute | solution.py:156
  35.4 15.7 %collective-permute-start.5 = (bf16[160,1024]{1,0:T(8,128)(2,1)}, bf16[160,1024]{1,0:T(8,128)(2,1)S(1)}, u32[]{:S(2)}, u32[]{:S(2)}) collective-permute-start(bf16[160,1024]{1,0:T(8,128)(2,1)} %param.7), channel_id=1, source_target_pairs={{0,1},{1,0},{2,3},{3,2},{4,5},{5,4},{6,7},{7,6},{8,9},{9,8},{10,11... | collective-permute-start | bytes 983048 | tf_op jit(solution)/shard_map/ppermute | solution.py:159
  36.9 30.7 %collective-permute-start.11 = (bf16[3,160,1024]{2,1,0:T(8,128)(2,1)S(1)}, bf16[3,160,1024]{2,1,0:T(8,128)(2,1)S(1)}, u32[]{:S(2)}, u32[]{:S(2)}) collective-permute-start(bf16[3,160,1024]{2,1,0:T(8,128)(2,1)S(1)} %pad_maximum_fusion.2.refs_6_.refs_12_), channel_id=1, source_target_pairs={{0,16},{16,0},{1,17},{17,1},{2,18},{18,2},{3,19},{19,3},{4,20},{20... | collective-permute-start | bytes 2949128 | tf_op jit(solution)/shard_map/ppermute | solution.py:153
  38.5 29.1 %collective-permute-start.12 = (bf16[160,1024]{1,0:T(8,128)(2,1)S(1)}, bf16[160,1024]{1,0:T(8,128)(2,1)S(1)}, u32[]{:S(2)}, u32[]{:S(2)}) collective-permute-start(bf16[160,1024]{1,0:T(8,128)(2,1)S(1)} %copy-done.6), channel_id=1, source_target_pairs={{0,16},{16,0},{1,17},{17,1},{2,18},{18,2},{3,19},{19,3},{4,20},{20... | collective-permute-start | bytes 983048 | tf_op jit(solution)/shard_map/ppermute | solution.py:153
  39.0 28.6 %collective-permute-start.13 = (bf16[160,1024]{1,0:T(8,128)(2,1)S(1)}, bf16[160,1024]{1,0:T(8,128)(2,1)S(1)}, u32[]{:S(2)}, u32[]{:S(2)}) collective-permute-start(bf16[160,1024]{1,0:T(8,128)(2,1)S(1)} %copy-done.17), channel_id=1, source_target_pairs={{0,3},{1,2},{2,1},{3,0},{4,7},{5,6},{6,5},{7,4},{8,11},{9,10},{10,... | collective-permute-start | bytes 983048 | tf_op jit(solution)/shard_map/ppermute | solution.py:159
  41.3 32.6 %copy-start.4 = (bf16[1792,1024]{1,0:T(8,128)(2,1)S(1)}, bf16[1792,1024]{1,0:T(8,128)(2,1)}, u32[]{:S(2)}) copy-start(bf16[1792,1024]{1,0:T(8,128)(2,1)} %multiply_convert_fusion.refs_5_) | copy-start | bytes 11010052
  51.0 20.7 %copy-start.9 = (bf16[160,1024]{1,0:T(8,128)(2,1)}, bf16[160,1024]{1,0:T(8,128)(2,1)S(1)}, u32[]{:S(2)}) copy-start(bf16[160,1024]{1,0:T(8,128)(2,1)S(1)} %get-tuple-element.71) | copy-start | bytes 983044
  51.1 20.7 %copy-start.12 = (bf16[160,1024]{1,0:T(8,128)(2,1)}, bf16[160,1024]{1,0:T(8,128)(2,1)S(1)}, u32[]{:S(2)}) copy-start(bf16[160,1024]{1,0:T(8,128)(2,1)S(1)} %get-tuple-element.72) | copy-start | bytes 983044
  51.1 16.6 %collective-permute-start.14 = (bf16[160,1024]{1,0:T(8,128)(2,1)S(1)}, bf16[160,1024]{1,0:T(8,128)(2,1)S(1)}, u32[]{:S(2)}, u32[]{:S(2)}) collective-permute-start(bf16[160,1024]{1,0:T(8,128)(2,1)S(1)} %get-tuple-element.76), channel_id=1, source_target_pairs={{0,1},{1,0},{2,3},{3,2},{4,5},{5,4},{6,7},{7,6},{8,9},{9,8},{10,11... | collective-permute-start | bytes 983048 | tf_op jit(solution)/shard_map/ppermute | solution.py:159
  67.6 6.2 %collective-permute-start.9 = (bf16[2,160,1792]{2,1,0:T(8,128)(2,1)S(1)}, bf16[2,160,1792]{2,1,0:T(8,128)(2,1)S(1)}, u32[]{:S(2)}, u32[]{:S(2)}) collective-permute-start(bf16[2,160,1792]{2,1,0:T(8,128)(2,1)S(1)} %collective-permute-done.1.refs_0_.refs_4_), channel_id=1, source_target_pairs={{0,4},{4,0},{8,12},{12,8},{1,5},{5,1},{9,13},{13,9},{2,6},{6,2},{1... | collective-permute-start | bytes 3440648 | tf_op jit(solution)/shard_map/ppermute | solution.py:156
  67.7 6.2 %collective-permute-start.15 = (bf16[2,160,1792]{2,1,0:T(8,128)(2,1)S(1)}, bf16[2,160,1792]{2,1,0:T(8,128)(2,1)S(1)}, u32[]{:S(2)}, u32[]{:S(2)}) collective-permute-start(bf16[2,160,1792]{2,1,0:T(8,128)(2,1)S(1)} %collective-permute-done.10.refs_2_.refs_6_), channel_id=1, source_target_pairs={{0,4},{4,0},{8,12},{12,8},{1,5},{5,1},{9,13},{13,9},{2,6},{6,2},{1... | collective-permute-start | bytes 3440648 | tf_op jit(solution)/shard_map/ppermute | solution.py:156
  68.3 30.8 %collective-permute-start.19 = (bf16[3,160,1024]{2,1,0:T(8,128)(2,1)S(1)}, bf16[3,160,1024]{2,1,0:T(8,128)(2,1)S(1)}, u32[]{:S(2)}, u32[]{:S(2)}) collective-permute-start(bf16[3,160,1024]{2,1,0:T(8,128)(2,1)S(1)} %pad_maximum_fusion.3.refs_8_), channel_id=1, source_target_pairs={{0,16},{16,0},{1,17},{17,1},{2,18},{18,2},{3,19},{19,3},{4,20},{20... | collective-permute-start | bytes 2949128 | tf_op jit(solution)/shard_map/ppermute | solution.py:153
  69.9 14.7 %collective-permute-start.18 = (bf16[160,1024]{1,0:T(8,128)(2,1)S(1)}, bf16[160,1024]{1,0:T(8,128)(2,1)S(1)}, u32[]{:S(2)}, u32[]{:S(2)}) collective-permute-start(bf16[160,1024]{1,0:T(8,128)(2,1)S(1)} %collective-permute-done.13), channel_id=1, source_target_pairs={{0,1},{1,0},{2,3},{3,2},{4,5},{5,4},{6,7},{7,6},{8,9},{9,8},{10,11... | collective-permute-start | bytes 983048 | tf_op jit(solution)/shard_map/ppermute | solution.py:159
  71.8 16.8 %collective-permute-start.17 = (bf16[160,1024]{1,0:T(8,128)(2,1)S(1)}, bf16[160,1024]{1,0:T(8,128)(2,1)S(1)}, u32[]{:S(2)}, u32[]{:S(2)}) collective-permute-start(bf16[160,1024]{1,0:T(8,128)(2,1)S(1)} %add_convert_fusion.3), channel_id=1, source_target_pairs={{0,3},{1,2},{2,1},{3,0},{4,7},{5,6},{6,5},{7,4},{8,11},{9,10},{10,... | collective-permute-start | bytes 983048 | tf_op jit(solution)/shard_map/ppermute | solution.py:159
  76.9 20.6 %copy-start.13 = (bf16[160,1024]{1,0:T(8,128)(2,1)S(1)}, bf16[160,1024]{1,0:T(8,128)(2,1)}, u32[]{:S(2)}) copy-start(bf16[160,1024]{1,0:T(8,128)(2,1)} %copy-done.12) | copy-start | bytes 983044
  76.9 22.2 %copy-start.1 = (bf16[1792,1024]{1,0:T(8,128)(2,1)S(1)}, bf16[1792,1024]{1,0:T(8,128)(2,1)}, u32[]{:S(2)}) copy-start(bf16[1792,1024]{1,0:T(8,128)(2,1)} %refs_16_.3) | copy-start | bytes 11010052
  76.9 22.2 %copy-start.3 = (bf16[2,160,1792]{2,1,0:T(8,128)(2,1)S(1)}, bf16[2,160,1792]{2,1,0:T(8,128)(2,1)}, u32[]{:S(2)}) copy-start(bf16[2,160,1792]{2,1,0:T(8,128)(2,1)} %copy-done.2) | copy-start | bytes 3440644
  84.6 10.9 %collective-permute-start.16 = (bf16[160,1024]{1,0:T(8,128)(2,1)S(1)}, bf16[160,1024]{1,0:T(8,128)(2,1)S(1)}, u32[]{:S(2)}, u32[]{:S(2)}) collective-permute-start(bf16[160,1024]{1,0:T(8,128)(2,1)S(1)} %get-tuple-element.80), channel_id=1, source_target_pairs={{0,1},{1,0},{2,3},{3,2},{4,5},{5,4},{6,7},{7,6},{8,9},{9,8},{10,11... | collective-permute-start | bytes 983048 | tf_op jit(solution)/shard_map/ppermute | solution.py:159
  84.7 14.4 %collective-permute-start.20 = (bf16[160,1024]{1,0:T(8,128)(2,1)S(1)}, bf16[160,1024]{1,0:T(8,128)(2,1)S(1)}, u32[]{:S(2)}, u32[]{:S(2)}) collective-permute-start(bf16[160,1024]{1,0:T(8,128)(2,1)S(1)} %collective-permute-done.18.refs_9_), channel_id=1, source_target_pairs={{0,16},{16,0},{1,17},{17,1},{2,18},{18,2},{3,19},{19,3},{4,20},{20... | collective-permute-start | bytes 983048 | tf_op jit(solution)/shard_map/ppermute | solution.py:153
  86.1 23.2 %collective-permute-start.21 = (bf16[160,1024]{1,0:T(8,128)(2,1)S(1)}, bf16[160,1024]{1,0:T(8,128)(2,1)S(1)}, u32[]{:S(2)}, u32[]{:S(2)}) collective-permute-start(bf16[160,1024]{1,0:T(8,128)(2,1)S(1)} %get-tuple-element.90), channel_id=1, source_target_pairs={{0,1},{1,0},{2,3},{3,2},{4,5},{5,4},{6,7},{7,6},{8,9},{9,8},{10,11... | collective-permute-start | bytes 983048 | tf_op jit(solution)/shard_map/ppermute | solution.py:159
  95.6 14.1 %collective-permute-start.22 = (bf16[160,1024]{1,0:T(8,128)(2,1)S(1)}, bf16[160,1024]{1,0:T(8,128)(2,1)S(1)}, u32[]{:S(2)}, u32[]{:S(2)}) collective-permute-start(bf16[160,1024]{1,0:T(8,128)(2,1)S(1)} %add_convert_fusion.2), channel_id=1, source_target_pairs={{0,3},{1,2},{2,1},{3,0},{4,7},{5,6},{6,5},{7,4},{8,11},{9,10},{10,... | collective-permute-start | bytes 983048 | tf_op jit(solution)/shard_map/ppermute | solution.py:159
  97.5 20.6 %collective-permute-start.8 = (bf16[160,1024]{1,0:T(8,128)(2,1)S(1)}, bf16[160,1024]{1,0:T(8,128)(2,1)S(1)}, u32[]{:S(2)}, u32[]{:S(2)}) collective-permute-start(bf16[160,1024]{1,0:T(8,128)(2,1)S(1)} %copy-done.13), channel_id=1, source_target_pairs={{0,1},{1,0},{2,3},{3,2},{4,5},{5,4},{6,7},{7,6},{8,9},{9,8},{10,11... | collective-permute-start | bytes 983048 | tf_op jit(solution)/shard_map/ppermute | solution.py:159
  109.9 8.5 %collective-permute-start.23 = (bf16[160,1024]{1,0:T(8,128)(2,1)S(1)}, bf16[160,1024]{1,0:T(8,128)(2,1)S(1)}, u32[]{:S(2)}, u32[]{:S(2)}) collective-permute-start(bf16[160,1024]{1,0:T(8,128)(2,1)S(1)} %add_convert_fusion.1), channel_id=1, source_target_pairs={{0,16},{16,0},{1,17},{17,1},{2,18},{18,2},{3,19},{19,3},{4,20},{20... | collective-permute-start | bytes 983048 | tf_op jit(solution)/shard_map/ppermute | solution.py:153
  (12 other events, 59.8 us)

commit v6 on v5

--- a/solution.py
+++ b/solution.py
@@ -7,8 +7,8 @@
 from jax.experimental.pallas import tpu as pltpu
 from jax.sharding import PartitionSpec as P
 
-VMEM_LIMIT = 34 * 1024 * 1024
-VMEM_LIMIT_GRAD = 18 * 1024 * 1024
+VMEM_LIMIT = 22 * 1024 * 1024
+VMEM_LIMIT_GRAD = 14 * 1024 * 1024
 OWN_LIMIT = 50 * 1024 * 1024
 ORDER = (0, 1, 3, 2)
 

time: 120 us -> 119 us (level)
    ppermute x12, waiting for transfers between devices: 27.7 us -> 29.1 us  [cross(): return lax.ppermute(value, 'col', [(i, i ^ bits) for i in range(n_col)])]
    unnamed x40 -> x28, local copies, waits for them, and re-layouts: 3.77 us -> 2.81 us
  transfers between devices with their start and end apart: 24 -> 24, of which waited for: 10 -> 9; matrix products, arithmetic and copies ran while one was open for 5% -> 5% of each run, Pallas kernels for 28% -> 28%
where the time goes in v6:
time: 119 us
  waiting for transfers between devices  46.5 us (39%)
  Pallas kernels  33.5 us (28%)
  starting transfers between devices  26 us (22%)
  other arithmetic  9.18 us (8%)
  local copies, waits for them, and re-layouts  2.81 us (2%)
    ppermute x12, waiting for transfers between devices, cross(): return lax.ppermute(value, 'col', [(i, i ^ bits) for i in range(n_col)])  29.1 us
    pallas_call x2, Pallas kernels, partial_input_grad(): pl.pallas_call(functools.partial(grad_kernel, n_piece), grid_spec=pltpu.P...  17.4 us
    ppermute x6, waiting for transfers between devices, hop(): lax.ppermute(value, 'depth', [(i, (i + step) % n_depth) for i in range(n_...  17.4 us
    pallas_call x2, Pallas kernels, weight_grads(): pl.pallas_call(functools.partial(weight_kernel, n_slab, n_piece, scale),...  16 us
    ppermute x12, starting transfers between devices, cross(): return lax.ppermute(value, 'col', [(i, i ^ bits) for i in range(n_col)])  15.1 us
    ppermute x6, starting transfers between devices, hop(): lax.ppermute(value, 'depth', [(i, (i + step) % n_depth) for i in range(n_...  6.8 us
    ppermute x6, starting transfers between devices, swap(): return lax.ppermute(value, 'row', [(i, i ^ bit) for i in range(n_row)])  4.11 us
    convert_element_type x1, other arithmetic, local(): (sigma_weight.astype(jnp.float32) * noise.astype(jnp.float32)).astype(jnp...  3.68 us
  transfers between devices with their start and end apart: 24, of which 9 were waited for; matrix products, arithmetic and copies ran while one was open for 5% of the time, Pallas kernels for 28%

profile of v6, /device:TPU:0, one launch (start us, length us, event | category | flops | bytes accessed | tf_op | source)
XLA Modules:
  0.0 118.8 jit_solution(16264330468732056149)
XLA Ops:
  0.7 2.5 %fusion.3 = (bf16[1,160,1792]{2,1,0:T(8,128)(2,1)S(1)}, bf16[1,160,1792]{2,1,0:T(8,128)(2,1)S(1)}, bf16[1,160,1792]{2,1,0:T(8,128)(2,1)S(1)}, bf16[1,160,1792]{2,1,0:T(8,128)(2,1)S(1)}) fusion(s32[160,3584]{1,0:T(8,128)} %param.10, s32[]{:T(128)S(6)} %select_n.22, bf16[160,3584]{1,0:T(8,128)(2,1)} %param.9, s32[]{:T(128)S(6)} %select_n.20), kind=kLoop, calls=%fused_computation.15 | loop fusion | flops 4014080 | bytes 5734408 | tf_op jit(solution)/shard_map/stack | solution.py:164
  3.3 3.0 %collective-permute-start = (bf16[2,160,1792]{2,1,0:T(8,128)(2,1)S(1)}, bf16[2,160,1792]{2,1,0:T(8,128)(2,1)S(1)}, u32[]{:S(2)}, u32[]{:S(2)}) collective-permute-start(bf16[2,160,1792]{2,1,0:T(8,128)(2,1)S(1)} %pad_maximum_fusion.refs_0_), channel_id=1, source_target_pairs={{0,8},{4,12},{8,0},{12,4},{1,9},{5,13},{9,1},{13,5},{2,10},{6,14},... | collective-permute-start | bytes 3440648 | tf_op jit(solution)/shard_map/ppermute | solution.py:156
  6.5 1.6 %collective-permute-start.1 = (bf16[2,160,1792]{2,1,0:T(8,128)(2,1)S(1)}, bf16[2,160,1792]{2,1,0:T(8,128)(2,1)S(1)}, u32[]{:S(2)}, u32[]{:S(2)}) collective-permute-start(bf16[2,160,1792]{2,1,0:T(8,128)(2,1)S(1)} %pad_maximum_fusion.1), channel_id=1, source_target_pairs={{0,16},{16,0},{1,17},{17,1},{2,18},{18,2},{3,19},{19,3},{4,20},{20... | collective-permute-start | bytes 3440648 | tf_op jit(solution)/shard_map/ppermute | solution.py:153
  8.1 1.6 %collective-permute-start.2 = (bf16[160,1024]{1,0:T(8,128)(2,1)S(1)}, bf16[160,1024]{1,0:T(8,128)(2,1)S(1)}, u32[]{:S(2)}, u32[]{:S(2)}) collective-permute-start(bf16[160,1024]{1,0:T(8,128)(2,1)S(1)} %subtract_convert_fusion.2), channel_id=1, source_target_pairs={{0,1},{1,0},{2,3},{3,2},{4,5},{5,4},{6,7},{7,6},{8,9},{9,8},{10,11... | collective-permute-start | bytes 983048 | tf_op jit(solution)/shard_map/ppermute | solution.py:159
  9.8 2.5 %collective-permute-start.3 = (bf16[160,1024]{1,0:T(8,128)(2,1)S(1)}, bf16[160,1024]{1,0:T(8,128)(2,1)S(1)}, u32[]{:S(2)}, u32[]{:S(2)}) collective-permute-start(bf16[160,1024]{1,0:T(8,128)(2,1)S(1)} %subtract_convert_fusion.2), channel_id=1, source_target_pairs={{0,3},{1,2},{2,1},{3,0},{4,7},{5,6},{6,5},{7,4},{8,11},{9,10},{10,... | collective-permute-start | bytes 983048 | tf_op jit(solution)/shard_map/ppermute | solution.py:159
  12.2 5.7 %collective-permute-done.2 = bf16[160,1024]{1,0:T(8,128)(2,1)S(1)} collective-permute-done((bf16[160,1024]{1,0:T(8,128)(2,1)S(1)}, bf16[160,1024]{1,0:T(8,128)(2,1)S(1)}, u32[]{:S(2)}, u32[]{:S(2)}) %collective-permute-start.2) | collective-permute-done | bytes 327712 | tf_op jit(solution)/shard_map/ppermute | solution.py:159
  17.9 8.3 %collective-permute-done.3 = bf16[160,1024]{1,0:T(8,128)(2,1)S(1)} collective-permute-done((bf16[160,1024]{1,0:T(8,128)(2,1)S(1)}, bf16[160,1024]{1,0:T(8,128)(2,1)S(1)}, u32[]{:S(2)}, u32[]{:S(2)}) %collective-permute-start.3) | collective-permute-done | bytes 327712 | tf_op jit(solution)/shard_map/ppermute | solution.py:159
  26.2 0.6 collective-permute-start.4
  26.8 3.7 %multiply_convert_fusion.refs_5_ = bf16[1792,1024]{1,0:T(8,128)(2,1)} fusion(bf16[1792,1024]{1,0:T(8,128)(2,1)S(1)} %copy-done, bf16[1792,1024]{1,0:T(8,128)(2,1)S(1)} %copy-done.8), kind=kLoop, calls=%fused_computation | loop fusion | flops 7340032 | bytes 11010048 | tf_op jit(solution)/shard_map/convert_element_type | solution.py:172
  30.5 3.6 %collective-permute-done.4.refs_7_.refs_13_ = bf16[160,1024]{1,0:T(8,128)(2,1)S(1)} collective-permute-done((bf16[160,1024]{1,0:T(8,128)(2,1)S(1)}, bf16[160,1024]{1,0:T(8,128)(2,1)S(1)}, u32[]{:S(2)}, u32[]{:S(2)}) %collective-permute-start.4) | collective-permute-done | bytes 327712 | tf_op jit(solution)/shard_map/ppermute | solution.py:159
  34.2 0.7 copy-done.5
  35.7 1.3 %pad_maximum_fusion.2.refs_6_.refs_12_ = bf16[3,160,1024]{2,1,0:T(8,128)(2,1)S(1)} fusion(bf16[1,160,1024]{2,1,0:T(8,128)(2,1)} %bitcast.20, bf16[1,160,1024]{2,1,0:T(8,128)(2,1)} %bitcast.19, bf16[1,160,1024]{2,1,0:T(8,128)(2,1)} %bitcast.15), kind=kLoop, calls=%fused_computation.5 | loop fusion | flops 983040 | bytes 1966080 | tf_op jit(solution)/shard_map/stack | solution.py:179
  37.0 1.6 %collective-permute-start.11 = (bf16[3,160,1024]{2,1,0:T(8,128)(2,1)S(1)}, bf16[3,160,1024]{2,1,0:T(8,128)(2,1)S(1)}, u32[]{:S(2)}, u32[]{:S(2)}) collective-permute-start(bf16[3,160,1024]{2,1,0:T(8,128)(2,1)S(1)} %pad_maximum_fusion.2.refs_6_.refs_12_), channel_id=1, source_target_pairs={{0,16},{16,0},{1,17},{17,1},{2,18},{18,2},{3,19},{19,3},{4,20},{20... | collective-permute-start | bytes 2949128 | tf_op jit(solution)/shard_map/ppermute | solution.py:153
  39.1 2.2 %collective-permute-start.13 = (bf16[160,1024]{1,0:T(8,128)(2,1)S(1)}, bf16[160,1024]{1,0:T(8,128)(2,1)S(1)}, u32[]{:S(2)}, u32[]{:S(2)}) collective-permute-start(bf16[160,1024]{1,0:T(8,128)(2,1)S(1)} %copy-done.11), channel_id=1, source_target_pairs={{0,3},{1,2},{2,1},{3,0},{4,7},{5,6},{6,5},{7,4},{8,11},{9,10},{10,... | collective-permute-start | bytes 983048 | tf_op jit(solution)/shard_map/ppermute | solution.py:159
  41.3 9.7 %input_grad.2 = (bf16[160,1024]{1,0:T(8,128)(2,1)S(1)}, bf16[160,1024]{1,0:T(8,128)(2,1)S(1)}, bf16[160,1024]{1,0:T(8,128)(2,1)S(1)}, bf16[160,1024]{1,0:T(8,128)(2,1)S(1)}) custom-call(s32[1]{0:T(128)} %bitcast.4.turn_ref, bf16[2,160,1792]{2,1,0:T(8,128)(2,1)S(1)} %pad_maximum_fusion.refs_0_, bf16[2,160,1792]{2,1,0:T(8,128)(2,1)} %collective-permute-done.6.refs_1_, ...), custom_call_target="tpu_custom_call" | custom-call | flops 75161927680 | bytes 14548992 | tf_op jit(solution)/shard_map/input_grad/pallas_call | solution.py:50
  51.1 0.7 collective-permute-start.14
  51.8 15.9 %collective-permute-done.12.refs_7_.refs_15_ = bf16[160,1024]{1,0:T(8,128)(2,1)S(1)} collective-permute-done((bf16[160,1024]{1,0:T(8,128)(2,1)S(1)}, bf16[160,1024]{1,0:T(8,128)(2,1)S(1)}, u32[]{:S(2)}, u32[]{:S(2)}) %collective-permute-start.12) | collective-permute-done | bytes 327712 | tf_op jit(solution)/shard_map/ppermute | solution.py:153
  68.4 1.6 %collective-permute-start.19 = (bf16[3,160,1024]{2,1,0:T(8,128)(2,1)S(1)}, bf16[3,160,1024]{2,1,0:T(8,128)(2,1)S(1)}, u32[]{:S(2)}, u32[]{:S(2)}) collective-permute-start(bf16[3,160,1024]{2,1,0:T(8,128)(2,1)S(1)} %pad_maximum_fusion.3.refs_8_), channel_id=1, source_target_pairs={{0,16},{16,0},{1,17},{17,1},{2,18},{18,2},{3,19},{19,3},{4,20},{20... | collective-permute-start | bytes 2949128 | tf_op jit(solution)/shard_map/ppermute | solution.py:153
  70.0 1.7 %collective-permute-start.18 = (bf16[160,1024]{1,0:T(8,128)(2,1)S(1)}, bf16[160,1024]{1,0:T(8,128)(2,1)S(1)}, u32[]{:S(2)}, u32[]{:S(2)}) collective-permute-start(bf16[160,1024]{1,0:T(8,128)(2,1)S(1)} %collective-permute-done.13), channel_id=1, source_target_pairs={{0,1},{1,0},{2,3},{3,2},{4,5},{5,4},{6,7},{7,6},{8,9},{9,8},{10,11... | collective-permute-start | bytes 983048 | tf_op jit(solution)/shard_map/ppermute | solution.py:159
  71.8 2.0 %collective-permute-start.17 = (bf16[160,1024]{1,0:T(8,128)(2,1)S(1)}, bf16[160,1024]{1,0:T(8,128)(2,1)S(1)}, u32[]{:S(2)}, u32[]{:S(2)}) collective-permute-start(bf16[160,1024]{1,0:T(8,128)(2,1)S(1)} %add_convert_fusion.3), channel_id=1, source_target_pairs={{0,3},{1,2},{2,1},{3,0},{4,7},{5,6},{6,5},{7,4},{8,11},{9,10},{10,... | collective-permute-start | bytes 983048 | tf_op jit(solution)/shard_map/ppermute | solution.py:159
  73.9 2.0 %copy-done.7 = bf16[1792,1024]{1,0:T(8,128)(2,1)S(1)} copy-done((bf16[1792,1024]{1,0:T(8,128)(2,1)S(1)}, bf16[1792,1024]{1,0:T(8,128)(2,1)}, u32[]{:S(2)}) %copy-start.7) | copy-done | bytes 3670040
  75.9 7.7 %input_grad.3 = (bf16[160,1024]{1,0:T(8,128)(2,1)S(1)}, bf16[160,1024]{1,0:T(8,128)(2,1)S(1)}, bf16[160,1024]{1,0:T(8,128)(2,1)S(1)}, bf16[160,1024]{1,0:T(8,128)(2,1)S(1)}) custom-call(s32[1]{0:T(128)} %bitcast.4.turn_ref, bf16[2,160,1792]{2,1,0:T(8,128)(2,1)S(1)} %collective-permute-done.1.refs_0_.refs_4_, ...), custom_call_target="tpu_custom_call" | custom-call | flops 4697620480 | bytes 14548992 | tf_op jit(solution)/shard_map/input_grad/pallas_call | solution.py:50
  83.7 1.5 %collective-permute-start.20 = (bf16[160,1024]{1,0:T(8,128)(2,1)S(1)}, bf16[160,1024]{1,0:T(8,128)(2,1)S(1)}, u32[]{:S(2)}, u32[]{:S(2)}) collective-permute-start(bf16[160,1024]{1,0:T(8,128)(2,1)S(1)} %collective-permute-done.18.refs_9_), channel_id=1, source_target_pairs={{0,16},{16,0},{1,17},{17,1},{2,18},{18,2},{3,19},{19,3},{4,20},{20... | collective-permute-start | bytes 983048 | tf_op jit(solution)/shard_map/ppermute | solution.py:153
  85.2 1.0 collective-permute-start.21
  86.2 3.1 %collective-permute-done.17 = bf16[160,1024]{1,0:T(8,128)(2,1)S(1)} collective-permute-done((bf16[160,1024]{1,0:T(8,128)(2,1)S(1)}, bf16[160,1024]{1,0:T(8,128)(2,1)S(1)}, u32[]{:S(2)}, u32[]{:S(2)}) %collective-permute-start.17) | collective-permute-done | bytes 327712 | tf_op jit(solution)/shard_map/ppermute | solution.py:159
  89.3 6.0 %collective-permute-done.16 = bf16[160,1024]{1,0:T(8,128)(2,1)S(1)} collective-permute-done((bf16[160,1024]{1,0:T(8,128)(2,1)S(1)}, bf16[160,1024]{1,0:T(8,128)(2,1)S(1)}, u32[]{:S(2)}, u32[]{:S(2)}) %collective-permute-start.16) | collective-permute-done | bytes 327712 | tf_op jit(solution)/shard_map/ppermute | solution.py:159
  95.4 1.9 %collective-permute-start.22 = (bf16[160,1024]{1,0:T(8,128)(2,1)S(1)}, bf16[160,1024]{1,0:T(8,128)(2,1)S(1)}, u32[]{:S(2)}, u32[]{:S(2)}) collective-permute-start(bf16[160,1024]{1,0:T(8,128)(2,1)S(1)} %add_convert_fusion.2), channel_id=1, source_target_pairs={{0,3},{1,2},{2,1},{3,0},{4,7},{5,6},{6,5},{7,4},{8,11},{9,10},{10,... | collective-permute-start | bytes 983048 | tf_op jit(solution)/shard_map/ppermute | solution.py:159
  97.6 1.5 %collective-permute-done.20.refs_11_ = bf16[160,1024]{1,0:T(8,128)(2,1)S(1)} collective-permute-done((bf16[160,1024]{1,0:T(8,128)(2,1)S(1)}, bf16[160,1024]{1,0:T(8,128)(2,1)S(1)}, u32[]{:S(2)}, u32[]{:S(2)}) %collective-permute-start.20) | collective-permute-done | bytes 327712 | tf_op jit(solution)/shard_map/ppermute | solution.py:153
  99.1 8.9 %weight_grads.2 = (f32[1792,1024]{1,0:T(8,128)}, f32[1792,1024]{1,0:T(8,128)}) custom-call(s32[1]{0:T(128)} %bitcast.4.turn_ref, bf16[2,160,1792]{2,1,0:T(8,128)(2,1)S(1)} %pad_maximum_fusion.refs_0_, bf16[2,160,1792]{2,1,0:T(8,128)(2,1)} %collective-permute-done.6.refs_1_, bf16[2,160,1792]{2,1,0:T(8,128)(2,1)S(1)} %copy-done.3, ...), custom_call_target="tpu_custom_call" | custom-call | flops 1 | bytes 1 | tf_op jit(solution)/shard_map/weight_grads/pallas_call | solution.py:115
  108.2 2.2 %collective-permute-done.22 = bf16[160,1024]{1,0:T(8,128)(2,1)S(1)} collective-permute-done((bf16[160,1024]{1,0:T(8,128)(2,1)S(1)}, bf16[160,1024]{1,0:T(8,128)(2,1)S(1)}, u32[]{:S(2)}, u32[]{:S(2)}) %collective-permute-start.22) | collective-permute-done | bytes 327712 | tf_op jit(solution)/shard_map/ppermute | solution.py:159
  110.6 7.2 %weight_grads.3 = (f32[1792,1024]{1,0:T(8,128)}, f32[1792,1024]{1,0:T(8,128)}) custom-call(s32[1]{0:T(128)} %bitcast.4.turn_ref, bf16[2,160,1792]{2,1,0:T(8,128)(2,1)S(1)} %pad_maximum_fusion.refs_0_, bf16[2,160,1792]{2,1,0:T(8,128)(2,1)} %collective-permute-done.6.refs_1_, ...), custom_call_target="tpu_custom_call", output_to_operand_aliasing={{0}: (18, {}), {1}: (19, {})} | custom-call | flops 4026531840 | bytes 17039360 | tf_op jit(solution)/shard_map/weight_grads/pallas_call | solution.py:115
  117.8 0.9 add_convert_fusion
  (59 shorter events, 3.4 us)
Async XLA Ops:
  0.7 26.2 %copy-start.8 = (bf16[1792,1024]{1,0:T(8,128)(2,1)S(1)}, bf16[1792,1024]{1,0:T(8,128)(2,1)}, u32[]{:S(2)}) copy-start(bf16[1792,1024]{1,0:T(8,128)(2,1)} %param.12) | copy-start | bytes 11010052
  3.2 23.6 %copy-start = (bf16[1792,1024]{1,0:T(8,128)(2,1)S(1)}, bf16[1792,1024]{1,0:T(8,128)(2,1)}, u32[]{:S(2)}) copy-start(bf16[1792,1024]{1,0:T(8,128)(2,1)} %refs_16_.3) | copy-start | bytes 11010052
  3.3 30.8 %collective-permute-start = (bf16[2,160,1792]{2,1,0:T(8,128)(2,1)S(1)}, bf16[2,160,1792]{2,1,0:T(8,128)(2,1)S(1)}, u32[]{:S(2)}, u32[]{:S(2)}) collective-permute-start(bf16[2,160,1792]{2,1,0:T(8,128)(2,1)S(1)} %pad_maximum_fusion.refs_0_), channel_id=1, source_target_pairs={{0,8},{4,12},{8,0},{12,4},{1,9},{5,13},{9,1},{13,5},{2,10},{6,14},... | collective-permute-start | bytes 3440648 | tf_op jit(solution)/shard_map/ppermute | solution.py:156
  6.5 27.7 %collective-permute-start.1 = (bf16[2,160,1792]{2,1,0:T(8,128)(2,1)S(1)}, bf16[2,160,1792]{2,1,0:T(8,128)(2,1)S(1)}, u32[]{:S(2)}, u32[]{:S(2)}) collective-permute-start(bf16[2,160,1792]{2,1,0:T(8,128)(2,1)S(1)} %pad_maximum_fusion.1), channel_id=1, source_target_pairs={{0,16},{16,0},{1,17},{17,1},{2,18},{18,2},{3,19},{19,3},{4,20},{20... | collective-permute-start | bytes 3440648 | tf_op jit(solution)/shard_map/ppermute | solution.py:153
  8.1 9.8 %copy-start.9 = (bf16[160,1024]{1,0:T(8,128)(2,1)}, bf16[160,1024]{1,0:T(8,128)(2,1)S(1)}, u32[]{:S(2)}) copy-start(bf16[160,1024]{1,0:T(8,128)(2,1)S(1)} %subtract_convert_fusion.2) | copy-start | bytes 983044
  8.1 9.8 %collective-permute-start.2 = (bf16[160,1024]{1,0:T(8,128)(2,1)S(1)}, bf16[160,1024]{1,0:T(8,128)(2,1)S(1)}, u32[]{:S(2)}, u32[]{:S(2)}) collective-permute-start(bf16[160,1024]{1,0:T(8,128)(2,1)S(1)} %subtract_convert_fusion.2), channel_id=1, source_target_pairs={{0,1},{1,0},{2,3},{3,2},{4,5},{5,4},{6,7},{7,6},{8,9},{9,8},{10,11... | collective-permute-start | bytes 983048 | tf_op jit(solution)/shard_map/ppermute | solution.py:159
  9.8 16.5 %collective-permute-start.3 = (bf16[160,1024]{1,0:T(8,128)(2,1)S(1)}, bf16[160,1024]{1,0:T(8,128)(2,1)S(1)}, u32[]{:S(2)}, u32[]{:S(2)}) collective-permute-start(bf16[160,1024]{1,0:T(8,128)(2,1)S(1)} %subtract_convert_fusion.2), channel_id=1, source_target_pairs={{0,3},{1,2},{2,1},{3,0},{4,7},{5,6},{6,5},{7,4},{8,11},{9,10},{10,... | collective-permute-start | bytes 983048 | tf_op jit(solution)/shard_map/ppermute | solution.py:159
  12.2 26.3 %collective-permute-start.6 = (bf16[2,160,1792]{2,1,0:T(8,128)(2,1)S(1)}, bf16[2,160,1792]{2,1,0:T(8,128)(2,1)}, u32[]{:S(2)}, u32[]{:S(2)}) collective-permute-start(bf16[2,160,1792]{2,1,0:T(8,128)(2,1)S(1)} %pad_maximum_fusion.refs_0_), channel_id=1, source_target_pairs={{0,4},{4,0},{8,12},{12,8},{1,5},{5,1},{9,13},{13,9},{2,6},{6,2},{1... | collective-permute-start | bytes 3440648 | tf_op jit(solution)/shard_map/ppermute | solution.py:156
  17.9 12.6 %copy-start.12 = (bf16[160,1024]{1,0:T(8,128)(2,1)}, bf16[160,1024]{1,0:T(8,128)(2,1)S(1)}, u32[]{:S(2)}) copy-start(bf16[160,1024]{1,0:T(8,128)(2,1)S(1)} %collective-permute-done.2) | copy-start | bytes 983044
  26.2 7.9 %collective-permute-start.4 = (bf16[160,1024]{1,0:T(8,128)(2,1)S(1)}, bf16[160,1024]{1,0:T(8,128)(2,1)S(1)}, u32[]{:S(2)}, u32[]{:S(2)}) collective-permute-start(bf16[160,1024]{1,0:T(8,128)(2,1)S(1)} %collective-permute-done.3), channel_id=1, source_target_pairs={{0,1},{1,0},{2,3},{3,2},{4,5},{5,4},{6,7},{7,6},{8,9},{9,8},{10,11... | collective-permute-start | bytes 983048 | tf_op jit(solution)/shard_map/ppermute | solution.py:159
  34.1 7.1 %copy-start.2 = (bf16[2,160,1792]{2,1,0:T(8,128)(2,1)}, bf16[2,160,1792]{2,1,0:T(8,128)(2,1)S(1)}, u32[]{:S(2)}) copy-start(bf16[2,160,1792]{2,1,0:T(8,128)(2,1)S(1)} %collective-permute-done.refs_2_) | copy-start | bytes 3440644
  34.9 4.2 %collective-permute-start.7 = (bf16[2,160,1792]{2,1,0:T(8,128)(2,1)S(1)}, bf16[2,160,1792]{2,1,0:T(8,128)(2,1)}, u32[]{:S(2)}, u32[]{:S(2)}) collective-permute-start(bf16[2,160,1792]{2,1,0:T(8,128)(2,1)S(1)} %collective-permute-done.refs_2_), channel_id=1, source_target_pairs={{0,4},{4,0},{8,12},{12,8},{1,5},{5,1},{9,13},{13,9},{2,6},{6,2},{1... | collective-permute-start | bytes 3440648 | tf_op jit(solution)/shard_map/ppermute | solution.py:156
  34.9 32.8 %collective-permute-start.10 = (bf16[2,160,1792]{2,1,0:T(8,128)(2,1)S(1)}, bf16[2,160,1792]{2,1,0:T(8,128)(2,1)S(1)}, u32[]{:S(2)}, u32[]{:S(2)}) collective-permute-start(bf16[2,160,1792]{2,1,0:T(8,128)(2,1)S(1)} %collective-permute-done.1.refs_0_.refs_4_), channel_id=1, source_target_pairs={{0,8},{4,12},{8,0},{12,4},{1,9},{5,13},{9,1},{13,5},{2,10},{6,14},... | collective-permute-start | bytes 3440648 | tf_op jit(solution)/shard_map/ppermute | solution.py:156
  35.4 15.6 %collective-permute-start.5 = (bf16[160,1024]{1,0:T(8,128)(2,1)}, bf16[160,1024]{1,0:T(8,128)(2,1)S(1)}, u32[]{:S(2)}, u32[]{:S(2)}) collective-permute-start(bf16[160,1024]{1,0:T(8,128)(2,1)} %param.7), channel_id=1, source_target_pairs={{0,1},{1,0},{2,3},{3,2},{4,5},{5,4},{6,7},{7,6},{8,9},{9,8},{10,11... | collective-permute-start | bytes 983048 | tf_op jit(solution)/shard_map/ppermute | solution.py:159
  37.0 30.7 %collective-permute-start.11 = (bf16[3,160,1024]{2,1,0:T(8,128)(2,1)S(1)}, bf16[3,160,1024]{2,1,0:T(8,128)(2,1)S(1)}, u32[]{:S(2)}, u32[]{:S(2)}) collective-permute-start(bf16[3,160,1024]{2,1,0:T(8,128)(2,1)S(1)} %pad_maximum_fusion.2.refs_6_.refs_12_), channel_id=1, source_target_pairs={{0,16},{16,0},{1,17},{17,1},{2,18},{18,2},{3,19},{19,3},{4,20},{20... | collective-permute-start | bytes 2949128 | tf_op jit(solution)/shard_map/ppermute | solution.py:153
  38.6 29.1 %collective-permute-start.12 = (bf16[160,1024]{1,0:T(8,128)(2,1)S(1)}, bf16[160,1024]{1,0:T(8,128)(2,1)S(1)}, u32[]{:S(2)}, u32[]{:S(2)}) collective-permute-start(bf16[160,1024]{1,0:T(8,128)(2,1)S(1)} %copy-done.6), channel_id=1, source_target_pairs={{0,16},{16,0},{1,17},{17,1},{2,18},{18,2},{3,19},{19,3},{4,20},{20... | collective-permute-start | bytes 983048 | tf_op jit(solution)/shard_map/ppermute | solution.py:153
  39.1 28.6 %collective-permute-start.13 = (bf16[160,1024]{1,0:T(8,128)(2,1)S(1)}, bf16[160,1024]{1,0:T(8,128)(2,1)S(1)}, u32[]{:S(2)}, u32[]{:S(2)}) collective-permute-start(bf16[160,1024]{1,0:T(8,128)(2,1)S(1)} %copy-done.11), channel_id=1, source_target_pairs={{0,3},{1,2},{2,1},{3,0},{4,7},{5,6},{6,5},{7,4},{8,11},{9,10},{10,... | collective-permute-start | bytes 983048 | tf_op jit(solution)/shard_map/ppermute | solution.py:159
  41.3 32.5 %copy-start.4 = (bf16[1792,1024]{1,0:T(8,128)(2,1)S(1)}, bf16[1792,1024]{1,0:T(8,128)(2,1)}, u32[]{:S(2)}) copy-start(bf16[1792,1024]{1,0:T(8,128)(2,1)} %multiply_convert_fusion.refs_5_) | copy-start | bytes 11010052
  51.1 16.6 %collective-permute-start.14 = (bf16[160,1024]{1,0:T(8,128)(2,1)S(1)}, bf16[160,1024]{1,0:T(8,128)(2,1)S(1)}, u32[]{:S(2)}, u32[]{:S(2)}) collective-permute-start(bf16[160,1024]{1,0:T(8,128)(2,1)S(1)} %get-tuple-element.76), channel_id=1, source_target_pairs={{0,1},{1,0},{2,3},{3,2},{4,5},{5,4},{6,7},{7,6},{8,9},{9,8},{10,11... | collective-permute-start | bytes 983048 | tf_op jit(solution)/shard_map/ppermute | solution.py:159
  67.7 6.2 %collective-permute-start.9 = (bf16[2,160,1792]{2,1,0:T(8,128)(2,1)S(1)}, bf16[2,160,1792]{2,1,0:T(8,128)(2,1)S(1)}, u32[]{:S(2)}, u32[]{:S(2)}) collective-permute-start(bf16[2,160,1792]{2,1,0:T(8,128)(2,1)S(1)} %collective-permute-done.1.refs_0_.refs_4_), channel_id=1, source_target_pairs={{0,4},{4,0},{8,12},{12,8},{1,5},{5,1},{9,13},{13,9},{2,6},{6,2},{1... | collective-permute-start | bytes 3440648 | tf_op jit(solution)/shard_map/ppermute | solution.py:156
  67.7 6.1 %collective-permute-start.15 = (bf16[2,160,1792]{2,1,0:T(8,128)(2,1)S(1)}, bf16[2,160,1792]{2,1,0:T(8,128)(2,1)S(1)}, u32[]{:S(2)}, u32[]{:S(2)}) collective-permute-start(bf16[2,160,1792]{2,1,0:T(8,128)(2,1)S(1)} %collective-permute-done.10.refs_2_.refs_6_), channel_id=1, source_target_pairs={{0,4},{4,0},{8,12},{12,8},{1,5},{5,1},{9,13},{13,9},{2,6},{6,2},{1... | collective-permute-start | bytes 3440648 | tf_op jit(solution)/shard_map/ppermute | solution.py:156
  68.4 30.8 %collective-permute-start.19 = (bf16[3,160,1024]{2,1,0:T(8,128)(2,1)S(1)}, bf16[3,160,1024]{2,1,0:T(8,128)(2,1)S(1)}, u32[]{:S(2)}, u32[]{:S(2)}) collective-permute-start(bf16[3,160,1024]{2,1,0:T(8,128)(2,1)S(1)} %pad_maximum_fusion.3.refs_8_), channel_id=1, source_target_pairs={{0,16},{16,0},{1,17},{17,1},{2,18},{18,2},{3,19},{19,3},{4,20},{20... | collective-permute-start | bytes 2949128 | tf_op jit(solution)/shard_map/ppermute | solution.py:153
  70.0 13.7 %collective-permute-start.18 = (bf16[160,1024]{1,0:T(8,128)(2,1)S(1)}, bf16[160,1024]{1,0:T(8,128)(2,1)S(1)}, u32[]{:S(2)}, u32[]{:S(2)}) collective-permute-start(bf16[160,1024]{1,0:T(8,128)(2,1)S(1)} %collective-permute-done.13), channel_id=1, source_target_pairs={{0,1},{1,0},{2,3},{3,2},{4,5},{5,4},{6,7},{7,6},{8,9},{9,8},{10,11... | collective-permute-start | bytes 983048 | tf_op jit(solution)/shard_map/ppermute | solution.py:159
  71.8 17.5 %collective-permute-start.17 = (bf16[160,1024]{1,0:T(8,128)(2,1)S(1)}, bf16[160,1024]{1,0:T(8,128)(2,1)S(1)}, u32[]{:S(2)}, u32[]{:S(2)}) collective-permute-start(bf16[160,1024]{1,0:T(8,128)(2,1)S(1)} %add_convert_fusion.3), channel_id=1, source_target_pairs={{0,3},{1,2},{2,1},{3,0},{4,7},{5,6},{6,5},{7,4},{8,11},{9,10},{10,... | collective-permute-start | bytes 983048 | tf_op jit(solution)/shard_map/ppermute | solution.py:159
  75.9 23.3 %copy-start.1 = (bf16[1792,1024]{1,0:T(8,128)(2,1)S(1)}, bf16[1792,1024]{1,0:T(8,128)(2,1)}, u32[]{:S(2)}) copy-start(bf16[1792,1024]{1,0:T(8,128)(2,1)} %refs_16_.3) | copy-start | bytes 11010052
  75.9 23.3 %copy-start.3 = (bf16[2,160,1792]{2,1,0:T(8,128)(2,1)S(1)}, bf16[2,160,1792]{2,1,0:T(8,128)(2,1)}, u32[]{:S(2)}) copy-start(bf16[2,160,1792]{2,1,0:T(8,128)(2,1)} %copy-done.2) | copy-start | bytes 3440644
  83.6 11.7 %collective-permute-start.16 = (bf16[160,1024]{1,0:T(8,128)(2,1)S(1)}, bf16[160,1024]{1,0:T(8,128)(2,1)S(1)}, u32[]{:S(2)}, u32[]{:S(2)}) collective-permute-start(bf16[160,1024]{1,0:T(8,128)(2,1)S(1)} %get-tuple-element.80), channel_id=1, source_target_pairs={{0,1},{1,0},{2,3},{3,2},{4,5},{5,4},{6,7},{7,6},{8,9},{9,8},{10,11... | collective-permute-start | bytes 983048 | tf_op jit(solution)/shard_map/ppermute | solution.py:159
  83.7 15.5 %collective-permute-start.20 = (bf16[160,1024]{1,0:T(8,128)(2,1)S(1)}, bf16[160,1024]{1,0:T(8,128)(2,1)S(1)}, u32[]{:S(2)}, u32[]{:S(2)}) collective-permute-start(bf16[160,1024]{1,0:T(8,128)(2,1)S(1)} %collective-permute-done.18.refs_9_), channel_id=1, source_target_pairs={{0,16},{16,0},{1,17},{17,1},{2,18},{18,2},{3,19},{19,3},{4,20},{20... | collective-permute-start | bytes 983048 | tf_op jit(solution)/shard_map/ppermute | solution.py:153
  85.2 23.1 %collective-permute-start.21 = (bf16[160,1024]{1,0:T(8,128)(2,1)S(1)}, bf16[160,1024]{1,0:T(8,128)(2,1)S(1)}, u32[]{:S(2)}, u32[]{:S(2)}) collective-permute-start(bf16[160,1024]{1,0:T(8,128)(2,1)S(1)} %get-tuple-element.90), channel_id=1, source_target_pairs={{0,1},{1,0},{2,3},{3,2},{4,5},{5,4},{6,7},{7,6},{8,9},{9,8},{10,11... | collective-permute-start | bytes 983048 | tf_op jit(solution)/shard_map/ppermute | solution.py:159
  95.4 15.0 %collective-permute-start.22 = (bf16[160,1024]{1,0:T(8,128)(2,1)S(1)}, bf16[160,1024]{1,0:T(8,128)(2,1)S(1)}, u32[]{:S(2)}, u32[]{:S(2)}) collective-permute-start(bf16[160,1024]{1,0:T(8,128)(2,1)S(1)} %add_convert_fusion.2), channel_id=1, source_target_pairs={{0,3},{1,2},{2,1},{3,0},{4,7},{5,6},{6,5},{7,4},{8,11},{9,10},{10,... | collective-permute-start | bytes 983048 | tf_op jit(solution)/shard_map/ppermute | solution.py:159
  97.3 20.5 %collective-permute-start.8 = (bf16[160,1024]{1,0:T(8,128)(2,1)S(1)}, bf16[160,1024]{1,0:T(8,128)(2,1)S(1)}, u32[]{:S(2)}, u32[]{:S(2)}) collective-permute-start(bf16[160,1024]{1,0:T(8,128)(2,1)S(1)} %get-tuple-element.72), channel_id=1, source_target_pairs={{0,1},{1,0},{2,3},{3,2},{4,5},{5,4},{6,7},{7,6},{8,9},{9,8},{10,11... | collective-permute-start | bytes 983048 | tf_op jit(solution)/shard_map/ppermute | solution.py:159
  110.6 7.3 %collective-permute-start.23 = (bf16[160,1024]{1,0:T(8,128)(2,1)S(1)}, bf16[160,1024]{1,0:T(8,128)(2,1)S(1)}, u32[]{:S(2)}, u32[]{:S(2)}) collective-permute-start(bf16[160,1024]{1,0:T(8,128)(2,1)S(1)} %add_convert_fusion.1), channel_id=1, source_target_pairs={{0,16},{16,0},{1,17},{17,1},{2,18},{18,2},{3,19},{19,3},{4,20},{20... | collective-permute-start | bytes 983048 | tf_op jit(solution)/shard_map/ppermute | solution.py:153
  (6 other events, 16.6 us)
